TPU v7x, 32 devices: a whole 2x2x4 slice. The times are simulated.
32 devices in a mesh: dp: 8 (over z, x), pipe: 4 (over y, core).
Axes of the slice: x: 2, y: 2, z: 4, core: 2. Of those that a mesh axis runs over, the one named last changes fastest.
Arguments:
- tokens: bfloat16 [18816, 768], P('dp'), may hold values from -6 to 6
- cotangent: bfloat16 [18816, 768], P('dp'), may hold values from -6 to 6
- norm_gain: float32 [4, 768], P('pipe'), may hold values from 0.5 to 1.5
- norm_shift: float32 [4, 768], P('pipe'), may hold values from -1.5 to 1.5
- w_first: bfloat16 [4, 768, 3072], P('pipe'), may hold values from -1.5 to 1.5
- b_first: float32 [4, 3072], P('pipe'), may hold values from -1.5 to 1.5
- w_second: bfloat16 [4, 3072, 768], P('pipe'), may hold values from -0.109375 to 0.109375
- b_second: float32 [4, 768], P('pipe'), may hold values from -1.5 to 1.5
Outputs:
- layer_output: bfloat16 [18816, 768], P(('dp', 'pipe'))
- input_grad: bfloat16 [18816, 768], P(('dp', 'pipe'))
- grad_norm_gain: float32 [4, 768], P('pipe', 'dp')
- grad_norm_shift: float32 [4, 768], P('pipe', 'dp')
- grad_w_first: float32 [4, 768, 3072], P('pipe', 'dp')
- grad_b_first: float32 [4, 3072], P('pipe', 'dp')
- grad_w_second: float32 [4, 3072, 768], P('pipe', None, 'dp')
- grad_b_second: float32 [4, 768], P('pipe', 'dp')
All inputs are finite; a program needn't handle non-finite values.
Results may differ from a plain program's by a relative error of at most 0.023.
Values may be sent and summed in bfloat16 or wider, within the bound.
A program may use at most 704 MiB of HBM per device.

v0:
```python
import jax
import jax.numpy as jnp
from jax import lax
from jax.sharding import PartitionSpec as P

D = 768
FF = 3072
HEADS = 24
HEAD_DIM = 32
PATCHES = 49


NORM_EPS = 1e-05


def shortened(shard):
    return jax.tree.map(lambda a: a.astype(jnp.bfloat16) if a.dtype == jnp.float32 else a, shard)


def passed_along(block, axis, distance):
    devices = range(lax.axis_size(axis))
    route = [(i - distance, i) for i in devices if i - distance in devices]
    return lax.ppermute(block, axis, route)


def matmul(former, latter):
    return jnp.dot(former, latter, preferred_element_type=jnp.float32)


def outer_sum(former, latter):
    return lax.dot_general(
        former, latter, (((0,), (0,)), ((), ())), preferred_element_type=jnp.float32
    )


def back_dot(former, latter):
    return lax.dot_general(
        former, latter, (((1,), (1,)), ((), ())), preferred_element_type=jnp.float32
    )


def exact_gelu(values):
    return jax.nn.gelu(values, approximate=False)


def layer_norm(values, gain_vec, shift_vec):
    center = values - jnp.mean(values, -1, keepdims=True)
    variance = jnp.mean(center * center, -1, keepdims=True)
    inverse = lax.rsqrt(variance + NORM_EPS)
    scaled = center * inverse
    return (scaled * gain_vec + shift_vec, scaled, inverse)


def norm_back(grad_normed, scaled, inverse, gain_vec):
    grad_scaled = grad_normed * gain_vec
    mean_grad = jnp.mean(grad_scaled, -1, keepdims=True)
    mean_cross = jnp.mean(grad_scaled * scaled, -1, keepdims=True)
    grad_values = inverse * (grad_scaled - mean_grad - scaled * mean_cross)
    return (grad_values, jnp.sum(grad_normed * scaled, 0), jnp.sum(grad_normed, 0))


def split_heads(flat, images):
    return flat.reshape(images, PATCHES, HEADS, HEAD_DIM)


def attention_forward(x_low, params, spatial):
    gain_vec, shift_vec, w_in, b_in, w_out, b_out = params
    count = x_low.shape[0]
    images = count // PATCHES
    x_wide = x_low.astype(jnp.float32)
    normed, scaled, inverse = layer_norm(x_wide, gain_vec, shift_vec)
    normed_low = normed.astype(jnp.bfloat16)
    projected = (matmul(normed_low, w_in[:, : 3 * D]) + b_in[: 3 * D]).astype(jnp.bfloat16)
    queries = split_heads(projected[:, :D], images)
    key_rows = split_heads(projected[:, D : 2 * D], images)
    value_rows = split_heads(projected[:, 2 * D :], images)
    score_scale = HEAD_DIM ** (-0.5)
    if spatial:
        scores = (
            jnp.einsum("bnhd,bmhd->bhnm", queries, key_rows, preferred_element_type=jnp.float32)
            * score_scale
        )
        attn_probs = jax.nn.softmax(scores, axis=-1)
        probs_low = attn_probs.astype(jnp.bfloat16)
        attended = jnp.einsum(
            "bhnm,bmhd->bnhd", probs_low, value_rows, preferred_element_type=jnp.float32
        )
    else:
        scores = (
            jnp.einsum("bnhc,bnhe->bhce", queries, key_rows, preferred_element_type=jnp.float32)
            * score_scale
        )
        attn_probs = jax.nn.softmax(scores, axis=-1)
        probs_low = attn_probs.astype(jnp.bfloat16)
        attended = jnp.einsum(
            "bhce,bnhe->bnhc", probs_low, value_rows, preferred_element_type=jnp.float32
        )
    attended_low = attended.reshape(count, D).astype(jnp.bfloat16)
    branch = matmul(attended_low, w_in[:, 3 * D :]) + b_in[3 * D :]
    result = (x_wide + branch).astype(jnp.bfloat16)
    saved = (
        scaled,
        inverse,
        normed_low,
        queries,
        key_rows,
        value_rows,
        attn_probs,
        probs_low,
        attended_low,
    )
    return (result, saved)


def attention_backward(x_low, grad_low, params, spatial):
    gain_vec, shift_vec, w_in, b_in, w_out, b_out = params
    result, saved = attention_forward(x_low, params, spatial)
    (
        scaled,
        inverse,
        normed_low,
        queries,
        key_rows,
        value_rows,
        attn_probs,
        probs_low,
        attended_low,
    ) = saved
    count = x_low.shape[0]
    images = count // PATCHES
    score_scale = HEAD_DIM ** (-0.5)
    grad_wide = grad_low.astype(jnp.float32)
    grad_b_proj = jnp.sum(grad_wide, 0)
    grad_att = split_heads(back_dot(grad_low, w_in[:, 3 * D :]).astype(jnp.bfloat16), images)
    if spatial:
        grad_probs = jnp.einsum(
            "bnhd,bmhd->bhnm", grad_att, value_rows, preferred_element_type=jnp.float32
        )
        grad_vals = jnp.einsum(
            "bhnm,bnhd->bmhd", probs_low, grad_att, preferred_element_type=jnp.float32
        )
    else:
        grad_probs = jnp.einsum(
            "bnhc,bnhe->bhce", grad_att, value_rows, preferred_element_type=jnp.float32
        )
        grad_vals = jnp.einsum(
            "bhce,bnhc->bnhe", probs_low, grad_att, preferred_element_type=jnp.float32
        )
    grad_scores = attn_probs * (grad_probs - jnp.sum(attn_probs * grad_probs, -1, keepdims=True))
    scores_low = grad_scores.astype(jnp.bfloat16)
    if spatial:
        grad_query = (
            jnp.einsum("bhnm,bmhd->bnhd", scores_low, key_rows, preferred_element_type=jnp.float32)
            * score_scale
        )
        grad_key = (
            jnp.einsum("bhnm,bnhd->bmhd", scores_low, queries, preferred_element_type=jnp.float32)
            * score_scale
        )
    else:
        grad_query = (
            jnp.einsum("bhce,bnhe->bnhc", scores_low, key_rows, preferred_element_type=jnp.float32)
            * score_scale
        )
        grad_key = (
            jnp.einsum("bhce,bnhc->bnhe", scores_low, queries, preferred_element_type=jnp.float32)
            * score_scale
        )
    grad_proj_low = jnp.concatenate(
        [grad_query.reshape(count, D), grad_key.reshape(count, D), grad_vals.reshape(count, D)], 1
    ).astype(jnp.bfloat16)
    grad_b_qkv = jnp.sum(grad_proj_low.astype(jnp.float32), 0)
    grad_normed = back_dot(grad_proj_low, w_in[:, : 3 * D])
    grad_values, grad_gain, grad_shift = norm_back(grad_normed, scaled, inverse, gain_vec)
    grad_x = (grad_wide + grad_values).astype(jnp.bfloat16)
    small = (
        grad_gain,
        grad_shift,
        jnp.concatenate([grad_b_qkv, grad_b_proj], 0),
        jnp.zeros((D,), jnp.float32),
    )
    operands = (
        normed_low,
        jnp.concatenate([grad_proj_low, grad_low], 1),
        jnp.concatenate([attended_low, jnp.zeros((count, FF - D), jnp.bfloat16)], 1),
        jnp.zeros((count, D), jnp.bfloat16),
    )
    return (grad_x, small, operands)


def mlp_forward(x_low, params):
    gain_vec, shift_vec, w_in, b_in, w_out, b_out = params
    x_wide = x_low.astype(jnp.float32)
    normed, scaled, inverse = layer_norm(x_wide, gain_vec, shift_vec)
    normed_low = normed.astype(jnp.bfloat16)
    hidden = matmul(normed_low, w_in) + b_in
    active_low = exact_gelu(hidden).astype(jnp.bfloat16)
    result = (x_wide + matmul(active_low, w_out) + b_out).astype(jnp.bfloat16)
    return (result, (scaled, inverse, normed_low, hidden, active_low))


def mlp_backward(x_low, grad_low, params):
    gain_vec, shift_vec, w_in, b_in, w_out, b_out = params
    result, saved = mlp_forward(x_low, params)
    scaled, inverse, normed_low, hidden, active_low = saved
    grad_wide = grad_low.astype(jnp.float32)
    grad_b_out = jnp.sum(grad_wide, 0)
    grad_active = back_dot(grad_low, w_out)
    gelu_value, gelu_pull = jax.vjp(exact_gelu, hidden)
    grad_hidden = gelu_pull(grad_active)[0].astype(jnp.bfloat16)
    grad_b_in = jnp.sum(grad_hidden.astype(jnp.float32), 0)
    grad_normed = back_dot(grad_hidden, w_in)
    grad_values, grad_gain, grad_shift = norm_back(grad_normed, scaled, inverse, gain_vec)
    grad_x = (grad_wide + grad_values).astype(jnp.bfloat16)
    small = (grad_gain, grad_shift, grad_b_in, grad_b_out)
    operands = (normed_low, grad_hidden, active_low, grad_low)
    return (grad_x, small, operands)


def attention_weights(operands):
    left_in, right_in, left_out, right_out = operands
    first = jnp.concatenate(
        [
            outer_sum(left_in, right_in[:, : 3 * D]),
            outer_sum(left_out[:, :D], right_in[:, 3 * D :]),
        ],
        1,
    )
    return (first, jnp.zeros((FF, D), jnp.float32))


def mlp_weights(operands):
    left_in, right_in, left_out, right_out = operands
    return (outer_sum(left_in, right_in), outer_sum(left_out, right_out))


def no_weights(operands):
    return (jnp.zeros((D, FF), jnp.float32), jnp.zeros((FF, D), jnp.float32))


def zero_small():
    return (
        jnp.zeros((D,), jnp.float32),
        jnp.zeros((D,), jnp.float32),
        jnp.zeros((FF,), jnp.float32),
        jnp.zeros((D,), jnp.float32),
    )


def zero_operands(rows):
    return (
        jnp.zeros((rows, D), jnp.bfloat16),
        jnp.zeros((rows, FF), jnp.bfloat16),
        jnp.zeros((rows, FF), jnp.bfloat16),
        jnp.zeros((rows, D), jnp.bfloat16),
    )


def zero_pack():
    return (
        jnp.zeros((D,), jnp.float32),
        jnp.zeros((D,), jnp.float32),
        jnp.zeros((D, FF), jnp.float32),
        jnp.zeros((FF,), jnp.float32),
        jnp.zeros((FF, D), jnp.float32),
        jnp.zeros((D,), jnp.float32),
    )


def make_pack(small, mats):
    return (small[0], small[1], mats[0], small[3 - 1], mats[1], small[3])


def flatten_pack(pack, groups):
    gain_part, shift_part, first_mat, first_bias, second_mat, second_bias = pack
    pieces = [
        gain_part.reshape(groups, -1),
        shift_part.reshape(groups, -1),
        first_mat.reshape(groups, -1),
        first_bias.reshape(groups, -1),
        second_mat.T.reshape(groups, -1),
        second_bias.reshape(groups, -1),
    ]
    return jnp.concatenate(pieces, 1)


def unflatten_pack(summed_row, groups):
    flat = summed_row[0]
    width_share = D // groups
    hidden_share = FF // groups
    offset = 0
    gain_part = flat[offset : offset + width_share][None]
    offset = offset + width_share
    shift_part = flat[offset : offset + width_share][None]
    offset = offset + width_share
    first_mat = flat[offset : offset + width_share * FF].reshape(1, width_share, FF)
    offset = offset + width_share * FF
    first_bias = flat[offset : offset + hidden_share][None]
    offset = offset + hidden_share
    second_mat = flat[offset : offset + width_share * FF].reshape(width_share, FF).T[None]
    offset = offset + width_share * FF
    second_bias = flat[offset : offset + width_share][None]
    return (gain_part, shift_part, first_mat, first_bias, second_mat, second_bias)


def on_device(tokens, cotangent, norm_gain, norm_shift, w_first, b_first, w_second, b_second):
    params = (norm_gain[0], norm_shift[0], w_first[0], b_first[0], w_second[0], b_second[0])
    sections = lax.axis_size("pipe")
    section_num = lax.axis_index("pipe")
    groups = lax.axis_size("dp")
    last_section = sections - 1
    micro_rows = tokens.shape[0] // sections
    tick_count = 2 * sections - 1

    def window_step(arriving_rows):
        return attention_forward(arriving_rows, params, True)[0]

    def channel_step(arriving_rows):
        return attention_forward(arriving_rows, params, False)[0]

    def feed_step(arriving_rows):
        return mlp_forward(arriving_rows, params)[0]

    def spare_step(arriving_rows):
        return jnp.zeros_like(arriving_rows)

    def window_back(held_rows, grad_rows):
        return attention_backward(held_rows, grad_rows, params, True)

    def channel_back(held_rows, grad_rows):
        return attention_backward(held_rows, grad_rows, params, False)

    def feed_back(held_rows, grad_rows):
        return mlp_backward(held_rows, grad_rows, params)

    def spare_back(held_rows, grad_rows):
        return (jnp.zeros_like(grad_rows), zero_small(), zero_operands(grad_rows.shape[0]))

    forward_kinds = [window_step, feed_step, channel_step, feed_step, spare_step]
    backward_kinds = [window_back, feed_back, channel_back, feed_back, spare_back]
    weight_kinds = [attention_weights, mlp_weights, no_weights]
    stash = jnp.zeros((sections, micro_rows, D), jnp.bfloat16)
    produced = jnp.zeros((sections, micro_rows, D), jnp.bfloat16)
    arriving = jnp.zeros((micro_rows, D), jnp.bfloat16)
    for tick_num in range(tick_count):
        micro_idx = tick_num - section_num
        is_live = (micro_idx >= 0) & (micro_idx < sections)
        slot_idx = jnp.clip(micro_idx, 0, sections - 1)
        fresh_rows = lax.dynamic_slice_in_dim(tokens, slot_idx * micro_rows, micro_rows, 0)
        section_in = jnp.where(section_num == 0, fresh_rows, arriving)
        section_out = lax.switch(
            jnp.where(is_live, section_num, sections), forward_kinds, section_in
        )
        old_in = lax.dynamic_index_in_dim(stash, slot_idx, 0, keepdims=False)
        keep_in = jnp.where(is_live, section_in, old_in)
        stash = lax.dynamic_update_slice_in_dim(stash, keep_in[None], slot_idx, 0)
        old_out = lax.dynamic_index_in_dim(produced, slot_idx, 0, keepdims=False)
        keep_out = jnp.where(is_live & (section_num == last_section), section_out, old_out)
        produced = lax.dynamic_update_slice_in_dim(produced, keep_out[None], slot_idx, 0)
        if tick_num < tick_count - 1:
            arriving = jax.tree.map(
                lambda part, own: part.astype(own.dtype),
                passed_along(shortened(section_out), "pipe", 1),
                section_out,
            )
    layer_out = lax.all_to_all(produced, "pipe", split_axis=0, concat_axis=0, tiled=True)[
        last_section
    ]
    totals = zero_pack()
    produced_grads = jnp.zeros((sections, micro_rows, D), jnp.bfloat16)
    grad_arriving = jnp.zeros((micro_rows, D), jnp.bfloat16)
    for tick_num in range(tick_count):
        micro_idx = tick_num - (last_section - section_num)
        is_live = (micro_idx >= 0) & (micro_idx < sections)
        slot_idx = jnp.clip(micro_idx, 0, sections - 1)
        held_rows = lax.dynamic_index_in_dim(stash, slot_idx, 0, keepdims=False)
        fresh_grad = lax.dynamic_slice_in_dim(cotangent, slot_idx * micro_rows, micro_rows, 0)
        grad_in = jnp.where(section_num == last_section, fresh_grad, grad_arriving)
        grad_x, small, operands = lax.switch(
            jnp.where(is_live, section_num, sections), backward_kinds, held_rows, grad_in
        )
        mats = lax.switch(jnp.where(is_live, section_num % 2, 2), weight_kinds, operands)
        totals = jax.tree.map(jnp.add, totals, make_pack(small, mats))
        old_grad = lax.dynamic_index_in_dim(produced_grads, slot_idx, 0, keepdims=False)
        keep_grad = jnp.where(is_live & (section_num == 0), grad_x, old_grad)
        produced_grads = lax.dynamic_update_slice_in_dim(
            produced_grads, keep_grad[None], slot_idx, 0
        )
        if tick_num < tick_count - 1:
            grad_arriving = jax.tree.map(
                lambda part, own: part.astype(own.dtype),
                passed_along(shortened(grad_x), "pipe", -1),
                grad_x,
            )
    input_grad = lax.all_to_all(produced_grads, "pipe", split_axis=0, concat_axis=0, tiled=True)[0]
    summed_row = lax.psum_scatter(
        flatten_pack(totals, groups), "dp", scatter_dimension=0, tiled=True
    )
    leads = unflatten_pack(summed_row, groups)
    return (layer_out, input_grad, leads[0], leads[1], leads[2], leads[3], leads[4], leads[5])


def solution(mesh):
    in_specs = (
        P("dp", None),
        P("dp", None),
        P("pipe", None),
        P("pipe", None),
        P("pipe", None, None),
        P("pipe", None),
        P("pipe", None, None),
        P("pipe", None),
    )
    out_specs = (
        P(("dp", "pipe"), None),
        P(("dp", "pipe"), None),
        P("pipe", "dp"),
        P("pipe", "dp"),
        P("pipe", "dp", None),
        P("pipe", "dp"),
        P("pipe", None, "dp"),
        P("pipe", "dp"),
    )
    return jax.shard_map(
        on_device, mesh=mesh, in_specs=in_specs, out_specs=out_specs, check_vma=False
    )
```

profile of v0, /device:TPU:1, one launch (start us, length us, event | category | flops | bytes accessed | tf_op | source)
XLA Modules:
  0.0 2393.6 jit_solution(18428683025092855507)
XLA Ops:
  10.9 30.5 %conditional.21 = (bf16[588,768]{1,0:T(8,128)(2,1)}) conditional(s32[]{:T(128)} %clamp.63, (bf16[588,768]{1,0:T(8,128)(2,1)S(1)}, f32[1,768]{1,0:T(1,128)S(1)}, f32[1,768]{1,0:T(1,128)S(1)}, bf16[768,3072]{1,0:T(8,128)(2,1)}, f32[3072]{0:T(1024)S(1)}) %tuple.1059, (bf16[588,768]{1,0:T(8,128)(2,1)S(1)}, ...), branch_computations={%region_0.5_spmd, %region_5.8_spmd, %region_8.13_spmd, %region_13.... | conditional | flops 5675508224 | bytes 42145216 | solution.py:351
  47.2 50.1 %collective-permute-done = bf16[588,768]{1,0:T(8,128)(2,1)S(1)} collective-permute-done((bf16[588,768]{1,0:T(8,128)(2,1)}, bf16[588,768]{1,0:T(8,128)(2,1)S(1)}, u32[]{:S(2)}, u32[]{:S(2)}) %collective-permute-start) | collective-permute-done | bytes 903200 | tf_op jit(solution)/shard_map/ppermute | solution.py:23
  100.0 46.0 %conditional.22 = (bf16[588,768]{1,0:T(8,128)(2,1)}) conditional(s32[]{:T(128)} %clamp.64, (bf16[588,768]{1,0:T(8,128)(2,1)S(1)}, f32[1,768]{1,0:T(1,128)S(1)}, f32[1,768]{1,0:T(1,128)S(1)}, bf16[768,3072]{1,0:T(8,128)(2,1)}, f32[3072]{0:T(1024)S(1)}) %tuple.1063, (bf16[588,768]{1,0:T(8,128)(2,1)S(1)}, ...), branch_computations={%region_17.22_spmd, %region_22.25_spmd, %region_25.30_spmd, %regio... | conditional | flops 5675508224 | bytes 42145216 | solution.py:351
  149.2 29.1 %collective-permute-done.1 = bf16[588,768]{1,0:T(8,128)(2,1)S(1)} collective-permute-done((bf16[588,768]{1,0:T(8,128)(2,1)}, bf16[588,768]{1,0:T(8,128)(2,1)S(1)}, u32[]{:S(2)}, u32[]{:S(2)}) %collective-permute-start.1) | collective-permute-done | bytes 903200 | tf_op jit(solution)/shard_map/ppermute | solution.py:23
  180.9 46.3 %conditional.23 = (bf16[588,768]{1,0:T(8,128)(2,1)}) conditional(s32[]{:T(128)} %clamp.65, (bf16[588,768]{1,0:T(8,128)(2,1)S(1)}, f32[1,768]{1,0:T(1,128)S(1)}, f32[1,768]{1,0:T(1,128)S(1)}, bf16[768,3072]{1,0:T(8,128)(2,1)}, f32[3072]{0:T(1024)S(1)}) %tuple.1070, (bf16[588,768]{1,0:T(8,128)(2,1)S(1)}, ...), branch_computations={%region_34.39_spmd, %region_39.42_spmd, %region_42.47_spmd, %regio... | conditional | flops 5675508224 | bytes 42145216 | solution.py:351
  230.5 28.4 %collective-permute-done.2 = bf16[588,768]{1,0:T(8,128)(2,1)S(1)} collective-permute-done((bf16[588,768]{1,0:T(8,128)(2,1)}, bf16[588,768]{1,0:T(8,128)(2,1)S(1)}, u32[]{:S(2)}, u32[]{:S(2)}) %collective-permute-start.2) | collective-permute-done | bytes 903200 | tf_op jit(solution)/shard_map/ppermute | solution.py:23
  261.5 46.3 %conditional.24 = (bf16[588,768]{1,0:T(8,128)(2,1)}) conditional(s32[]{:T(128)} %clamp.66, (bf16[588,768]{1,0:T(8,128)(2,1)S(1)}, f32[1,768]{1,0:T(1,128)S(1)}, f32[1,768]{1,0:T(1,128)S(1)}, bf16[768,3072]{1,0:T(8,128)(2,1)}, f32[3072]{0:T(1024)S(1)}) %tuple.1071, (bf16[588,768]{1,0:T(8,128)(2,1)S(1)}, ...), branch_computations={%region_51.56_spmd, %region_56.59_spmd, %region_59.64_spmd, %regio... | conditional | flops 5675508224 | bytes 42145216 | solution.py:351
  311.5 28.3 %collective-permute-done.3 = bf16[588,768]{1,0:T(8,128)(2,1)S(1)} collective-permute-done((bf16[588,768]{1,0:T(8,128)(2,1)}, bf16[588,768]{1,0:T(8,128)(2,1)S(1)}, u32[]{:S(2)}, u32[]{:S(2)}) %collective-permute-start.3) | collective-permute-done | bytes 903200 | tf_op jit(solution)/shard_map/ppermute | solution.py:23
  342.4 46.0 %conditional.25 = (bf16[588,768]{1,0:T(8,128)(2,1)}) conditional(s32[]{:T(128)} %clamp.67, (bf16[588,768]{1,0:T(8,128)(2,1)S(1)}, f32[1,768]{1,0:T(1,128)S(1)}, f32[1,768]{1,0:T(1,128)S(1)}, bf16[768,3072]{1,0:T(8,128)(2,1)}, f32[3072]{0:T(1024)S(1)}) %tuple.1075, (bf16[588,768]{1,0:T(8,128)(2,1)S(1)}, ...), branch_computations={%region_68.73_spmd, %region_73.76_spmd, %region_76.81_spmd, %regio... | conditional | flops 5675508224 | bytes 42145216 | solution.py:351
  404.3 34.7 %conditional.26 = (bf16[588,768]{1,0:T(8,128)(2,1)}) conditional(s32[]{:T(128)} %clamp.68, (bf16[588,768]{1,0:T(8,128)(2,1)S(1)}, f32[1,768]{1,0:T(1,128)S(1)}, f32[1,768]{1,0:T(1,128)S(1)}, bf16[768,3072]{1,0:T(8,128)(2,1)}, f32[3072]{0:T(1024)S(1)}) %tuple.1079, (bf16[588,768]{1,0:T(8,128)(2,1)S(1)}, ...), branch_computations={%region_85.90_spmd, %region_90.93_spmd, %region_93.98_spmd, %regio... | conditional | flops 5675508224 | bytes 42145216 | solution.py:351
  439.0 37.2 %collective-permute-start.5 = (bf16[588,768]{1,0:T(8,128)(2,1)}, bf16[588,768]{1,0:T(8,128)(2,1)S(1)}, u32[]{:S(2)}, u32[]{:S(2)}) collective-permute-start(bf16[588,768]{1,0:T(8,128)(2,1)} %get-tuple-element.2533), channel_id=1, source_target_pairs={{0,1},{1,2},{2,3},{4,5},{5,6},{6,7},{8,9},{9,10},{10,11},{12,13},{... | collective-permute-start | bytes 2709512 | tf_op jit(solution)/shard_map/ppermute | solution.py:23
  494.9 32.8 %conditional.28 = (bf16[588,768]{1,0:T(8,128)(2,1)}, f32[768]{0:T(1024)S(1)}, f32[768]{0:T(1024)S(1)}, f32[3072]{0:T(1024)S(1)}, f32[768]{0:T(1024)S(1)}, /*inde...) conditional(s32[]{:T(128)} %clamp.70, ...), branch_computations={%region_119.131_spmd, %region_131.140_spmd, %region_140.152_spmd, ... | conditional | flops 8488870912 | bytes 180257184 | solution.py:379
  544.6 32.7 %conditional.29 = (bf16[588,768]{1,0:T(8,128)(2,1)}, f32[768]{0:T(1024)S(1)}, f32[768]{0:T(1024)S(1)}, f32[3072]{0:T(1024)S(1)}, f32[768]{0:T(1024)S(1)}, /*inde...) conditional(s32[]{:T(128)} %clamp.71, ...), branch_computations={%region_162.174_spmd, %region_174.183_spmd, %region_183.195_spmd, ... | conditional | flops 8488870912 | bytes 180257184 | solution.py:379
  579.3 149.2 %collective-permute-done.7 = bf16[588,768]{1,0:T(8,128)(2,1)S(1)} collective-permute-done((bf16[588,768]{1,0:T(8,128)(2,1)}, bf16[588,768]{1,0:T(8,128)(2,1)S(1)}, u32[]{:S(2)}, u32[]{:S(2)}) %collective-permute-start.7) | collective-permute-done | bytes 903200 | tf_op jit(solution)/shard_map/ppermute | solution.py:23
  730.1 63.9 %conditional.30 = (bf16[588,768]{1,0:T(8,128)(2,1)}, f32[768]{0:T(1024)S(1)}, f32[768]{0:T(1024)S(1)}, f32[3072]{0:T(1024)S(1)}, f32[768]{0:T(1024)S(1)}, /*inde...) conditional(s32[]{:T(128)} %clamp.72, ...), branch_computations={%region_205.217_spmd, %region_217.226_spmd, %region_226.238_spmd, ... | conditional | flops 8488870912 | bytes 180257184 | solution.py:379
  796.0 103.9 %collective-permute-done.8 = bf16[588,768]{1,0:T(8,128)(2,1)S(1)} collective-permute-done((bf16[588,768]{1,0:T(8,128)(2,1)}, bf16[588,768]{1,0:T(8,128)(2,1)S(1)}, u32[]{:S(2)}, u32[]{:S(2)}) %collective-permute-start.8) | collective-permute-done | bytes 903200 | tf_op jit(solution)/shard_map/ppermute | solution.py:23
  901.5 63.8 %conditional.31 = (bf16[588,768]{1,0:T(8,128)(2,1)}, f32[768]{0:T(1024)S(1)}, f32[768]{0:T(1024)S(1)}, f32[3072]{0:T(1024)S(1)}, f32[768]{0:T(1024)S(1)}, /*inde...) conditional(s32[]{:T(128)} %clamp.73, ...), branch_computations={%region_248.260_spmd, %region_260.269_spmd, %region_269.281_spmd, ... | conditional | flops 8488870912 | bytes 180257184 | solution.py:379
  976.2 95.4 %collective-permute-done.9 = bf16[588,768]{1,0:T(8,128)(2,1)S(1)} collective-permute-done((bf16[588,768]{1,0:T(8,128)(2,1)}, bf16[588,768]{1,0:T(8,128)(2,1)S(1)}, u32[]{:S(2)}, u32[]{:S(2)}) %collective-permute-start.9) | collective-permute-done | bytes 903200 | tf_op jit(solution)/shard_map/ppermute | solution.py:23
  1073.1 64.7 %conditional.32 = (bf16[588,768]{1,0:T(8,128)(2,1)}, f32[768]{0:T(1024)S(1)}, f32[768]{0:T(1024)S(1)}, f32[3072]{0:T(1024)S(1)}, f32[768]{0:T(1024)S(1)}, /*inde...) conditional(s32[]{:T(128)} %clamp.74, ...), branch_computations={%region_291.303_spmd, %region_303.312_spmd, %region_312.324_spmd, ... | conditional | flops 8488870912 | bytes 180257184 | solution.py:379
  1157.5 86.9 %collective-permute-done.10 = bf16[588,768]{1,0:T(8,128)(2,1)S(1)} collective-permute-done((bf16[588,768]{1,0:T(8,128)(2,1)}, bf16[588,768]{1,0:T(8,128)(2,1)S(1)}, u32[]{:S(2)}, u32[]{:S(2)}) %collective-permute-start.10) | collective-permute-done | bytes 903200 | tf_op jit(solution)/shard_map/ppermute | solution.py:23
  1245.9 59.9 %conditional.33 = (bf16[588,768]{1,0:T(8,128)(2,1)}, f32[768]{0:T(1024)S(1)}, f32[768]{0:T(1024)S(1)}, f32[3072]{0:T(1024)S(1)}, f32[768]{0:T(1024)S(1)}, /*inde...) conditional(s32[]{:T(128)} %clamp.75, ...), branch_computations={%region_334.346_spmd, %region_346.355_spmd, %region_355.367_spmd, ... | conditional | flops 8488870912 | bytes 180251040 | solution.py:379
  1355.2 26.2 %conditional.37 = (f32[768,3072]{1,0:T(8,128)}, f32[3072,768]{1,0:T(8,128)}) conditional(s32[]{:T(128)} %clamp.79, (bf16[588,3072]{1,0:T(8,128)(2,1)}, bf16[588,768]{1,0:T(8,128)(2,1)}, bf16[588,3072]{1,0:T(8,128)(2,1)}) %tuple.385, (bf16[588,768]{1,0:T(8,128)(2,1)}, bf16[588,3072]{1,0:T(8,128)(2,1)}, ...), branch_computations={%region_426.427_spmd, %region_427.428_spmd, %region_428.429_spmd} | conditional | flops 5549064192 | bytes 43204628 | solution.py:382
  1381.4 26.7 %conditional.38 = (f32[768,3072]{1,0:T(8,128)}, f32[3072,768]{1,0:T(8,128)}) conditional(s32[]{:T(128)} %clamp.80, (bf16[588,3072]{1,0:T(8,128)(2,1)}, bf16[588,768]{1,0:T(8,128)(2,1)}, bf16[588,3072]{1,0:T(8,128)(2,1)}) %tuple.388, (bf16[588,768]{1,0:T(8,128)(2,1)}, bf16[588,3072]{1,0:T(8,128)(2,1)}, ...), branch_computations={%region_429.430_spmd, %region_430.431_spmd, %region_431.432_spmd} | conditional | flops 5549064192 | bytes 43204628 | solution.py:382
  1453.0 31.1 %conditional.34 = (bf16[588,768]{1,0:T(8,128)(2,1)S(1)}, f32[768]{0:T(1024)S(1)}, f32[768]{0:T(1024)S(1)}, f32[3072]{0:T(1024)S(1)}, f32[768]{0:T(1024)S(1)}, /*...) conditional(s32[]{:T(128)} %clamp.76, ...), branch_computations={%region_377.389_spmd, %region_389.398_spmd, %region_398.410_spmd, ... | conditional | flops 8488870912 | bytes 176644480 | solution.py:379
  1500.2 26.6 %add_add_fusion = f32[768,3072]{1,0:T(8,128)} fusion(f32[768,3072]{1,0:T(8,128)} %get-tuple-element.1379, f32[768,3072]{1,0:T(8,128)} %get-tuple-element.1374, f32[768,3072]{1,0:T(8,128)} %get-tuple-element.1369, f32[768,3072]{1,0:T(8,128)} %get-tuple-element.1364, f32[768,3072]{1,0:T(8,128)} %get-tuple-element.1359, f32[768,3072]{1,0:T(8,128)} %get-tuple-element.1349, ...), kind=kLoop, calls=%fused_computation.2766 | loop fusion | flops 14155776 | bytes 75497472 | tf_op jit(solution)/shard_map/add | solution.py:383
  1535.8 25.3 %add_bitcast_fusion = f32[768,3072]{0,1:T(8,128)} fusion(f32[3072,768]{1,0:T(8,128)} %get-tuple-element.1393, f32[3072,768]{1,0:T(8,128)} %copy-done.10, f32[3072,768]{1,0:T(8,128)} %copy-done.9, f32[3072,768]{1,0:T(8,128)} %get-tuple-element.1390, f32[3072,768]{1,0:T(8,128)} %get-tuple-element.1389, f32[3072,768]{1,0:T(8,128)} %get-tuple-element.1387, ...), kind=kLoop, calls=%fused_computation.2765 | loop fusion | flops 14155776 | bytes 75497472 | tf_op jit(solution)/shard_map/transpose | solution.py:281
  1582.5 26.5 %dynamic-update-slice.44 = f32[8,590496]{1,0:T(8,128)} dynamic-update-slice(f32[8,590496]{1,0:T(8,128)} %dynamic-update-slice.43, f32[8,294912]{1,0:T(8,128)} %reshape.1580, s32[]{} %constant.2848, s32[]{} %constant.2850) | dynamic-update-slice | bytes 18874372
  1610.5 26.1 %dynamic-update-slice.46 = f32[8,590496]{1,0:T(8,128)} dynamic-update-slice(f32[8,590496]{1,0:T(8,128)} %dynamic-update-slice.45, f32[8,294912]{1,0:T(8,128)} %reshape.1582, s32[]{} %constant.2848, s32[]{} %constant.2852) | dynamic-update-slice | bytes 18874372
  1644.5 32.0 %conditional.27 = (bf16[588,768]{1,0:T(8,128)(2,1)}) conditional(s32[]{:T(128)} %clamp.69, (bf16[588,768]{1,0:T(8,128)(2,1)S(1)}, f32[1,768]{1,0:T(1,128)S(1)}, f32[1,768]{1,0:T(1,128)S(1)}, bf16[768,3072]{1,0:T(8,128)(2,1)}, f32[3072]{0:T(1024)S(1)}) %tuple.1111, (bf16[588,768]{1,0:T(8,128)(2,1)S(1)}, ...), branch_computations={%region_102.107_spmd, %region_107.110_spmd, %region_110.115_spmd, ... | conditional | flops 5675508224 | bytes 42145216 | solution.py:351
  1677.7 159.4 %all-to-all-start = ((bf16[4,588,768]{2,1,0:T(8,128)(2,1)}), bf16[4,588,768]{2,1,0:T(8,128)(2,1)}, u32[]{:S(2)}, u32[]{:S(2)}) async-start(bf16[4,588,768]{2,1,0:T(8,128)(2,1)} %bitcast_dynamic-update-slice_fusion.14), calls=%async_computation | async-start | bytes 7274496 | tf_op jit(solution)/shard_map/all_to_all | solution.py:366
  1887.0 38.7 %all-to-all-done.1 = bf16[4,588,768]{2,1,0:T(8,128)(2,1)} async-done(((bf16[4,588,768]{2,1,0:T(8,128)(2,1)}), bf16[4,588,768]{2,1,0:T(8,128)(2,1)}, u32[]{:S(2)}, u32[]{:S(2)}) %all-to-all-start.1) | async-done | bytes 3612704 | tf_op jit(solution)/shard_map/all_to_all | solution.py:395
  1927.8 436.3 %all-reduce.17.cloned.1.call-done = f32[8,590496]{1,0:T(8,128)} async-done(((f32[8,590496]{1,0:T(8,128)}), f32[8,590496]{1,0:T(8,128)}) %all-reduce.17.cloned.1.call-update) | async-done | bytes 18895888
  (409 shorter events, 733.1 us)
Async XLA Ops:
  7.2 2356.9 %all-reduce.17.cloned.1.call-start = ((), (), s32[]{:S(2)}) async-start(), calls=%async_computation.2 | async-start | bytes 37797888
  41.4 55.9 %collective-permute-start = (bf16[588,768]{1,0:T(8,128)(2,1)}, bf16[588,768]{1,0:T(8,128)(2,1)S(1)}, u32[]{:S(2)}, u32[]{:S(2)}) collective-permute-start(bf16[588,768]{1,0:T(8,128)(2,1)} %get-tuple-element.2528), channel_id=1, source_target_pairs={{0,1},{1,2},{2,3},{4,5},{5,6},{6,7},{8,9},{9,10},{10,11},{12,13},{... | collective-permute-start | bytes 2709512 | tf_op jit(solution)/shard_map/ppermute | solution.py:23
  146.0 32.3 %collective-permute-start.1 = (bf16[588,768]{1,0:T(8,128)(2,1)}, bf16[588,768]{1,0:T(8,128)(2,1)S(1)}, u32[]{:S(2)}, u32[]{:S(2)}) collective-permute-start(bf16[588,768]{1,0:T(8,128)(2,1)} %get-tuple-element.2529), channel_id=1, source_target_pairs={{0,1},{1,2},{2,3},{4,5},{5,6},{6,7},{8,9},{9,10},{10,11},{12,13},{... | collective-permute-start | bytes 2709512 | tf_op jit(solution)/shard_map/ppermute | solution.py:23
  227.3 31.6 %collective-permute-start.2 = (bf16[588,768]{1,0:T(8,128)(2,1)}, bf16[588,768]{1,0:T(8,128)(2,1)S(1)}, u32[]{:S(2)}, u32[]{:S(2)}) collective-permute-start(bf16[588,768]{1,0:T(8,128)(2,1)} %get-tuple-element.2530), channel_id=1, source_target_pairs={{0,1},{1,2},{2,3},{4,5},{5,6},{6,7},{8,9},{9,10},{10,11},{12,13},{... | collective-permute-start | bytes 2709512 | tf_op jit(solution)/shard_map/ppermute | solution.py:23
  307.8 32.0 %collective-permute-start.3 = (bf16[588,768]{1,0:T(8,128)(2,1)}, bf16[588,768]{1,0:T(8,128)(2,1)S(1)}, u32[]{:S(2)}, u32[]{:S(2)}) collective-permute-start(bf16[588,768]{1,0:T(8,128)(2,1)} %get-tuple-element.2531), channel_id=1, source_target_pairs={{0,1},{1,2},{2,3},{4,5},{5,6},{6,7},{8,9},{9,10},{10,11},{12,13},{... | collective-permute-start | bytes 2709512 | tf_op jit(solution)/shard_map/ppermute | solution.py:23
  388.5 13.2 collective-permute-start.4
  439.0 47.7 %collective-permute-start.5 = (bf16[588,768]{1,0:T(8,128)(2,1)}, bf16[588,768]{1,0:T(8,128)(2,1)S(1)}, u32[]{:S(2)}, u32[]{:S(2)}) collective-permute-start(bf16[588,768]{1,0:T(8,128)(2,1)} %get-tuple-element.2533), channel_id=1, source_target_pairs={{0,1},{1,2},{2,3},{4,5},{5,6},{6,7},{8,9},{9,10},{10,11},{12,13},{... | collective-permute-start | bytes 2709512 | tf_op jit(solution)/shard_map/ppermute | solution.py:23
  527.8 15.3 collective-permute-start.6
  544.6 185.5 %copy-start.4 = (bf16[588,768]{1,0:T(8,128)(2,1)S(1)}, bf16[588,768]{1,0:T(8,128)(2,1)}, u32[]{:S(2)}) copy-start(bf16[588,768]{1,0:T(8,128)(2,1)} %get-tuple-element.2166) | copy-start | bytes 2709508
  577.3 152.8 %copy-start.110 = (f32[3072]{0:T(1024)}, f32[3072]{0:T(1024)S(1)}, u32[]{:S(2)}) copy-start(f32[3072]{0:T(1024)S(1)} %get-tuple-element.1381) | copy-start | bytes 36868
  577.4 152.8 %copy-start.122 = (f32[768]{0:T(1024)}, f32[768]{0:T(1024)S(1)}, u32[]{:S(2)}) copy-start(f32[768]{0:T(1024)S(1)} %get-tuple-element.1395) | copy-start | bytes 9220
  577.4 152.8 %copy-start.134 = (f32[768]{0:T(1024)}, f32[768]{0:T(1024)S(1)}, u32[]{:S(2)}) copy-start(f32[768]{0:T(1024)S(1)} %get-tuple-element.1339) | copy-start | bytes 9220
  577.4 152.8 %copy-start.146 = (f32[768]{0:T(1024)}, f32[768]{0:T(1024)S(1)}, u32[]{:S(2)}) copy-start(f32[768]{0:T(1024)S(1)} %get-tuple-element.1332) | copy-start | bytes 9220
  577.4 151.2 %collective-permute-start.7 = (bf16[588,768]{1,0:T(8,128)(2,1)}, bf16[588,768]{1,0:T(8,128)(2,1)S(1)}, u32[]{:S(2)}, u32[]{:S(2)}) collective-permute-start(bf16[588,768]{1,0:T(8,128)(2,1)} %get-tuple-element.1325), channel_id=1, source_target_pairs={{1,0},{2,1},{3,2},{5,4},{6,5},{7,6},{9,8},{10,9},{11,10},{13,12},{... | collective-permute-start | bytes 2709512 | tf_op jit(solution)/shard_map/ppermute | solution.py:23
  730.1 171.4 %copy-start.3 = (bf16[588,768]{1,0:T(8,128)(2,1)S(1)}, bf16[588,768]{1,0:T(8,128)(2,1)}, u32[]{:S(2)}) copy-start(bf16[588,768]{1,0:T(8,128)(2,1)} %get-tuple-element.2165) | copy-start | bytes 2709508
  794.1 107.4 %copy-start.112 = (f32[3072]{0:T(1024)}, f32[3072]{0:T(1024)S(1)}, u32[]{:S(2)}) copy-start(f32[3072]{0:T(1024)S(1)} %get-tuple-element.1382) | copy-start | bytes 36868
  794.1 105.8 %collective-permute-start.8 = (bf16[588,768]{1,0:T(8,128)(2,1)}, bf16[588,768]{1,0:T(8,128)(2,1)S(1)}, u32[]{:S(2)}, u32[]{:S(2)}) collective-permute-start(bf16[588,768]{1,0:T(8,128)(2,1)} %get-tuple-element.1326), channel_id=1, source_target_pairs={{1,0},{2,1},{3,2},{5,4},{6,5},{7,6},{9,8},{10,9},{11,10},{13,12},{... | collective-permute-start | bytes 2709512 | tf_op jit(solution)/shard_map/ppermute | solution.py:23
  901.5 171.6 %copy-start.2 = (bf16[588,768]{1,0:T(8,128)(2,1)S(1)}, bf16[588,768]{1,0:T(8,128)(2,1)}, u32[]{:S(2)}) copy-start(bf16[588,768]{1,0:T(8,128)(2,1)} %get-tuple-element.2164) | copy-start | bytes 2709508
  965.4 107.7 %copy-start.114 = (f32[3072]{0:T(1024)}, f32[3072]{0:T(1024)S(1)}, u32[]{:S(2)}) copy-start(f32[3072]{0:T(1024)S(1)} %get-tuple-element.1383) | copy-start | bytes 36868
  965.4 107.7 %copy-start.126 = (f32[768]{0:T(1024)}, f32[768]{0:T(1024)S(1)}, u32[]{:S(2)}) copy-start(f32[768]{0:T(1024)S(1)} %get-tuple-element.1397) | copy-start | bytes 9220
  965.4 107.7 %copy-start.138 = (f32[768]{0:T(1024)}, f32[768]{0:T(1024)S(1)}, u32[]{:S(2)}) copy-start(f32[768]{0:T(1024)S(1)} %get-tuple-element.1341) | copy-start | bytes 9220
  965.4 107.7 %copy-start.150 = (f32[768]{0:T(1024)}, f32[768]{0:T(1024)S(1)}, u32[]{:S(2)}) copy-start(f32[768]{0:T(1024)S(1)} %get-tuple-element.1334) | copy-start | bytes 9220
  965.4 106.2 %collective-permute-start.9 = (bf16[588,768]{1,0:T(8,128)(2,1)}, bf16[588,768]{1,0:T(8,128)(2,1)S(1)}, u32[]{:S(2)}, u32[]{:S(2)}) collective-permute-start(bf16[588,768]{1,0:T(8,128)(2,1)} %get-tuple-element.1327), channel_id=1, source_target_pairs={{1,0},{2,1},{3,2},{5,4},{6,5},{7,6},{9,8},{10,9},{11,10},{13,12},{... | collective-permute-start | bytes 2709512 | tf_op jit(solution)/shard_map/ppermute | solution.py:23
  1073.1 172.8 %copy-start.1 = (bf16[588,768]{1,0:T(8,128)(2,1)S(1)}, bf16[588,768]{1,0:T(8,128)(2,1)}, u32[]{:S(2)}) copy-start(bf16[588,768]{1,0:T(8,128)(2,1)} %get-tuple-element.2163) | copy-start | bytes 2709508
  1137.8 108.0 %copy-start.116 = (f32[3072]{0:T(1024)}, f32[3072]{0:T(1024)S(1)}, u32[]{:S(2)}) copy-start(f32[3072]{0:T(1024)S(1)} %get-tuple-element.1384) | copy-start | bytes 36868
  1137.8 108.0 %copy-start.128 = (f32[768]{0:T(1024)}, f32[768]{0:T(1024)S(1)}, u32[]{:S(2)}) copy-start(f32[768]{0:T(1024)S(1)} %get-tuple-element.1398) | copy-start | bytes 9220
  1137.9 108.0 %copy-start.140 = (f32[768]{0:T(1024)}, f32[768]{0:T(1024)S(1)}, u32[]{:S(2)}) copy-start(f32[768]{0:T(1024)S(1)} %get-tuple-element.1342) | copy-start | bytes 9220
  1137.9 108.0 %copy-start.152 = (f32[768]{0:T(1024)}, f32[768]{0:T(1024)S(1)}, u32[]{:S(2)}) copy-start(f32[768]{0:T(1024)S(1)} %get-tuple-element.1335) | copy-start | bytes 9220
  1137.9 106.5 %collective-permute-start.10 = (bf16[588,768]{1,0:T(8,128)(2,1)}, bf16[588,768]{1,0:T(8,128)(2,1)S(1)}, u32[]{:S(2)}, u32[]{:S(2)}) collective-permute-start(bf16[588,768]{1,0:T(8,128)(2,1)} %get-tuple-element.1328), channel_id=1, source_target_pairs={{1,0},{2,1},{3,2},{5,4},{6,5},{7,6},{9,8},{10,9},{11,10},{13,12},{... | collective-permute-start | bytes 2709512 | tf_op jit(solution)/shard_map/ppermute | solution.py:23
  1305.8 143.2 %collective-permute-start.11 = (bf16[588,768]{1,0:T(8,128)(2,1)}, bf16[588,768]{1,0:T(8,128)(2,1)}, u32[]{:S(2)}, u32[]{:S(2)}) collective-permute-start(bf16[588,768]{1,0:T(8,128)(2,1)} %get-tuple-element.1329), channel_id=1, source_target_pairs={{1,0},{2,1},{3,2},{5,4},{6,5},{7,6},{9,8},{10,9},{11,10},{13,12},{... | collective-permute-start | bytes 2709512 | tf_op jit(solution)/shard_map/ppermute | solution.py:23
  1677.7 200.9 %all-to-all-start = ((bf16[4,588,768]{2,1,0:T(8,128)(2,1)}), bf16[4,588,768]{2,1,0:T(8,128)(2,1)}, u32[]{:S(2)}, u32[]{:S(2)}) async-start(bf16[4,588,768]{2,1,0:T(8,128)(2,1)} %bitcast_dynamic-update-slice_fusion.14), calls=%async_computation | async-start | bytes 7274496 | tf_op jit(solution)/shard_map/all_to_all | solution.py:366
  1878.6 47.1 %all-to-all-start.1 = ((bf16[4,588,768]{2,1,0:T(8,128)(2,1)}), bf16[4,588,768]{2,1,0:T(8,128)(2,1)}, u32[]{:S(2)}, u32[]{:S(2)}) async-start(bf16[4,588,768]{2,1,0:T(8,128)(2,1)} %bitcast_dynamic-update-slice_fusion), calls=%async_computation.1 | async-start | bytes 7274496 | tf_op jit(solution)/shard_map/all_to_all | solution.py:395
  (73 other events, 1687.3 us)
Sparse Core Ops, SparseCore 0:
  1638.2 725.8 all-reduce.16
where the time goes:
time: 2410 us; the launch traced here: 2390 us
  waiting for transfers between devices  1100 us (46%)
  loops' own time  374 us (16%)
  matrix products  313 us (13%)
  starting transfers between devices  275 us (11%)
  local copies, waits for them, and re-layouts  203 us (8%)
  other arithmetic  111 us (5%)
    ppermute x12, waiting for transfers between devices, passed_along(): return lax.ppermute(block, axis, route)  602 us
    unnamed x2, waiting for transfers between devices  436 us
    dot_general x8, matrix products, matmul(): return jnp.dot(former, latter, preferred_element_type=jnp.float32)  187 us
    another operation x7, loops' own time, on_device(): lax.switch(jnp.where(is_live, section_num, sections), forward_kinds, sect...  177 us
    another operation x7, loops' own time, on_device(): lax.switch(jnp.where(is_live, section_num, sections), backward_kinds, hel...  163 us
    all_to_all x1, starting transfers between devices, on_device(): lax.all_to_all(produced, 'pipe', split_axis=0, concat_axis=0, tiled=True)  159 us
    ppermute x12, starting transfers between devices, passed_along(): return lax.ppermute(block, axis, route)  110 us
    dot_general x8, matrix products, outer_sum(): lax.dot_general(former, latter, (((0,), (0,)), ((), ())), preferred_eleme...  69.5 us
  transfers between devices with their start and end apart: 15, of which 14 were waited for; matrix products, arithmetic and copies ran while one was open for 5% of the time, Pallas kernels for 0%

commit v1 on v0

v1 whole, which is shorter than its diff:
```python
import functools

import jax
import jax.experimental.pallas as pl
import jax.experimental.pallas.tpu as pltpu
import jax.numpy as jnp
from jax import lax
from jax.sharding import PartitionSpec as P

D = 768
FF = 3072
PATCHES = 49
PAD = 64
EPS = 1e-05
SCALE = 32 ** (-0.5)
MICROS = 4
MEMBERS = 8
BLOCK = D // MEMBERS
WIDE = 384
MESH = pl.DeviceIdType.MESH
BF = jnp.bfloat16
F32 = jnp.float32


def dot(a, b, ca, cb):
    return lax.dot_general(a, b, (((ca,), (cb,)), ((), ())), preferred_element_type=F32)


def gelu_pair(h):
    t = 1.0 / (1.0 + 0.3275911 * 0.7071067811865476 * jnp.abs(h))
    poly = t * (0.127414796 + t * (-0.142248368 + t * (0.7107068705 + t * (-0.7265760135 + t * 0.5307027145))))
    bell = jnp.exp(-0.5 * h * h)
    tail = poly * bell
    cdf = jnp.where(h >= 0, 1.0 - tail, tail)
    return h * cdf, cdf + h * (0.3989422804014327 * bell)


def norm_parts(x):
    center = x - jnp.mean(x, -1, keepdims=True)
    inverse = lax.rsqrt(jnp.mean(center * center, -1, keepdims=True) + EPS)
    return center * inverse, inverse


def head_masks(width):
    lane = lax.broadcasted_iota(jnp.int32, (1, width), 1) // 32
    return [lane == h for h in range(width // 32)]


def spread(block, masks):
    return jnp.concatenate([jnp.where(m, block, jnp.zeros_like(block)) for m in masks], 0)


def gather_heads(stacked, masks):
    total = None
    for h, m in enumerate(masks):
        part = jnp.where(m, stacked[PAD * h : PAD * (h + 1)], 0.0)
        total = part if total is None else total + part
    return total


def window_forward(q, k, v):
    eight, four = head_masks(256), head_masks(128)
    scores = dot(k, spread(q, eight), 1, 1)
    row = lax.broadcasted_iota(jnp.int32, (PAD, 1), 0)
    scores = jnp.where(row < PATCHES, scores, -1e30)
    top = jnp.max(scores, 0, keepdims=True)
    e = jnp.exp((scores - top) * SCALE)
    probs = (e * (1.0 / jnp.sum(e, 0, keepdims=True))).astype(BF)
    halves = []
    for a in range(2):
        stacked = dot(probs[:, 256 * a : 256 * (a + 1)], v[:, 128 * a : 128 * (a + 1)], 0, 0)
        halves.append(gather_heads(stacked, four))
    return probs, jnp.concatenate(halves, 1)


def window_backward(q, k, v, probs, d_att):
    eight, four = head_masks(256), head_masks(128)
    d_wide = spread(d_att, eight)
    d_probs = dot(v, d_wide, 1, 1)
    p = probs.astype(F32)
    d_scores = p * (d_probs - jnp.sum(p * d_probs, 0, keepdims=True))
    d_scores = d_scores.astype(BF)
    d_v = dot(probs, d_wide, 1, 0)
    d_k = dot(d_scores, spread(q, eight), 1, 0) * SCALE
    halves = []
    for a in range(2):
        stacked = dot(d_scores[:, 256 * a : 256 * (a + 1)], k[:, 128 * a : 128 * (a + 1)], 0, 0)
        halves.append(gather_heads(stacked, four))
    return jnp.concatenate(halves, 1) * SCALE, d_k, d_v


def channel_forward(q, k, v):
    scores = dot(q, k, 0, 0)
    r = lax.broadcasted_iota(jnp.int32, (128, 128), 0) // 32
    c = lax.broadcasted_iota(jnp.int32, (128, 128), 1) // 32
    scores = jnp.where(r == c, scores, -1e30)
    e = jnp.exp((scores - jnp.max(scores, 1, keepdims=True)) * SCALE)
    probs = (e * (1.0 / jnp.sum(e, 1, keepdims=True))).astype(BF)
    return probs, dot(v, probs, 1, 1)


def channel_backward(q, k, v, probs, d_att):
    d_probs = dot(d_att, v, 0, 0)
    p = probs.astype(F32)
    d_scores = (p * (d_probs - jnp.sum(p * d_probs, 1, keepdims=True))).astype(BF)
    d_v = dot(d_att, probs, 1, 0)
    d_q = dot(k, d_scores, 1, 1) * SCALE
    d_k = dot(q, d_scores, 1, 0) * SCALE
    return d_q, d_k, d_v


def sections_kernel(
    micros, rows, real,
    x_ref, par_ref, w1_ref, w2_ref,
    lo_ref, ig_ref, left_ref, right_ref, small_ref,
    w1, w2, par, xs, arr, snd, fin, mid, slope, qkv, probs_w, probs_c,
    att_in, normed_a, att_low, normed_f, act, d_proj, g_mid, d_att, wide_tmp, acc, tmp,
    w_local, w_send, w_recv, x_sem, s_send, s_recv, f_send, f_recv, f_local, o_sem, keep_sem,
):
    dp, pipe = lax.axis_index("dp"), lax.axis_index("pipe")
    y, core = pipe // 2, pipe % 2
    sibling = (dp, 2 * y + 1 - core)
    across = (dp, 2 * (1 - y) + core)
    images = real // PATCHES
    half = micros // 2

    barrier = pltpu.get_barrier_semaphore()
    pl.semaphore_signal(barrier, inc=1, device_id=sibling, device_id_type=MESH)
    pl.semaphore_signal(barrier, inc=1, device_id=across, device_id_type=MESH)

    own_x = pltpu.make_async_copy(x_ref, xs, x_sem)
    own_x.start()
    own_1 = pltpu.make_async_copy(w1_ref, w1.at[core], w_local.at[0])
    own_1.start()
    own_2 = pltpu.make_async_copy(w2_ref, w2, w_local.at[1])
    own_p = pltpu.make_async_copy(par_ref, par.at[core], w_local.at[2])
    own_p.start()
    pl.semaphore_wait(barrier, 2)

    def to_sibling(src, dst, n):
        return pltpu.make_async_remote_copy(
            src_ref=src, dst_ref=dst, send_sem=w_send.at[n], recv_sem=w_recv.at[n],
            device_id=sibling, device_id_type=MESH,
        )

    send_p = to_sibling(par_ref, par.at[core], 2)
    send_1 = to_sibling(w1_ref, w1.at[core], 0)
    send_2 = to_sibling(w2_ref, w2, 1)
    send_p.start()
    send_1.start()

    @pl.when(core == 1)
    def _():
        send_2.start()
        own_2.start()

    small_ref[...] = jnp.zeros_like(small_ref)
    tmp[pl.ds(rows, tmp.shape[0] - rows), :] = jnp.zeros((tmp.shape[0] - rows, 3 * D), F32)
    own_x.wait()
    own_p.wait()
    to_sibling(par_ref, par.at[1 - core], 2).wait_recv()

    @pl.when(core == 0)
    def _():
        own_1.wait()

    @pl.when(core == 1)
    def _():
        to_sibling(w1_ref, w1.at[1 - core], 0).wait_recv()

    def feed_weights():
        @pl.when(core == 1)
        def _():
            own_1.wait()
            own_2.wait()

        @pl.when(core == 0)
        def _():
            to_sibling(w1_ref, w1.at[1 - core], 0).wait_recv()
            to_sibling(w2_ref, w2, 1).wait_recv()

    def out_rows(m):
        return pl.ds(pl.multiple_of(m * rows, 16), rows)

    def put_left(n, m, src):
        return pltpu.make_async_copy(src, left_ref.at[n, out_rows(m)], o_sem.at[n])

    def put_right(n, m, src, start):
        return pltpu.make_async_copy(
            src, right_ref.at[out_rows(m), pl.ds(start, src.shape[-1])], o_sem.at[4 + n]
        )

    kept_start = ((0, normed_f), (2, normed_a), (3, att_low))

    def wait_left(m, n, src):
        @pl.when(m > 0)
        def _():
            put_left(n, m, src).wait()

    def wait_right(m, n, src, start):
        @pl.when(m > 0)
        def _():
            put_right(n, m, src, start).wait()

    row = lax.broadcasted_iota(jnp.int32, (PAD, 1), 0)

    def stage(src, dst, first, cols):
        for i in range(images):
            for c in range(0, cols, D):
                part = src[PATCHES * i : PATCHES * i + PAD, c : c + D]
                dst[first + i, :, c : c + D] = jnp.where(row < PATCHES, part, 0.0).astype(BF)

    def attention_forward(m, x_in, spatial):
        x = x_in[m].astype(F32)
        scaled, _ = norm_parts(x)
        wait_left(m, 2, normed_a)
        normed_a[...] = (scaled * par[0, 1:2, :D] + par[0, 1:2, D : 2 * D]).astype(BF)
        put_left(2, m, normed_a).start()
        for c in range(0, 3 * D, D):
            tmp[0:rows, c : c + D] = dot(normed_a[...], w1[0, :, c : c + D], 1, 0) + par[0, 0:1, c : c + D]
        first = m * images if spatial else 0
        stage(tmp, qkv, first, 3 * D)

        def one_image(i, carry):
            if spatial:
                for g in range(3):
                    s = 256 * g
                    p, a = window_forward(
                        qkv[first + i, :, s : s + 256],
                        qkv[first + i, :, D + s : D + s + 256],
                        qkv[first + i, :, 2 * D + s : 2 * D + s + 256],
                    )
                    probs_w[first + i, :, 512 * g : 512 * (g + 1)] = p
                    att_in[i, :, s : s + 256] = a
            else:
                for g in range(6):
                    s = 128 * g
                    p, a = channel_forward(
                        qkv[first + i, :, s : s + 128],
                        qkv[first + i, :, D + s : D + s + 128],
                        qkv[first + i, :, 2 * D + s : 2 * D + s + 128],
                    )
                    probs_c[i, s : s + 128, :] = p
                    att_in[i, :, s : s + 128] = a
            return carry

        lax.fori_loop(0, images, one_image, 0)
        for i in range(images):
            acc[PATCHES * i : PATCHES * i + PAD, :] = att_in[i]
        acc[real:rows, :] = jnp.zeros((rows - real, D), F32)
        wait_left(m, 3, att_low)
        att_low[...] = acc[0:rows, :].astype(BF)
        put_left(3, m, att_low).start()
        branch = dot(att_low[...], w1[0, :, 3 * D :], 1, 0) + par[0, 0:1, 3 * D :]
        mid[m] = (x + branch).astype(BF)

    def feed_forward(m, dst):
        x = mid[m].astype(F32)
        scaled, _ = norm_parts(x)
        wait_left(m, 0, normed_f)
        normed_f[...] = (scaled * par[1, 1:2, :D] + par[1, 1:2, D : 2 * D]).astype(BF)
        put_left(0, m, normed_f).start()
        wait_right(m, 0, act, FF)
        acc[0:rows, :] = x + par[1, 1:2, 2 * D : 3 * D]
        for c in range(0, FF, D):
            hidden = dot(normed_f[...], w1[1, :, c : c + D], 1, 0) + par[1, 0:1, c : c + D]
            value, diff = gelu_pair(hidden)
            act[:, c : c + D] = value.astype(BF)
            slope[m, :, c : c + D] = diff.astype(BF)
            acc[0:rows, :] += dot(act[:, c : c + D], w2[c : c + D, :], 1, 0)
        put_right(0, m, act, FF).start()
        dst[m] = acc[0:rows, :].astype(BF)

    def norm_back(d_normed, x, gain, at):
        scaled, inverse = norm_parts(x)
        small_ref[at : at + 1, :D] += jnp.sum(d_normed * scaled, 0, keepdims=True)
        small_ref[at : at + 1, D : 2 * D] += jnp.sum(d_normed, 0, keepdims=True)
        d_scaled = d_normed * gain
        mean = jnp.mean(d_scaled, -1, keepdims=True)
        cross = jnp.mean(d_scaled * scaled, -1, keepdims=True)
        return inverse * (d_scaled - mean - scaled * cross)

    def keep_gout(m, g_in):
        return pltpu.make_async_copy(g_in.at[m], left_ref.at[1, out_rows(m)], keep_sem.at[0, m])

    def keep_hidden(m):
        return pltpu.make_async_copy(slope.at[m], right_ref.at[out_rows(m), pl.ds(0, FF)], keep_sem.at[1, m])

    def feed_backward(m, g_in):
        keep_gout(m, g_in).start()
        small_ref[3:4, 2 * D : 3 * D] += jnp.sum(g_in[m].astype(F32), 0, keepdims=True)
        for c in range(0, FF, D):
            d_act = dot(g_in[m], w2[c : c + D, :], 1, 1)
            d_hid = (d_act * slope[m, :, c : c + D].astype(F32)).astype(BF)
            slope[m, :, c : c + D] = d_hid
            small_ref[2:3, c : c + D] += jnp.sum(d_hid.astype(F32), 0, keepdims=True)
            back = dot(d_hid, w1[1, :, c : c + D], 1, 1)
            if c == 0:
                acc[0:rows, :] = back
            else:
                acc[0:rows, :] += back
        keep_hidden(m).start()
        back = norm_back(acc[0:rows, :], mid[m].astype(F32), par[1, 1:2, :D], 3)
        wait_right(m, 2, g_mid, 3 * FF - D)
        g_mid[...] = (g_in[m].astype(F32) + back).astype(BF)
        put_right(2, m, g_mid, 3 * FF - D).start()

    def attention_backward(m, x_in, dst, spatial):
        g = g_mid[...]
        small_ref[0:1, 3 * D :] += jnp.sum(g.astype(F32), 0, keepdims=True)
        acc[0:rows, :] = dot(g, w1[0, :, 3 * D :], 1, 1)
        stage(acc, d_att, 0, D)
        first = m * images if spatial else 0

        def one_image(i, carry):
            if spatial:
                for n in range(3):
                    s = 256 * n
                    d_q, d_k, d_v = window_backward(
                        qkv[first + i, :, s : s + 256],
                        qkv[first + i, :, D + s : D + s + 256],
                        qkv[first + i, :, 2 * D + s : 2 * D + s + 256],
                        probs_w[first + i, :, 512 * n : 512 * (n + 1)],
                        d_att[i, :, s : s + 256],
                    )
                    wide_tmp[i, :, s : s + 256] = d_q
                    wide_tmp[i, :, D + s : D + s + 256] = d_k
                    wide_tmp[i, :, 2 * D + s : 2 * D + s + 256] = d_v
            else:
                for n in range(6):
                    s = 128 * n
                    d_q, d_k, d_v = channel_backward(
                        qkv[first + i, :, s : s + 128],
                        qkv[first + i, :, D + s : D + s + 128],
                        qkv[first + i, :, 2 * D + s : 2 * D + s + 128],
                        probs_c[i, s : s + 128, :],
                        d_att[i, :, s : s + 128],
                    )
                    wide_tmp[i, :, s : s + 128] = d_q
                    wide_tmp[i, :, D + s : D + s + 128] = d_k
                    wide_tmp[i, :, 2 * D + s : 2 * D + s + 128] = d_v
            return carry

        lax.fori_loop(0, images, one_image, 0)
        for i in range(images):
            for c in range(0, 3 * D, D):
                tmp[PATCHES * i : PATCHES * i + PAD, c : c + D] = wide_tmp[i, :, c : c + D]
        tmp[real:rows, :] = jnp.zeros((rows - real, 3 * D), F32)
        wait_right(m, 1, d_proj, 2 * FF)
        d_proj[...] = tmp[0:rows, :].astype(BF)
        put_right(1, m, d_proj, 2 * FF).start()
        small_ref[0:1, : 3 * D] += jnp.sum(d_proj[...].astype(F32), 0, keepdims=True)
        d_normed = dot(d_proj[...], w1[0, :, : 3 * D], 1, 1)
        back = norm_back(d_normed, x_in[m].astype(F32), par[0, 1:2, :D], 1)
        dst[m] = (g.astype(F32) + back).astype(BF)

    def hop(m):
        return pltpu.make_async_remote_copy(
            src_ref=snd.at[m], dst_ref=arr.at[m], send_sem=s_send.at[m], recv_sem=s_recv.at[m],
            device_id=across, device_id_type=MESH,
        )

    def final_hop(m, ref, slot):
        return pltpu.make_async_remote_copy(
            src_ref=fin.at[m], dst_ref=ref.at[slot], send_sem=f_send.at[slot], recv_sem=f_recv.at[slot],
            device_id=across, device_id_type=MESH,
        )

    def final_own(m, ref, slot):
        return pltpu.make_async_copy(fin.at[m], ref.at[slot], f_local.at[slot])

    @pl.when(y == 0)
    def _():
        def forward(m, carry):
            attention_forward(m, xs, True)

            @pl.when(m == 0)
            def _():
                feed_weights()

            feed_forward(m, snd)
            hop(m).start()
            return carry

        lax.fori_loop(0, micros, forward, 0)

        def backward(m, carry):
            hop(m).wait_recv()
            feed_backward(m, arr)
            attention_backward(m, xs, fin, True)

            @pl.when(m < half)
            def _():
                final_hop(m, ig_ref, m).start()

            @pl.when(m >= half)
            def _():
                final_own(m, ig_ref, m - half).start()

            return carry

        lax.fori_loop(0, micros, backward, 0)

        def finish(n, carry):
            final_hop(n, ig_ref, n).wait_send()
            final_hop(n, lo_ref, n).wait_recv()
            final_own(n, ig_ref, n).wait()
            return carry

        lax.fori_loop(0, half, finish, 0)

        def kept(m, carry):
            keep_gout(m, arr).wait()
            return carry

        lax.fori_loop(0, micros, kept, 0)

    @pl.when(y == 1)
    def _():
        def both(m, carry):
            hop(m).wait_recv()
            attention_forward(m, arr, False)

            @pl.when(m == 0)
            def _():
                feed_weights()

            feed_forward(m, fin)

            @pl.when(m < half)
            def _():
                final_own(m, lo_ref, m).start()

            feed_backward(m, xs)
            attention_backward(m, arr, snd, False)
            hop(m).start()

            @pl.when(m >= half)
            def _():
                final_hop(m, lo_ref, m - half).start()

            return carry

        lax.fori_loop(0, micros, both, 0)

        def finish(n, carry):
            final_hop(n, lo_ref, n).wait_send()
            final_hop(n, ig_ref, n).wait_recv()
            final_own(n, lo_ref, n).wait()
            return carry

        lax.fori_loop(0, half, finish, 0)

        def kept(m, carry):
            keep_gout(m, xs).wait()
            return carry

        lax.fori_loop(0, micros, kept, 0)

    def sent(m, carry):
        hop(m).wait_send()
        keep_hidden(m).wait()
        return carry

    lax.fori_loop(0, micros, sent, 0)
    last = micros - 1
    put_left(0, last, normed_f).wait()
    put_left(2, last, normed_a).wait()
    put_left(3, last, att_low).wait()
    put_right(0, last, act, FF).wait()
    put_right(1, last, d_proj, 2 * FF).wait()
    put_right(2, last, g_mid, 3 * FF - D).wait()
    send_p.wait_send()
    send_1.wait_send()

    @pl.when(core == 1)
    def _():
        send_2.wait_send()


def run_sections(x, par, w1, w2, micros, rows, real):
    images = real // PATCHES
    half = micros // 2
    tall = (PATCHES * (images - 1) + PAD + 7) // 8 * 8
    tall = max(tall, rows)
    hbm = pl.BlockSpec(memory_space=pl.ANY)
    vmem = pl.BlockSpec(memory_space=pltpu.VMEM)
    dma = pltpu.SemaphoreType.DMA
    scratch = [
        pltpu.VMEM((2, D, FF), BF),
        pltpu.VMEM((FF, D), BF),
        pltpu.VMEM((2, 8, FF), F32),
        pltpu.VMEM((micros, rows, D), BF),
        pltpu.VMEM((micros, rows, D), BF),
        pltpu.VMEM((micros, rows, D), BF),
        pltpu.VMEM((micros, rows, D), BF),
        pltpu.VMEM((micros, rows, D), BF),
        pltpu.VMEM((micros, rows, FF), BF),
        pltpu.VMEM((micros * images, PAD, 3 * D), BF),
        pltpu.VMEM((micros * images, PAD, 3 * 512), BF),
        pltpu.VMEM((images, D, 128), BF),
        pltpu.VMEM((images, PAD, D), F32),
        pltpu.VMEM((rows, D), BF),
        pltpu.VMEM((rows, D), BF),
        pltpu.VMEM((rows, D), BF),
        pltpu.VMEM((rows, FF), BF),
        pltpu.VMEM((rows, 3 * D), BF),
        pltpu.VMEM((rows, D), BF),
        pltpu.VMEM((images, PAD, D), BF),
        pltpu.VMEM((images, PAD, 3 * D), F32),
        pltpu.VMEM((tall, D), F32),
        pltpu.VMEM((tall, 3 * D), F32),
        dma((3,)), dma((3,)), dma((3,)), dma(()),
        dma((micros,)), dma((micros,)), dma((half,)), dma((half,)), dma((half,)),
        dma((7,)), dma((2, micros)),
    ]
    out_shape = (
        jax.ShapeDtypeStruct((half, rows, D), BF),
        jax.ShapeDtypeStruct((half, rows, D), BF),
        jax.ShapeDtypeStruct((4, micros * rows, D), BF),
        jax.ShapeDtypeStruct((micros * rows, 3 * FF), BF),
        jax.ShapeDtypeStruct((8, FF), F32),
    )
    flops = 2 * 6 * 3 * D * D * 4 * micros * rows
    return pl.pallas_call(
        functools.partial(sections_kernel, micros, rows, real),
        out_shape=out_shape,
        in_specs=[hbm, vmem, hbm, hbm],
        out_specs=(hbm, hbm, hbm, hbm, vmem),
        scratch_shapes=scratch,
        compiler_params=pltpu.CompilerParams(
            collective_id=0, has_side_effects=True, vmem_limit_bytes=63 * 2**20
        ),
        cost_estimate=pl.CostEstimate(flops=flops, bytes_accessed=60_000_000, transcendentals=0),
        name="sections",
    )(x, par, w1, w2)


LAG_SUM, LAG_Z, LAG_OUT = 1, 4, 7
RING = 4


def weights_kernel(
    inner, left_ref, right_ref, out_ref,
    left, ring, part, sib, from_x, from_z,
    l_sem, r_sem, c_send, c_recv, x_send, x_recv, z_send, z_recv,
):
    dp, pipe = lax.axis_index("dp"), lax.axis_index("pipe")
    y, core = pipe // 2, pipe % 2
    outer, rest = dp // inner, dp % inner
    z, x = outer // 2, outer % 2
    lines = MEMBERS // 2
    per = FF // WIDE
    steps = 3 * per

    def at(zz, xx):
        return ((zz * 2 + xx) * inner + rest, pipe)

    sibling = (dp, 2 * y + 1 - core)
    x_peer = at(z, 1 - x)

    barrier = pltpu.get_barrier_semaphore()
    pl.semaphore_signal(barrier, inc=1, device_id=sibling, device_id_type=MESH)
    pl.semaphore_signal(barrier, inc=1, device_id=x_peer, device_id_type=MESH)
    for i in range(1, lines):
        pl.semaphore_signal(barrier, inc=1, device_id=at((z + i) % lines, x), device_id_type=MESH)

    def load_left(n):
        return pltpu.make_async_copy(left_ref.at[n], left.at[n], l_sem.at[n])

    def load_right(k):
        cols = pl.ds(pl.multiple_of(k * WIDE, 128), WIDE)
        return pltpu.make_async_copy(right_ref.at[:, cols], ring.at[k % RING], r_sem.at[k % RING])

    load_left(0).start()
    load_right(0).start()
    load_left(1).start()
    for k in range(1, RING - 1):
        load_right(k).start()
    load_left(2).start()
    load_left(3).start()
    pl.semaphore_wait(barrier, 1 + lines)

    def owner(k):
        is_attn = k // (2 * per)
        return 1 - is_attn, k - is_attn * 2 * per

    def to_sibling(k, j):
        return pltpu.make_async_remote_copy(
            src_ref=part.at[k], dst_ref=sib.at[j], send_sem=c_send.at[k], recv_sem=c_recv.at[j],
            device_id=sibling, device_id_type=MESH,
        )

    def to_x(k, j):
        return pltpu.make_async_remote_copy(
            src_ref=part.at[k, :, 1 - x], dst_ref=from_x.at[j], send_sem=x_send.at[j], recv_sem=x_recv.at[j],
            device_id=x_peer, device_id_type=MESH,
        )

    def to_z(k, j, zz):
        return pltpu.make_async_remote_copy(
            src_ref=part.at[k, zz, x], dst_ref=from_z.at[j, z], send_sem=z_send.at[j, zz],
            recv_sem=z_recv.at[j, z], device_id=at(zz, x), device_id_type=MESH,
        )

    def arrived_z(k, j, zz):
        return pltpu.make_async_remote_copy(
            src_ref=part.at[k, zz, x], dst_ref=from_z.at[j, zz], send_sem=z_send.at[j, zz],
            recv_sem=z_recv.at[j, zz], device_id=at(zz, x), device_id_type=MESH,
        )

    load_left(0).wait()

    def step(s, carry):
        @pl.when(s < steps)
        def _():
            k = s
            for n in range(1, 4):
                edge = (per, 2 * per, 3 * per - D // WIDE)[n - 1]

                @pl.when(k == edge)
                def _():
                    load_left(n).wait()

            load_right(k).wait()

            @pl.when(k + RING - 1 < steps)
            def _():
                load_right(k + RING - 1).start()

            which = k // per + k // (3 * per - D // WIDE)
            product = dot(left[which], ring[k % RING], 0, 0)
            part[k] = product.astype(BF).reshape(lines, 2, BLOCK, WIDE)
            own, j = owner(k)

            @pl.when(own != core)
            def _():
                to_sibling(k, j).start()

        k1 = s - LAG_SUM

        @pl.when((k1 >= 0) & (k1 < steps))
        def _():
            own, j = owner(k1)

            @pl.when(own == core)
            def _():
                to_sibling(k1, j).wait_recv()
                part[k1] = (part[k1].astype(F32) + sib[j].astype(F32)).astype(BF)
                to_x(k1, j).start()

        k2 = s - LAG_Z

        @pl.when((k2 >= 0) & (k2 < steps))
        def _():
            own, j = owner(k2)

            @pl.when(own == core)
            def _():
                to_x(k2, j).wait_recv()
                part[k2, :, x] = (part[k2, :, x].astype(F32) + from_x[j].astype(F32)).astype(BF)
                for i in range(1, lines):
                    to_z(k2, j, (z + i) % lines).start()

        k3 = s - LAG_OUT

        @pl.when((k3 >= 0) & (k3 < steps))
        def _():
            own, j = owner(k3)

            @pl.when(own == core)
            def _():
                total = part[k3, z, x].astype(F32)
                for i in range(1, lines):
                    zz = (z + i) % lines
                    arrived_z(k3, j, zz).wait_recv()
                    total += from_z[j, zz].astype(F32)
                out_ref[j // per, :, pl.ds(pl.multiple_of((j % per) * WIDE, 128), WIDE)] = total

        return carry

    lax.fori_loop(0, steps + LAG_OUT, step, 0)

    def drain(k, carry):
        own, j = owner(k)

        @pl.when(own != core)
        def _():
            to_sibling(k, j).wait_send()

        @pl.when(own == core)
        def _():
            to_x(k, j).wait_send()
            for i in range(1, lines):
                to_z(k, j, (z + i) % lines).wait_send()

        return carry

    lax.fori_loop(0, steps, drain, 0)


def reduce_weights(left, right, inner):
    count = left.shape[1]
    lines = MEMBERS // 2
    per = FF // WIDE
    hbm = pl.BlockSpec(memory_space=pl.ANY)
    vmem = pl.BlockSpec(memory_space=pltpu.VMEM)
    dma = pltpu.SemaphoreType.DMA
    return pl.pallas_call(
        functools.partial(weights_kernel, inner),
        out_shape=jax.ShapeDtypeStruct((2, BLOCK, FF), F32),
        in_specs=[hbm, hbm],
        out_specs=vmem,
        scratch_shapes=[
            pltpu.VMEM((4, count, D), BF),
            pltpu.VMEM((RING, count, WIDE), BF),
            pltpu.VMEM((3 * per, lines, 2, BLOCK, WIDE), BF),
            pltpu.VMEM((2 * per, lines, 2, BLOCK, WIDE), BF),
            pltpu.VMEM((2 * per, lines, BLOCK, WIDE), BF),
            pltpu.VMEM((2 * per, lines, BLOCK, WIDE), BF),
            dma((4,)), dma((RING,)), dma((3 * per,)), dma((2 * per,)), dma((2 * per,)), dma((2 * per,)),
            dma((2 * per, lines)), dma((2 * per, lines)),
        ],
        compiler_params=pltpu.CompilerParams(
            collective_id=1, has_side_effects=True, vmem_limit_bytes=63 * 2**20
        ),
        cost_estimate=pl.CostEstimate(
            flops=2 * 3 * D * FF * count, bytes_accessed=40_000_000, transcendentals=0
        ),
        name="weights",
    )(left, right)


def on_device(tokens, cotangent, norm_gain, norm_shift, w_first, b_first, w_second, b_second):
    pipe = lax.axis_index("pipe")
    dp = lax.axis_index("dp")
    groups = lax.axis_size("dp")
    y, core = pipe // 2, pipe % 2
    inner = groups // MEMBERS
    share = tokens.shape[0] // 4
    micros = MICROS
    real = 2 * share // micros
    rows = (real + 15) // 16 * 16

    def own_rows(whole):
        parts = whole.reshape(2, 2, share, D)
        picked = lax.dynamic_index_in_dim(parts, core, 1, keepdims=False)
        return picked[::-1].reshape(micros, real, D)

    x = jnp.where(y == 0, own_rows(tokens), own_rows(cotangent))
    x = jnp.pad(x, ((0, 0), (0, rows - real), (0, 0)))
    line = jnp.concatenate([norm_gain, norm_shift, b_second, jnp.zeros((1, FF - 3 * D), F32)], 1)
    par = jnp.concatenate([b_first, line, jnp.zeros((6, FF), F32)], 0)
    lo, ig, left, right, small = run_sections(x, par, w_first[0], w_second[0], micros, rows, real)
    layer_out = lo[:, :real].reshape(share, D)
    input_grad = ig[:, :real].reshape(share, D)
    grads = reduce_weights(left, right, inner)

    pairs = small[:4].reshape(2, 2, FF)
    mine = lax.dynamic_index_in_dim(pairs, core, 0, keepdims=False)
    other = lax.dynamic_index_in_dim(pairs, 1 - core, 0, keepdims=False)
    swap = [(i, i + 1 - 2 * (i % 2)) for i in range(4)]
    mine = mine + lax.ppermute(other, "pipe", swap)
    mine = lax.psum(mine, "dp")

    def piece(vec):
        size = vec.shape[0] // groups
        return lax.dynamic_slice_in_dim(vec, dp * size, size, 0)[None]

    if inner > 1:
        members = [[o * inner + i for i in range(inner)] for o in range(MEMBERS)]
        grads = lax.psum_scatter(
            grads, "dp", scatter_dimension=1, axis_index_groups=members, tiled=True
        )
    g_first = grads[0][None]
    g_second = jnp.where(core == 1, grads[1], 0.0).T[None]
    return (
        layer_out,
        input_grad,
        piece(mine[1, :D]),
        piece(mine[1, D : 2 * D]),
        g_first,
        piece(mine[0]),
        g_second,
        piece(mine[1, 2 * D : 3 * D]),
    )


def solution(mesh):
    in_specs = (
        P("dp", None), P("dp", None), P("pipe", None), P("pipe", None),
        P("pipe", None, None), P("pipe", None), P("pipe", None, None), P("pipe", None),
    )
    out_specs = (
        P(("dp", "pipe"), None), P(("dp", "pipe"), None), P("pipe", "dp"), P("pipe", "dp"),
        P("pipe", "dp", None), P("pipe", "dp"), P("pipe", None, "dp"), P("pipe", "dp"),
    )
    return jax.shard_map(
        on_device, mesh=mesh, in_specs=in_specs, out_specs=out_specs, check_vma=False
    )
```

time: 2410 us -> 345 us (0.14)
  the two profiles are of different devices: /device:TPU:1 before, /device:TPU:0 now
where the time goes in v1:
time: 345 us
  Pallas kernels  281 us (81%)
  blocking collectives  35 us (10%)
  local copies, waits for them, and re-layouts  19.7 us (6%)
  other arithmetic  4.49 us (1%)
  starting transfers between devices  3.85 us (1%)
    pallas_call x1, Pallas kernels, run_sections(): pl.pallas_call(functools.partial(sections_kernel, micros, rows, real), ou...  182 us
    pallas_call x1, Pallas kernels, reduce_weights(): pl.pallas_call(functools.partial(weights_kernel, inner), out_shape=jax.Sh...  98.4 us
    psum x1, blocking collectives, on_device(): mine = lax.psum(mine, 'dp')  35 us
    reshape x2, local copies, waits for them, and re-layouts, own_rows(): parts = whole.reshape(2, 2, share, D)  7.3 us
  transfers between devices with their start and end apart: 1, of which 0 were waited for; matrix products, arithmetic and copies ran while one was open for 2% of the time, Pallas kernels for 29%

profile of v1, /device:TPU:0, one launch (start us, length us, event | category | flops | bytes accessed | tf_op | source)
XLA Modules:
  0.0 344.6 jit_solution(8147774537161005955)
XLA Ops:
  0.7 3.7 %reshape.46 = bf16[2,2,588,768]{3,2,1,0:T(8,128)(2,1)} reshape(bf16[2352,768]{1,0:T(8,128)(2,1)} %param.8) | data formatting | bytes 7225344 | tf_op jit(solution)/shard_map/reshape | solution.py:746
  4.3 3.6 %reshape.47 = bf16[2,2,588,768]{3,2,1,0:T(8,128)(2,1)} reshape(bf16[2352,768]{1,0:T(8,128)(2,1)} %param.9) | data formatting | bytes 7225344 | tf_op jit(solution)/shard_map/reshape | solution.py:746
  8.0 2.3 dynamic-slice_bitcast_fusion
  10.2 0.4 reverse_select_fusion
  10.7 1.4 select_n.56
  12.1 0.1 pad.10.clone
  12.2 0.0 copy-start.2
  12.2 0.0 copy-start.3
  12.2 2.9 pad.4.x_ref
  15.1 0.0 copy-done.2
  15.1 0.0 copy-done.3
  15.1 0.0 copy-done.4
  15.1 0.0 copy-done.5
  15.1 0.7 maximum_maximum_fusion.par_ref
  15.8 182.4 %sections.1 = (bf16[2,304,768]{2,1,0:T(8,128)(2,1)}, bf16[2,304,768]{2,1,0:T(8,128)(2,1)}, bf16[4,1216,768]{2,1,0:T(8,128)(2,1)}, bf16[1216,9216]{1,0:T(8,128)(2,1)}, f32[8,3072]{1,0:T(8,128)}) custom-call(bf16[4,304,768]{2,1,0:T(8,128)(2,1)} %pad.4.x_ref, f32[8,3072]{1,0:T(8,128)} %maximum_maximum_fusion.par_ref, bf16[768,3072]{1,0:T(8,128)(2,1)} %bitcast.16, ...), custom_call_target="tpu_custom_call" | custom-call | flops 103280541696 | bytes 60000000 | tf_op jit(solution)/shard_map/sections/pallas_call | solution.py:525
  198.3 0.9 slice.29
  199.2 3.9 %collective-permute-start = (f32[2,3072]{1,0:T(2,128)S(1)}, f32[2,3072]{1,0:T(2,128)S(1)}, u32[]{:S(2)}, u32[]{:S(2)}) collective-permute-start(f32[2,3072]{1,0:T(2,128)S(1)} %dynamic-slice_bitcast_fusion.2), channel_id=1, source_target_pairs={{0,1},{1,0},{2,3},{3,2},{4,5},{5,4},{6,7},{7,6},{8,9},{9,8},{10,11... | collective-permute-start | bytes 73736 | tf_op jit(solution)/shard_map/ppermute | solution.py:763
  203.1 98.4 %weights.1 = f32[2,96,3072]{2,1,0:T(8,128)} custom-call(bf16[4,1216,768]{2,1,0:T(8,128)(2,1)} %get-tuple-element.16.left_ref, bf16[1216,9216]{1,0:T(8,128)(2,1)} %get-tuple-element.17.right_ref), custom_call_target="tpu_custom_call" | custom-call | flops 17213423616 | bytes 40000000 | tf_op jit(solution)/shard_map/weights/pallas_call | solution.py:709
  301.5 0.0 copy-start.1
  301.5 3.3 select_bitcast_fusion
  304.8 0.0 copy-done.1
  304.8 0.1 slice.27
  304.9 1.1 reshape.48
  306.0 0.1 copy-done
  306.1 0.1 slice.28
  306.1 1.1 reshape.49
  307.2 0.0 collective-permute-done
  307.2 35.0 %psum.7 = f32[2,3072]{1,0:T(2,128)S(1)} all-reduce(f32[2,3072]{1,0:T(2,128)S(1)} %bitcast_add_fusion), channel_id=1, replica_groups=mesh['dp'=8,'pipe'=4] {'dp'}, use_global_device_ids=true, to_apply=%region_0.1 | all-reduce | flops 6144 | bytes 49152 | tf_op jit(solution)/shard_map/psum | solution.py:764
  342.3 0.6 constant_dynamic-slice_fusion
  342.9 0.6 constant_dynamic-slice_fusion.2
  343.5 0.6 constant_dynamic-slice_fusion.3
  344.0 0.6 constant_dynamic-slice_fusion.1
  (10 shorter events, 0.1 us)
Async XLA Ops:
  12.2 2.9 copy-start.2
  12.2 2.9 copy-start.3
  12.2 2.9 copy-start.4
  12.2 2.9 copy-start.5
  199.2 108.0 %collective-permute-start = (f32[2,3072]{1,0:T(2,128)S(1)}, f32[2,3072]{1,0:T(2,128)S(1)}, u32[]{:S(2)}, u32[]{:S(2)}) collective-permute-start(f32[2,3072]{1,0:T(2,128)S(1)} %dynamic-slice_bitcast_fusion.2), channel_id=1, source_target_pairs={{0,1},{1,0},{2,3},{3,2},{4,5},{5,4},{6,7},{7,6},{8,9},{9,8},{10,11... | collective-permute-start | bytes 73736 | tf_op jit(solution)/shard_map/ppermute | solution.py:763
  301.5 3.4 copy-start.1
  304.8 1.2 copy-start

commit v2 on v1

v2 whole, which is shorter than its diff:
```python
import functools

import jax
import jax.experimental.pallas as pl
import jax.experimental.pallas.tpu as pltpu
import jax.numpy as jnp
from jax import lax
from jax.sharding import PartitionSpec as P

D = 768
FF = 3072
PATCHES = 49
PAD = 64
EPS = 1e-05
SCALE = 32 ** (-0.5)
MICROS = 8
MEMBERS = 8
BLOCK = D // MEMBERS
WIDE = 384
MESH = pl.DeviceIdType.MESH
BF = jnp.bfloat16
F32 = jnp.float32


def dot(a, b, ca, cb):
    return lax.dot_general(a, b, (((ca,), (cb,)), ((), ())), preferred_element_type=F32)


def gelu_pair(h):
    t = 1.0 / (1.0 + 0.3275911 * 0.7071067811865476 * jnp.abs(h))
    poly = t * (0.127414796 + t * (-0.142248368 + t * (0.7107068705 + t * (-0.7265760135 + t * 0.5307027145))))
    bell = jnp.exp(-0.5 * h * h)
    tail = poly * bell
    cdf = jnp.where(h >= 0, 1.0 - tail, tail)
    return h * cdf, cdf + h * (0.3989422804014327 * bell)


def norm_parts(x):
    center = x - jnp.mean(x, -1, keepdims=True)
    inverse = lax.rsqrt(jnp.mean(center * center, -1, keepdims=True) + EPS)
    return center * inverse, inverse


def head_masks(width):
    lane = lax.broadcasted_iota(jnp.int32, (1, width), 1) // 32
    return [lane == h for h in range(width // 32)]


def spread(block, masks):
    return jnp.concatenate([jnp.where(m, block, jnp.zeros_like(block)) for m in masks], 0)


def gather_heads(stacked, masks):
    total = None
    for h, m in enumerate(masks):
        part = jnp.where(m, stacked[PAD * h : PAD * (h + 1)], 0.0)
        total = part if total is None else total + part
    return total


def window_forward(q, k, v):
    eight, four = head_masks(256), head_masks(128)
    row = lax.broadcasted_iota(jnp.int32, (PAD, 1), 0)
    scores = [
        dot(k[:, s : s + 256], spread(q[:, s : s + 256], eight), 1, 1) for s in range(0, D, 256)
    ]
    probs = []
    for block in scores:
        block = jnp.where(row < PATCHES, block, -1e30)
        e = jnp.exp((block - jnp.max(block, 0, keepdims=True)) * SCALE)
        probs.append((e * (1.0 / jnp.sum(e, 0, keepdims=True))).astype(BF))
    parts = []
    for n in range(D // 128):
        cols = slice(256 * (n % 2), 256 * (n % 2) + 256)
        parts.append(dot(probs[n // 2][:, cols], v[:, 128 * n : 128 * n + 128], 0, 0))
    parts = [gather_heads(part, four) for part in parts]
    return jnp.concatenate(probs, 1), jnp.concatenate(parts, 1)


def window_backward(q, k, v, probs, d_att):
    eight, four = head_masks(256), head_masks(128)
    starts = range(0, D, 256)
    wide = [spread(d_att[:, s : s + 256], eight) for s in starts]
    d_probs = [dot(v[:, s : s + 256], wide[n], 1, 1) for n, s in enumerate(starts)]
    d_v = [dot(probs[:, 2 * s : 2 * s + 512], wide[n], 1, 0) for n, s in enumerate(starts)]
    d_scores = []
    for n, s in enumerate(starts):
        p = probs[:, 2 * s : 2 * s + 512].astype(F32)
        product = p * d_probs[n]
        d_scores.append((product - p * jnp.sum(product, 0, keepdims=True)).astype(BF))
    d_k = [
        dot(d_scores[n], spread(q[:, s : s + 256], eight), 1, 0) * SCALE for n, s in enumerate(starts)
    ]
    d_q = []
    for n in range(D // 128):
        cols = slice(256 * (n % 2), 256 * (n % 2) + 256)
        d_q.append(dot(d_scores[n // 2][:, cols], k[:, 128 * n : 128 * n + 128], 0, 0))
    d_q = [gather_heads(part, four) * SCALE for part in d_q]
    return jnp.concatenate(d_q, 1), jnp.concatenate(d_k, 1), jnp.concatenate(d_v, 1)


def compress(block, masks):
    total = None
    for h, m in enumerate(masks):
        part = jnp.where(m, block[32 * h : 32 * h + 32], 0.0)
        total = part if total is None else total + part
    return total


def diagonal(block, masks):
    return jnp.concatenate([jnp.where(m, block, jnp.zeros_like(block)) for m in masks], 0)


def channel_forward(q, k, v):
    four = head_masks(128)
    starts = range(0, D, 128)
    scores = [dot(k[:, s : s + 128], q[:, s : s + 128], 0, 0) for s in starts]
    scores = jnp.concatenate([compress(block, four) for block in scores], 1)
    e = jnp.exp((scores - jnp.max(scores, 0, keepdims=True)) * SCALE)
    probs = (e * (1.0 / jnp.sum(e, 0, keepdims=True))).astype(BF)
    parts = [dot(v[:, s : s + 128], diagonal(probs[:, s : s + 128], four), 1, 0) for s in starts]
    return probs, jnp.concatenate(parts, 1)


def channel_backward(q, k, v, probs, d_att):
    four = head_masks(128)
    starts = range(0, D, 128)
    d_probs = [dot(v[:, s : s + 128], d_att[:, s : s + 128], 0, 0) for s in starts]
    d_v = [dot(d_att[:, s : s + 128], diagonal(probs[:, s : s + 128], four), 1, 1) for s in starts]
    d_probs = jnp.concatenate([compress(block, four) for block in d_probs], 1)
    p = probs.astype(F32)
    product = p * d_probs
    d_scores = (product - p * jnp.sum(product, 0, keepdims=True)).astype(BF)
    blocks = [diagonal(d_scores[:, s : s + 128], four) for s in starts]
    d_q = [dot(k[:, s : s + 128], blocks[n], 1, 0) * SCALE for n, s in enumerate(starts)]
    d_k = [dot(q[:, s : s + 128], blocks[n], 1, 1) * SCALE for n, s in enumerate(starts)]
    return jnp.concatenate(d_q, 1), jnp.concatenate(d_k, 1), jnp.concatenate(d_v, 1)


def sections_kernel(
    micros, rows, real,
    tok_ref, cot_ref, par, w1_ref, w2_ref,
    lo_ref, ig_ref, left_ref, right_ref, small_ref,
    w1, w2, big, probs, x_in, g_in, v_out, g_out, raw, normed, att_low, wide, acc, tmp, att_in, d_att, d_split,
    w_sem, raw_sem, v_send, v_recv, g_send, g_recv, f_send, f_recv, k_sem, kg_sem, kh_sem,
):
    dp, role = lax.axis_index("dp"), lax.axis_index("pipe")
    images = real // PATCHES
    share = micros // 4
    slab = raw.shape[1]
    total = tok_ref.shape[0]

    barrier = pltpu.get_barrier_semaphore()
    for n in range(1, 4):
        pl.semaphore_signal(barrier, inc=1, device_id=(dp, (role + n) % 4), device_id_type=MESH)

    load_1 = pltpu.make_async_copy(w1_ref, w1, w_sem.at[0])
    load_2 = pltpu.make_async_copy(w2_ref, w2, w_sem.at[1])
    load_1.start()

    def owner(m):
        return (m // share + 2) % 4

    def first_row(m):
        return owner(m) * (share * real) + (m % share) * real

    def slab_start(m):
        return pl.multiple_of(jnp.minimum(first_row(m) // 16 * 16, total - slab), 16)

    def load_slab(ref, m):
        return pltpu.make_async_copy(ref.at[pl.ds(slab_start(m), slab)], raw.at[m % 2], raw_sem.at[m % 2])

    def take_slab(ref, m, dst):
        load_slab(ref, m).wait()
        shift = first_row(m) - slab_start(m)
        moved = pltpu.roll(raw[m % 2].astype(F32), slab - shift, 0)[:rows]
        row = lax.broadcasted_iota(jnp.int32, (rows, 1), 0)
        dst[m] = jnp.where(row < real, moved, 0.0).astype(BF)

        @pl.when(m + 2 < micros)
        def _():
            load_slab(ref, m + 2).start()

    small_ref[...] = jnp.zeros_like(small_ref)

    def out_rows(m):
        return pl.ds(pl.multiple_of(m * rows, 16), rows)

    def keep_left(n, m, src):
        return pltpu.make_async_copy(src, left_ref.at[n, out_rows(m)], k_sem.at[n])

    def keep_wide(m, start, size):
        return pltpu.make_async_copy(
            wide.at[:, pl.ds(0, size)], right_ref.at[out_rows(m), pl.ds(start, size)], k_sem.at[2]
        )

    def again(m, copy):
        @pl.when(m > 0)
        def _():
            copy.wait()

    def keep_gout_left(m):
        return pltpu.make_async_copy(g_in.at[m], left_ref.at[1, out_rows(m)], kg_sem.at[m])

    def keep_gout_right(m):
        return pltpu.make_async_copy(g_in.at[m], right_ref.at[out_rows(m), pl.ds(3 * D, D)], kg_sem.at[m])

    def keep_hidden(m):
        return pltpu.make_async_copy(
            big.at[m, pl.ds(0, rows)], right_ref.at[out_rows(m), pl.ds(0, FF)], kh_sem.at[m]
        )

    def next_hop(m):
        return pltpu.make_async_remote_copy(
            src_ref=v_out.at[m % 2], dst_ref=x_in.at[m], send_sem=v_send.at[m], recv_sem=v_recv.at[m],
            device_id=(dp, (role + 1) % 4), device_id_type=MESH,
        )

    def back_hop(m):
        return pltpu.make_async_remote_copy(
            src_ref=g_out.at[m % 2], dst_ref=g_in.at[m], send_sem=g_send.at[m], recv_sem=g_recv.at[m],
            device_id=(dp, (role + 3) % 4), device_id_type=MESH,
        )

    def result_hop(n, src, ref, m):
        return pltpu.make_async_remote_copy(
            src_ref=src.at[m % 2], dst_ref=ref.at[m % share], send_sem=f_send.at[m],
            recv_sem=f_recv.at[n, m % share], device_id=(dp, owner(m)), device_id_type=MESH,
        )

    def result_here(src, ref, m):
        return pltpu.make_async_copy(src.at[m % 2], ref.at[m % share], f_send.at[m])

    def result_start(n, src, ref, m):
        @pl.when(owner(m) == role)
        def _():
            result_here(src, ref, m).start()

        @pl.when(owner(m) != role)
        def _():
            result_hop(n, src, ref, m).start()

    def result_wait(n, src, ref, m):
        @pl.when(owner(m) == role)
        def _():
            result_here(src, ref, m).wait()

        @pl.when(owner(m) != role)
        def _():
            result_hop(n, src, ref, m).wait_send()

    bias = par[0:1, :]
    gain, shift_row, bias_out = par[1:2, :D], par[1:2, D : 2 * D], par[1:2, 2 * D : 3 * D]
    image_row = lax.broadcasted_iota(jnp.int32, (PAD, 1), 0)

    def norm_forward(m, x):
        scaled, _ = norm_parts(x)
        again(m, keep_left(0, m, normed))
        normed[...] = (scaled * gain + shift_row).astype(BF)
        keep_left(0, m, normed).start()

    def norm_back(d_normed, m):
        scaled, inverse = norm_parts(x_in[m].astype(F32))
        small_ref[0:1, :] += jnp.sum(d_normed * scaled, 0, keepdims=True)
        small_ref[1:2, :] += jnp.sum(d_normed, 0, keepdims=True)
        d_scaled = d_normed * gain
        mean = jnp.mean(d_scaled, -1, keepdims=True)
        cross = jnp.mean(d_scaled * scaled, -1, keepdims=True)
        return (g_in[m].astype(F32) + inverse * (d_scaled - mean - scaled * cross)).astype(BF)

    def cut(src, n, c):
        part = src[PATCHES * n : PATCHES * n + PAD, c : c + D]
        return jnp.where(image_row < PATCHES, part, 0.0).astype(BF)

    def image_at(i):
        return pl.ds(pl.multiple_of(i * PAD, PAD), PAD)

    def attention_forward(m, spatial):
        x = x_in[m].astype(F32)
        norm_forward(m, x)
        for c in range(0, 3 * D, D):
            tmp[0:rows, c : c + D] = dot(normed[...], w1[:, c : c + D], 1, 0) + bias[:, c : c + D]
        for i in range(images):
            for c in range(0, 3 * D, D):
                big[m, PAD * i : PAD * (i + 1), c : c + D] = cut(tmp, i, c)

        def one_image(i, carry):
            q, k, v = (big[m, image_at(i), n * D : (n + 1) * D] for n in range(3))
            if spatial:
                probs[m * images + i], att_in[i] = window_forward(q, k, v)
            else:
                probs[m * images + i, 0:32, 0:D], att_in[i] = channel_forward(q, k, v)
            return carry

        lax.fori_loop(0, images, one_image, 0)
        for i in range(images):
            acc[PATCHES * i : PATCHES * i + PAD, :] = att_in[i]
        acc[real:rows, :] = jnp.zeros((rows - real, D), F32)
        again(m, keep_left(1, m, att_low))
        att_low[...] = acc[0:rows, :].astype(BF)
        keep_left(1, m, att_low).start()
        branch = dot(att_low[...], w1[:, 3 * D :], 1, 0) + bias[:, 3 * D :]
        v_out[m % 2] = (x + branch).astype(BF)

    def attention_backward(m, spatial):
        keep_gout_right(m).start()
        g = g_in[m]
        small_ref[6:7, :] += jnp.sum(g.astype(F32), 0, keepdims=True)
        acc[0:rows, :] = dot(g, w1[:, 3 * D :], 1, 1)
        for i in range(images):
            d_att[i] = cut(acc, i, 0)

        def one_image(i, carry):
            q, k, v = (big[m, image_at(i), n * D : (n + 1) * D] for n in range(3))
            if spatial:
                grads = window_backward(q, k, v, probs[m * images + i], d_att[i])
            else:
                grads = channel_backward(q, k, v, probs[m * images + i, 0:32, 0:D], d_att[i])
            for n in range(3):
                d_split[i, :, n * D : (n + 1) * D] = grads[n].astype(BF)
            return carry

        lax.fori_loop(0, images, one_image, 0)
        for i in range(images):
            for c in range(0, 3 * D, D):
                tmp[PATCHES * i : PATCHES * i + PAD, c : c + D] = d_split[i, :, c : c + D].astype(F32)
        tmp[real:rows, :] = jnp.zeros((rows - real, 3 * D), F32)
        again(m, keep_wide(m, 0, 3 * D))
        for n in range(3):
            part = tmp[0:rows, n * D : (n + 1) * D]
            wide[:, n * D : (n + 1) * D] = part.astype(BF)
            small_ref[3 + n : 4 + n, :] += jnp.sum(part, 0, keepdims=True)
        keep_wide(m, 0, 3 * D).start()
        g_out[m % 2] = norm_back(dot(wide[:, : 3 * D], w1[:, : 3 * D], 1, 1), m)

    def feed_forward(m):
        x = x_in[m].astype(F32)
        norm_forward(m, x)
        again(m, keep_wide(m, FF, FF))
        acc[0:rows, :] = x + bias_out
        for c in range(0, FF, D):
            hidden = dot(normed[...], w1[:, c : c + D], 1, 0) + bias[:, c : c + D]
            value, diff = gelu_pair(hidden)
            wide[:, c : c + D] = value.astype(BF)
            big[m, 0:rows, c : c + D] = diff.astype(BF)
            acc[0:rows, :] += dot(wide[:, c : c + D], w2[c : c + D, :], 1, 0)
        keep_wide(m, FF, FF).start()
        v_out[m % 2] = acc[0:rows, :].astype(BF)

    def feed_backward(m):
        keep_gout_left(m).start()
        small_ref[2:3, :] += jnp.sum(g_in[m].astype(F32), 0, keepdims=True)
        for n in range(FF // D):
            c = n * D
            d_act = dot(g_in[m], w2[c : c + D, :], 1, 1)
            d_hid = (d_act * big[m, 0:rows, c : c + D].astype(F32)).astype(BF)
            big[m, 0:rows, c : c + D] = d_hid
            small_ref[3 + n : 4 + n, :] += jnp.sum(d_hid.astype(F32), 0, keepdims=True)
            back = dot(d_hid, w1[:, c : c + D], 1, 1)
            if n == 0:
                acc[0:rows, :] = back
            else:
                acc[0:rows, :] += back
        keep_hidden(m).start()
        g_out[m % 2] = norm_back(acc[0:rows, :], m)

    def forward(m, run, first, last):
        if first:
            take_slab(tok_ref, m, x_in)
        else:
            next_hop(m).wait_recv()

        @pl.when(m >= 2)
        def _():
            finish_forward(m - 2, last)

        run(m)
        if last is True:
            result_start(0, v_out, lo_ref, m)
        elif last is False:
            next_hop(m).start()
        else:

            @pl.when(last)
            def _():
                result_start(0, v_out, lo_ref, m)

            @pl.when(jnp.logical_not(last))
            def _():
                next_hop(m).start()

    def finish_forward(m, last):
        if last is False:
            next_hop(m).wait_send()
        else:

            @pl.when(last)
            def _():
                result_wait(0, v_out, lo_ref, m)

            @pl.when(jnp.logical_not(last))
            def _():
                next_hop(m).wait_send()

    def backward(m, run, first, last):
        if last is False:
            back_hop(m).wait_recv()
        else:

            @pl.when(last)
            def _():
                take_slab(cot_ref, m, g_in)

            @pl.when(jnp.logical_not(last))
            def _():
                back_hop(m).wait_recv()

        @pl.when(m >= 2)
        def _():
            finish_backward(m - 2, first)

        run(m)
        if first:
            result_start(1, g_out, ig_ref, m)
        else:
            back_hop(m).start()

    def finish_backward(m, first):
        if first:
            result_wait(1, g_out, ig_ref, m)
        else:
            back_hop(m).wait_send()

    def pipeline(run_forward, run_backward, lag, first, last):
        def step(s, carry):
            @pl.when(s < micros)
            def _():
                forward(s, run_forward, first, last)

            @pl.when(s >= lag)
            def _():
                backward(s - lag, run_backward, first, last)

            return carry

        lax.fori_loop(0, micros + lag, step, 0)
        for m in (micros - 2, micros - 1):
            finish_forward(m, last)
            finish_backward(m, first)

    @pl.when(role == 0)
    def _():
        load_slab(tok_ref, 0).start()
        load_slab(tok_ref, 1).start()

    @pl.when(role == 3)
    def _():
        load_slab(cot_ref, 0).start()
        load_slab(cot_ref, 1).start()

    @pl.when(role % 2 == 1)
    def _():
        load_2.start()

    load_1.wait()
    pl.semaphore_wait(barrier, 3)

    @pl.when(role == 0)
    def _():
        tmp[rows:, :] = jnp.zeros((tmp.shape[0] - rows, 3 * D), F32)
        acc[rows:, :] = jnp.zeros((acc.shape[0] - rows, D), F32)
        pipeline(
            functools.partial(attention_forward, spatial=True),
            functools.partial(attention_backward, spatial=True),
            micros, True, False,
        )

    @pl.when(role == 2)
    def _():
        tmp[rows:, :] = jnp.zeros((tmp.shape[0] - rows, 3 * D), F32)
        acc[rows:, :] = jnp.zeros((acc.shape[0] - rows, D), F32)
        pipeline(
            functools.partial(attention_forward, spatial=False),
            functools.partial(attention_backward, spatial=False),
            2, False, False,
        )

    @pl.when(role % 2 == 0)
    def _():
        keep_left(1, micros - 1, att_low).wait()
        keep_wide(micros - 1, 0, 3 * D).wait()

        def kept(m, carry):
            keep_gout_right(m).wait()
            return carry

        lax.fori_loop(0, micros, kept, 0)

    @pl.when(role % 2 == 1)
    def _():
        load_2.wait()
        pipeline(feed_forward, feed_backward, jnp.where(role == 3, 0, micros), False, role == 3)
        keep_wide(micros - 1, FF, FF).wait()

        def kept(m, carry):
            keep_gout_left(m).wait()
            keep_hidden(m).wait()
            return carry

        lax.fori_loop(0, micros, kept, 0)

    keep_left(0, micros - 1, normed).wait()

    def arrived(n, carry):
        @pl.when(role != 3)
        def _():
            result_hop(0, v_out, lo_ref, n).wait_recv()

        @pl.when(role != 0)
        def _():
            result_hop(1, g_out, ig_ref, n).wait_recv()

        return carry

    lax.fori_loop(0, share, arrived, 0)


def run_sections(tokens, cotangent, par, w1, w2, micros, rows, real):
    images = real // PATCHES
    tall = max((PATCHES * (images - 1) + PAD + 7) // 8 * 8, rows)
    share = micros // 4
    slab = min(rows + 16, tokens.shape[0])
    hbm = pl.BlockSpec(memory_space=pl.ANY)
    vmem = pl.BlockSpec(memory_space=pltpu.VMEM)
    dma = pltpu.SemaphoreType.DMA
    scratch = [
        pltpu.VMEM((D, FF), BF),
        pltpu.VMEM((FF, D), BF),
        pltpu.VMEM((micros, max(images * PAD, rows), FF), BF),
        pltpu.VMEM((micros * images, PAD, 3 * 512), BF),
        pltpu.VMEM((micros, rows, D), BF),
        pltpu.VMEM((micros, rows, D), BF),
        pltpu.VMEM((2, rows, D), BF),
        pltpu.VMEM((2, rows, D), BF),
        pltpu.VMEM((2, slab, D), BF),
        pltpu.VMEM((rows, D), BF),
        pltpu.VMEM((rows, D), BF),
        pltpu.VMEM((rows, FF), BF),
        pltpu.VMEM((tall, D), F32),
        pltpu.VMEM((tall, 3 * D), F32),
        pltpu.VMEM((images, PAD, D), F32),
        pltpu.VMEM((images, PAD, D), BF),
        pltpu.VMEM((images, PAD, 3 * D), BF),
        dma((2,)), dma((2,)), dma((micros,)), dma((micros,)), dma((micros,)), dma((micros,)),
        dma((micros,)), dma((2, share)), dma((3,)), dma((micros,)), dma((micros,)),
    ]
    out_shape = (
        jax.ShapeDtypeStruct((share, rows, D), BF),
        jax.ShapeDtypeStruct((share, rows, D), BF),
        jax.ShapeDtypeStruct((2, micros * rows, D), BF),
        jax.ShapeDtypeStruct((micros * rows, 2 * FF), BF),
        jax.ShapeDtypeStruct((8, D), F32),
    )
    return pl.pallas_call(
        functools.partial(sections_kernel, micros, rows, real),
        out_shape=out_shape,
        in_specs=[hbm, hbm, vmem, hbm, hbm],
        out_specs=(hbm, hbm, hbm, hbm, vmem),
        scratch_shapes=scratch,
        compiler_params=pltpu.CompilerParams(
            collective_id=0, has_side_effects=True, vmem_limit_bytes=63 * 2**20
        ),
        cost_estimate=pl.CostEstimate(
            flops=2 * 4 * 2 * D * FF * micros * rows, bytes_accessed=60_000_000, transcendentals=0
        ),
        name="sections",
    )(tokens, cotangent, par, w1, w2)


LAG_X, LAG_Z, LAG_OUT = 0, 3, 6
RING = 4


def weights_kernel(
    inner, real,
    left_ref, right_ref, small, lo_ref, ig_ref,
    first_ref, second_ref, vec_ref, lo_out, ig_out,
    left, ring, part, from_x, from_z, vec_x, vec_z, halves, joined,
    l_sem, r_sem, x_send, x_recv, z_send, z_recv, v_send, v_recv, h_sem,
):
    dp, role = lax.axis_index("dp"), lax.axis_index("pipe")
    feed = role % 2
    outer, rest = dp // inner, dp % inner
    z, x = outer // 2, outer % 2
    lines = MEMBERS // 2
    per = FF // WIDE
    steps = per + per * feed

    def at(zz, xx):
        return ((zz * 2 + xx) * inner + rest, role)

    barrier = pltpu.get_barrier_semaphore()
    pl.semaphore_signal(barrier, inc=1, device_id=at(z, 1 - x), device_id_type=MESH)
    for i in range(1, lines):
        pl.semaphore_signal(barrier, inc=1, device_id=at((z + i) % lines, x), device_id_type=MESH)

    def load_left(n):
        return pltpu.make_async_copy(left_ref.at[n], left.at[n], l_sem.at[n])

    def load_right(k):
        cols = pl.ds(pl.multiple_of(k * WIDE, 128), WIDE)
        return pltpu.make_async_copy(right_ref.at[:, cols], ring.at[k % RING], r_sem.at[k % RING])

    load_left(0).start()
    load_right(0).start()
    for k in range(1, RING - 1):
        load_right(k).start()
    load_left(1).start()
    load_lo = pltpu.make_async_copy(lo_ref, halves.at[0], h_sem.at[0])
    load_ig = pltpu.make_async_copy(ig_ref, halves.at[1], h_sem.at[1])
    load_lo.start()
    load_ig.start()
    pl.semaphore_wait(barrier, lines)

    def to_x(k):
        return pltpu.make_async_remote_copy(
            src_ref=part.at[k, :, 1 - x], dst_ref=from_x.at[k], send_sem=x_send.at[k], recv_sem=x_recv.at[k],
            device_id=at(z, 1 - x), device_id_type=MESH,
        )

    def to_z(k, zz):
        return pltpu.make_async_remote_copy(
            src_ref=part.at[k, zz, x], dst_ref=from_z.at[k, z], send_sem=z_send.at[k, zz],
            recv_sem=z_recv.at[k, z], device_id=at(zz, x), device_id_type=MESH,
        )

    def arrived_z(k, zz):
        return pltpu.make_async_remote_copy(
            src_ref=part.at[k, zz, x], dst_ref=from_z.at[k, zz], send_sem=z_send.at[k, zz],
            recv_sem=z_recv.at[k, zz], device_id=at(zz, x), device_id_type=MESH,
        )

    vec_to_x = pltpu.make_async_remote_copy(
        src_ref=small, dst_ref=vec_x.at[0], send_sem=v_send.at[0], recv_sem=v_recv.at[0],
        device_id=at(z, 1 - x), device_id_type=MESH,
    )

    def vec_to_z(zz):
        return pltpu.make_async_remote_copy(
            src_ref=vec_x.at[1], dst_ref=vec_z.at[z], send_sem=v_send.at[1 + zz], recv_sem=v_recv.at[1 + z],
            device_id=at(zz, x), device_id_type=MESH,
        )

    def vec_arrived(zz):
        return pltpu.make_async_remote_copy(
            src_ref=vec_x.at[1], dst_ref=vec_z.at[zz], send_sem=v_send.at[1 + zz], recv_sem=v_recv.at[1 + zz],
            device_id=at(zz, x), device_id_type=MESH,
        )

    load_left(0).wait()
    edge = jnp.where(feed == 1, per, 3 * D // WIDE)

    def step(s, carry):
        @pl.when(s < steps)
        def _():
            @pl.when(s == edge)
            def _():
                load_left(1).wait()

            load_right(s).wait()

            @pl.when(s + RING - 1 < steps)
            def _():
                load_right(s + RING - 1).start()

            product = dot(left[s // edge], ring[s % RING], 0, 0)
            part[s] = product.astype(BF).reshape(lines, 2, BLOCK, WIDE)
            to_x(s).start()

        k2 = s - LAG_Z

        @pl.when((k2 >= 0) & (k2 < steps))
        def _():
            to_x(k2).wait_recv()
            part[k2, :, x] = (part[k2, :, x].astype(F32) + from_x[k2].astype(F32)).astype(BF)
            for i in range(1, lines):
                to_z(k2, (z + i) % lines).start()

        k3 = s - LAG_OUT

        @pl.when((k3 >= 0) & (k3 < steps))
        def _():
            total = part[k3, z, x].astype(F32)
            for i in range(1, lines):
                zz = (z + i) % lines
                arrived_z(k3, zz).wait_recv()
                total += from_z[k3, zz].astype(F32)
            place = pl.multiple_of((k3 % per) * WIDE, 128)

            @pl.when(k3 < per)
            def _():
                first_ref[:, pl.ds(place, WIDE)] = total

            @pl.when(k3 >= per)
            def _():
                second_ref[pl.ds(place, WIDE), :] = total.T

        @pl.when(s == 0)
        def _():
            vec_to_x.start()

            @pl.when(feed == 0)
            def _():
                second_ref[...] = jnp.zeros_like(second_ref)

        @pl.when(s == 2)
        def _():
            for n, load, dst in ((0, load_lo, lo_out), (1, load_ig, ig_out)):
                load.wait()
                for i in range(halves.shape[1]):
                    joined[real * i : real * (i + 1), :] = halves[n, i, :real].astype(F32)
                dst[...] = joined[: dst.shape[0], :].astype(BF)

        @pl.when(s == 4)
        def _():
            vec_to_x.wait_recv()
            vec_x[1] = small[...] + vec_x[0]
            for i in range(1, lines):
                vec_to_z((z + i) % lines).start()

        return carry

    lax.fori_loop(0, steps + LAG_OUT, step, 0)
    total = vec_x[1]
    for i in range(1, lines):
        zz = (z + i) % lines
        vec_arrived(zz).wait_recv()
        total += vec_z[zz]
        vec_to_z(zz).wait_send()
    vec_ref[...] = total
    vec_to_x.wait_send()

    def drain(k, carry):
        to_x(k).wait_send()
        for i in range(1, lines):
            to_z(k, (z + i) % lines).wait_send()
        return carry

    lax.fori_loop(0, steps, drain, 0)


def reduce_weights(left, right, small, lo, ig, inner, real):
    count = left.shape[1]
    lines = MEMBERS // 2
    per = FF // WIDE
    share = lo.shape[0]
    hbm = pl.BlockSpec(memory_space=pl.ANY)
    vmem = pl.BlockSpec(memory_space=pltpu.VMEM)
    dma = pltpu.SemaphoreType.DMA
    return pl.pallas_call(
        functools.partial(weights_kernel, inner, real),
        out_shape=(
            jax.ShapeDtypeStruct((BLOCK, FF), F32),
            jax.ShapeDtypeStruct((FF, BLOCK), F32),
            jax.ShapeDtypeStruct((8, D), F32),
            jax.ShapeDtypeStruct((share * real, D), BF),
            jax.ShapeDtypeStruct((share * real, D), BF),
        ),
        in_specs=[hbm, hbm, vmem, hbm, hbm],
        out_specs=(vmem, vmem, vmem, vmem, vmem),
        scratch_shapes=[
            pltpu.VMEM((2, count, D), BF),
            pltpu.VMEM((RING, count, WIDE), BF),
            pltpu.VMEM((2 * per, lines, 2, BLOCK, WIDE), BF),
            pltpu.VMEM((2 * per, lines, BLOCK, WIDE), BF),
            pltpu.VMEM((2 * per, lines, BLOCK, WIDE), BF),
            pltpu.VMEM((2, 8, D), F32),
            pltpu.VMEM((lines, 8, D), F32),
            pltpu.VMEM((2,) + lo.shape, BF),
            pltpu.VMEM(((share * real + 7) // 8 * 8, D), F32),
            dma((2,)), dma((RING,)), dma((2 * per,)), dma((2 * per,)),
            dma((2 * per, lines)), dma((2 * per, lines)), dma((1 + lines,)), dma((1 + lines,)), dma((2,)),
        ],
        compiler_params=pltpu.CompilerParams(
            collective_id=1, has_side_effects=True, vmem_limit_bytes=63 * 2**20
        ),
        cost_estimate=pl.CostEstimate(
            flops=2 * 2 * D * FF * count, bytes_accessed=40_000_000, transcendentals=0
        ),
        name="weights",
    )(left, right, small, lo, ig)


def on_device(tokens, cotangent, norm_gain, norm_shift, w_first, b_first, w_second, b_second):
    dp = lax.axis_index("dp")
    groups = lax.axis_size("dp")
    inner = groups // MEMBERS
    micros = MICROS
    real = tokens.shape[0] // micros
    rows = (real + 15) // 16 * 16
    line = jnp.concatenate([norm_gain, norm_shift, b_second, jnp.zeros((1, FF - 3 * D), F32)], 1)
    par = jnp.concatenate([b_first, line, jnp.zeros((6, FF), F32)], 0)
    lo, ig, left, right, small = run_sections(
        tokens, cotangent, par, w_first[0], w_second[0], micros, rows, real
    )
    g_first, g_second, vec, layer_out, input_grad = reduce_weights(left, right, small, lo, ig, inner, real)

    if inner > 1:
        members = [[o * inner + i for i in range(inner)] for o in range(MEMBERS)]

        def over_members(part, dim):
            return lax.psum_scatter(
                part, "dp", scatter_dimension=dim, axis_index_groups=members, tiled=True
            )

        g_first = over_members(g_first, 0)
        g_second = over_members(g_second, 1)
        vec = lax.psum(vec, "dp", axis_index_groups=members)

    def piece(vec):
        size = vec.shape[0] // groups
        return lax.dynamic_slice_in_dim(vec, dp * size, size, 0)[None]

    return (
        layer_out,
        input_grad,
        piece(vec[0]),
        piece(vec[1]),
        g_first[None],
        piece(vec[3:7].reshape(FF)),
        g_second[None],
        piece(vec[2]),
    )


def solution(mesh):
    in_specs = (
        P("dp", None), P("dp", None), P("pipe", None), P("pipe", None),
        P("pipe", None, None), P("pipe", None), P("pipe", None, None), P("pipe", None),
    )
    out_specs = (
        P(("dp", "pipe"), None), P(("dp", "pipe"), None), P("pipe", "dp"), P("pipe", "dp"),
        P("pipe", "dp", None), P("pipe", "dp"), P("pipe", None, "dp"), P("pipe", "dp"),
    )
    return jax.shard_map(
        on_device, mesh=mesh, in_specs=in_specs, out_specs=out_specs, check_vma=False
    )
```

time: 345 us -> 259 us (0.75)
  the two profiles are of different devices: /device:TPU:0 before, /device:TPU:1 now
where the time goes in v2:
time: 259 us
  Pallas kernels  246 us (95%)
  local copies, waits for them, and re-layouts  10.6 us (4%)
    pallas_call x1, Pallas kernels, run_sections(): pl.pallas_call(functools.partial(sections_kernel, micros, rows, real), ou...  146 us
    pallas_call x1, Pallas kernels, reduce_weights(): pl.pallas_call(functools.partial(weights_kernel, inner, real), out_shape=...  100 us
    unnamed x8, local copies, waits for them, and re-layouts  6.98 us

profile of v2, /device:TPU:1, one launch (start us, length us, event | category | flops | bytes accessed | tf_op | source)
XLA Modules:
  0.0 259.0 jit_solution(17476426923278451128)
XLA Ops:
  0.6 0.1 pad.5.clone
  0.7 1.5 maximum_maximum_fusion.par
  2.2 146.0 %sections.1 = (bf16[2,304,768]{2,1,0:T(8,128)(2,1)}, bf16[2,304,768]{2,1,0:T(8,128)(2,1)}, bf16[2,2432,768]{2,1,0:T(8,128)(2,1)}, bf16[2432,6144]{1,0:T(8,128)(2,1)}, f32[8,768]{1,0:T(8,128)}) custom-call(bf16[2352,768]{1,0:T(8,128)(2,1)} %tok_ref.1, bf16[2352,768]{1,0:T(8,128)(2,1)} %cot_ref.1, f32[8,3072]{1,0:T(8,128)} %maximum_maximum_fusion.par, ...), custom_call_target="tpu_custom_call" | custom-call | flops 91804925952 | bytes 60000000 | tf_op jit(solution)/shard_map/sections/pallas_call | solution.py:564
  148.2 100.3 %weights.1 = (f32[96,3072]{1,0:T(8,128)}, f32[3072,96]{1,0:T(8,128)}, f32[8,768]{1,0:T(8,128)}, bf16[588,768]{1,0:T(8,128)(2,1)}, bf16[588,768]{1,0:T(8,128)(2,1)}) custom-call(bf16[2,2432,768]{2,1,0:T(8,128)(2,1)} %get-tuple-element.18.left_ref, bf16[2432,6144]{1,0:T(8,128)(2,1)} %get-tuple-element.19.right_ref, f32[8,768]{1,0:T(8,128)} %get-tuple-element.20.small, ...), custom_call_target="tpu_custom_call" | custom-call | flops 22951231488 | bytes 40000000 | tf_op jit(solution)/shard_map/weights/pallas_call | solution.py:760
  248.5 0.0 copy-start.1
  248.5 0.0 copy-start
  248.5 0.9 fusion
  249.5 0.6 constant_dynamic-slice_fusion
  250.1 0.6 constant_dynamic-slice_fusion.2
  250.6 0.7 slice.14
  251.4 0.1 dynamic_slice.14
  251.5 0.6 broadcast_in_dim.21
  252.0 2.9 %copy.16 = f32[1,3072,96]{1,2,0:T(8,128)} copy(f32[1,3072,96]{2,1,0:T(8,128)} %bitcast.4) | data formatting | bytes 2359296
  254.9 2.2 copy.20
  257.1 0.0 copy-done.1
  257.1 0.9 copy.21
  258.0 0.0 copy-done
  258.0 1.0 copy.22
  (3 shorter events, 0.0 us)
Async XLA Ops:
  248.5 8.6 %copy-start.1 = (bf16[588,768]{1,0:T(8,128)(2,1)S(1)}, bf16[588,768]{1,0:T(8,128)(2,1)}, u32[]{:S(2)}) copy-start(bf16[588,768]{1,0:T(8,128)(2,1)} %get-tuple-element.50) | copy-start | bytes 2709508
  248.5 9.5 %copy-start = (f32[96,3072]{1,0:T(8,128)S(1)}, f32[96,3072]{1,0:T(8,128)}, u32[]{:S(2)}) copy-start(f32[96,3072]{1,0:T(8,128)} %get-tuple-element.26) | copy-start | bytes 3538948

commit v3 on v2

--- a/solution.py
+++ b/solution.py
@@ -16,6 +16,8 @@
 MICROS = 8
 MEMBERS = 8
 BLOCK = D // MEMBERS
+CHUNK = 512
+GROUPS = {True: 3, False: 6}
 WIDE = 384
 MESH = pl.DeviceIdType.MESH
 BF = jnp.bfloat16
@@ -27,11 +29,8 @@
 
 
 def gelu_pair(h):
-    t = 1.0 / (1.0 + 0.3275911 * 0.7071067811865476 * jnp.abs(h))
-    poly = t * (0.127414796 + t * (-0.142248368 + t * (0.7107068705 + t * (-0.7265760135 + t * 0.5307027145))))
+    cdf = 0.5 + 0.5 * lax.erf(h * 0.7071067811865476)
     bell = jnp.exp(-0.5 * h * h)
-    tail = poly * bell
-    cdf = jnp.where(h >= 0, 1.0 - tail, tail)
     return h * cdf, cdf + h * (0.3989422804014327 * bell)
 
 
@@ -58,45 +57,75 @@
     return total
 
 
-def window_forward(q, k, v):
-    eight, four = head_masks(256), head_masks(128)
+def spread_turned(block):
+    turned = block.T
+    twice = jnp.concatenate([turned, turned], 1)
+    lane = lax.broadcasted_iota(jnp.int32, (1, 2 * PAD), 1) // PAD
+    none = jnp.zeros((32, 2 * PAD), block.dtype)
+    rows = []
+    for h in range(8):
+        part = jnp.where(lane == h % 2, twice[32 * h : 32 * (h + 1)], none)
+        rows.append(jnp.concatenate([part if c == h // 2 else none for c in range(4)], 1))
+    return jnp.concatenate(rows, 0)
+
+
+WIDE_STARTS = range(0, D, 256)
+STARTS = range(0, D, 128)
+
+
+def heads_apart(stacked, values):
+    four = head_masks(128)
+    parts = []
+    for n, s in enumerate(STARTS):
+        cols = slice(256 * (n % 2), 256 * (n % 2) + 256)
+        parts.append(gather_heads(dot(stacked[n // 2][:, cols], values[:, s : s + 128], 0, 0), four))
+    return parts
+
+
+def window_forward(qs, ks, vs):
+    every = range(len(qs))
     row = lax.broadcasted_iota(jnp.int32, (PAD, 1), 0)
     scores = [
-        dot(k[:, s : s + 256], spread(q[:, s : s + 256], eight), 1, 1) for s in range(0, D, 256)
+        [dot(ks[i][:, s : s + 256], spread_turned(qs[i][:, s : s + 256]), 1, 0) for s in WIDE_STARTS]
+        for i in every
     ]
     probs = []
-    for block in scores:
-        block = jnp.where(row < PATCHES, block, -1e30)
-        e = jnp.exp((block - jnp.max(block, 0, keepdims=True)) * SCALE)
-        probs.append((e * (1.0 / jnp.sum(e, 0, keepdims=True))).astype(BF))
-    parts = []
-    for n in range(D // 128):
-        cols = slice(256 * (n % 2), 256 * (n % 2) + 256)
-        parts.append(dot(probs[n // 2][:, cols], v[:, 128 * n : 128 * n + 128], 0, 0))
-    parts = [gather_heads(part, four) for part in parts]
-    return jnp.concatenate(probs, 1), jnp.concatenate(parts, 1)
-
-
-def window_backward(q, k, v, probs, d_att):
-    eight, four = head_masks(256), head_masks(128)
-    starts = range(0, D, 256)
-    wide = [spread(d_att[:, s : s + 256], eight) for s in starts]
-    d_probs = [dot(v[:, s : s + 256], wide[n], 1, 1) for n, s in enumerate(starts)]
-    d_v = [dot(probs[:, 2 * s : 2 * s + 512], wide[n], 1, 0) for n, s in enumerate(starts)]
+    for i in every:
+        blocks = []
+        for block in scores[i]:
+            block = jnp.where(row < PATCHES, block, -1e30)
+            e = jnp.exp((block - jnp.max(block, 0, keepdims=True)) * SCALE)
+            blocks.append((e * (1.0 / jnp.sum(e, 0, keepdims=True))).astype(BF))
+        probs.append(blocks)
+    parts = [jnp.concatenate(heads_apart(probs[i], vs[i]), 1) for i in every]
+    return [jnp.concatenate(blocks, 1) for blocks in probs], parts
+
+
+def window_backward(qs, ks, vs, probs, d_atts):
+    eight = head_masks(256)
+    every = range(len(qs))
+    d_probs = [
+        [dot(vs[i][:, s : s + 256], spread_turned(d_atts[i][:, s : s + 256]), 1, 0) for s in WIDE_STARTS]
+        for i in every
+    ]
+    d_v = [
+        [dot(probs[i][:, 2 * s : 2 * s + 512], spread(d_atts[i][:, s : s + 256], eight), 1, 0) for s in WIDE_STARTS]
+        for i in every
+    ]
     d_scores = []
-    for n, s in enumerate(starts):
-        p = probs[:, 2 * s : 2 * s + 512].astype(F32)
-        product = p * d_probs[n]
-        d_scores.append((product - p * jnp.sum(product, 0, keepdims=True)).astype(BF))
+    for i in every:
+        blocks = []
+        for n, s in enumerate(WIDE_STARTS):
+            p = probs[i][:, 2 * s : 2 * s + 512].astype(F32)
+            product = p * d_probs[i][n]
+            blocks.append((product - p * jnp.sum(product, 0, keepdims=True)).astype(BF))
+        d_scores.append(blocks)
     d_k = [
-        dot(d_scores[n], spread(q[:, s : s + 256], eight), 1, 0) * SCALE for n, s in enumerate(starts)
+        [dot(d_scores[i][n], spread(qs[i][:, s : s + 256], eight), 1, 0) * SCALE for n, s in enumerate(WIDE_STARTS)]
+        for i in every
     ]
-    d_q = []
-    for n in range(D // 128):
-        cols = slice(256 * (n % 2), 256 * (n % 2) + 256)
-        d_q.append(dot(d_scores[n // 2][:, cols], k[:, 128 * n : 128 * n + 128], 0, 0))
-    d_q = [gather_heads(part, four) * SCALE for part in d_q]
-    return jnp.concatenate(d_q, 1), jnp.concatenate(d_k, 1), jnp.concatenate(d_v, 1)
+    d_q = [[part * SCALE for part in heads_apart(d_scores[i], ks[i])] for i in every]
+    return [[jnp.concatenate(parts[i], 1) for parts in (d_q, d_k, d_v)] for i in every]
 
 
 def compress(block, masks):
@@ -107,41 +136,57 @@
     return total
 
 
-def diagonal(block, masks):
-    return jnp.concatenate([jnp.where(m, block, jnp.zeros_like(block)) for m in masks], 0)
-
-
-def channel_forward(q, k, v):
+def diagonal_turned(block):
+    turned = jnp.concatenate([block.T] * 4, 1)
+    r = lax.broadcasted_iota(jnp.int32, (128, 128), 0) // 32
+    c = lax.broadcasted_iota(jnp.int32, (128, 128), 1) // 32
+    return jnp.where(r == c, turned, jnp.zeros_like(turned))
+
+
+def channel_forward(qs, ks, vs):
     four = head_masks(128)
-    starts = range(0, D, 128)
-    scores = [dot(k[:, s : s + 128], q[:, s : s + 128], 0, 0) for s in starts]
-    scores = jnp.concatenate([compress(block, four) for block in scores], 1)
-    e = jnp.exp((scores - jnp.max(scores, 0, keepdims=True)) * SCALE)
-    probs = (e * (1.0 / jnp.sum(e, 0, keepdims=True))).astype(BF)
-    parts = [dot(v[:, s : s + 128], diagonal(probs[:, s : s + 128], four), 1, 0) for s in starts]
-    return probs, jnp.concatenate(parts, 1)
-
-
-def channel_backward(q, k, v, probs, d_att):
+    every = range(len(qs))
+    scores = [[dot(ks[i][:, s : s + 128], qs[i][:, s : s + 128], 0, 0) for s in STARTS] for i in every]
+    scores = [jnp.concatenate([compress(block, four) for block in scores[i]], 1) for i in every]
+    es = [jnp.exp((block - jnp.max(block, 0, keepdims=True)) * SCALE) for block in scores]
+    probs = [(e * (1.0 / jnp.sum(e, 0, keepdims=True))).astype(BF) for e in es]
+    parts = [
+        jnp.concatenate([dot(vs[i][:, s : s + 128], spread(probs[i][:, s : s + 128], four), 1, 0) for s in STARTS], 1)
+        for i in every
+    ]
+    return probs, parts
+
+
+def channel_backward(qs, ks, vs, probs, d_atts):
     four = head_masks(128)
-    starts = range(0, D, 128)
-    d_probs = [dot(v[:, s : s + 128], d_att[:, s : s + 128], 0, 0) for s in starts]
-    d_v = [dot(d_att[:, s : s + 128], diagonal(probs[:, s : s + 128], four), 1, 1) for s in starts]
-    d_probs = jnp.concatenate([compress(block, four) for block in d_probs], 1)
-    p = probs.astype(F32)
-    product = p * d_probs
-    d_scores = (product - p * jnp.sum(product, 0, keepdims=True)).astype(BF)
-    blocks = [diagonal(d_scores[:, s : s + 128], four) for s in starts]
-    d_q = [dot(k[:, s : s + 128], blocks[n], 1, 0) * SCALE for n, s in enumerate(starts)]
-    d_k = [dot(q[:, s : s + 128], blocks[n], 1, 1) * SCALE for n, s in enumerate(starts)]
-    return jnp.concatenate(d_q, 1), jnp.concatenate(d_k, 1), jnp.concatenate(d_v, 1)
+    every = range(len(qs))
+    d_probs = [[dot(vs[i][:, s : s + 128], d_atts[i][:, s : s + 128], 0, 0) for s in STARTS] for i in every]
+    d_v = [
+        [dot(d_atts[i][:, s : s + 128], diagonal_turned(probs[i][:, s : s + 128]), 1, 0) for s in STARTS]
+        for i in every
+    ]
+    d_scores = []
+    for i in every:
+        block = jnp.concatenate([compress(block, four) for block in d_probs[i]], 1)
+        p = probs[i].astype(F32)
+        product = p * block
+        d_scores.append((product - p * jnp.sum(product, 0, keepdims=True)).astype(BF))
+    d_q = [
+        [dot(ks[i][:, s : s + 128], spread(d_scores[i][:, s : s + 128], four), 1, 0) * SCALE for s in STARTS]
+        for i in every
+    ]
+    d_k = [
+        [dot(qs[i][:, s : s + 128], diagonal_turned(d_scores[i][:, s : s + 128]), 1, 0) * SCALE for s in STARTS]
+        for i in every
+    ]
+    return [[jnp.concatenate(parts[i], 1) for parts in (d_q, d_k, d_v)] for i in every]
 
 
 def sections_kernel(
     micros, rows, real,
     tok_ref, cot_ref, par, w1_ref, w2_ref,
     lo_ref, ig_ref, left_ref, right_ref, small_ref,
-    w1, w2, big, probs, x_in, g_in, v_out, g_out, raw, normed, att_low, wide, acc, tmp, att_in, d_att, d_split,
+    w1, w2, big, probs, x_in, g_in, v_out, g_out, raw, normed, att_low, wide, acc, tmp,
     w_sem, raw_sem, v_send, v_recv, g_send, g_recv, f_send, f_recv, k_sem, kg_sem, kh_sem,
 ):
     dp, role = lax.axis_index("dp"), lax.axis_index("pipe")
@@ -159,7 +204,7 @@
     load_1.start()
 
     def owner(m):
-        return (m // share + 2) % 4
+        return 3 - m // share
 
     def first_row(m):
         return owner(m) * (share * real) + (m % share) * real
@@ -272,9 +317,6 @@
         part = src[PATCHES * n : PATCHES * n + PAD, c : c + D]
         return jnp.where(image_row < PATCHES, part, 0.0).astype(BF)
 
-    def image_at(i):
-        return pl.ds(pl.multiple_of(i * PAD, PAD), PAD)
-
     def attention_forward(m, spatial):
         x = x_in[m].astype(F32)
         norm_forward(m, x)
@@ -284,17 +326,21 @@
             for c in range(0, 3 * D, D):
                 big[m, PAD * i : PAD * (i + 1), c : c + D] = cut(tmp, i, c)
 
-        def one_image(i, carry):
-            q, k, v = (big[m, image_at(i), n * D : (n + 1) * D] for n in range(3))
+        for start in range(0, images, GROUPS[spatial]):
+            some = range(start, min(start + GROUPS[spatial], images))
+            qs, ks, vs = (
+                [big[m, PAD * i : PAD * (i + 1), n * D : (n + 1) * D] for i in some] for n in range(3)
+            )
             if spatial:
-                probs[m * images + i], att_in[i] = window_forward(q, k, v)
+                kept, parts = window_forward(qs, ks, vs)
+                for i, p in zip(some, kept):
+                    probs[m * images + i] = p
             else:
-                probs[m * images + i, 0:32, 0:D], att_in[i] = channel_forward(q, k, v)
-            return carry
-
-        lax.fori_loop(0, images, one_image, 0)
-        for i in range(images):
-            acc[PATCHES * i : PATCHES * i + PAD, :] = att_in[i]
+                kept, parts = channel_forward(qs, ks, vs)
+                for i, p in zip(some, kept):
+                    probs[m * images + i, 0:32, 0:D] = p
+            for i, part in zip(some, parts):
+                acc[PATCHES * i : PATCHES * i + PAD, :] = part
         acc[real:rows, :] = jnp.zeros((rows - real, D), F32)
         again(m, keep_left(1, m, att_low))
         att_low[...] = acc[0:rows, :].astype(BF)
@@ -307,23 +353,20 @@
         g = g_in[m]
         small_ref[6:7, :] += jnp.sum(g.astype(F32), 0, keepdims=True)
         acc[0:rows, :] = dot(g, w1[:, 3 * D :], 1, 1)
-        for i in range(images):
-            d_att[i] = cut(acc, i, 0)
-
-        def one_image(i, carry):
-            q, k, v = (big[m, image_at(i), n * D : (n + 1) * D] for n in range(3))
+        for start in range(0, images, GROUPS[spatial]):
+            some = range(start, min(start + GROUPS[spatial], images))
+            qs, ks, vs = (
+                [big[m, PAD * i : PAD * (i + 1), n * D : (n + 1) * D] for i in some] for n in range(3)
+            )
+            d_atts = [cut(acc, i, 0) for i in some]
             if spatial:
-                grads = window_backward(q, k, v, probs[m * images + i], d_att[i])
+                grads = window_backward(qs, ks, vs, [probs[m * images + i] for i in some], d_atts)
             else:
-                grads = channel_backward(q, k, v, probs[m * images + i, 0:32, 0:D], d_att[i])
-            for n in range(3):
-                d_split[i, :, n * D : (n + 1) * D] = grads[n].astype(BF)
-            return carry
-
-        lax.fori_loop(0, images, one_image, 0)
-        for i in range(images):
-            for c in range(0, 3 * D, D):
-                tmp[PATCHES * i : PATCHES * i + PAD, c : c + D] = d_split[i, :, c : c + D].astype(F32)
+                kept = [probs[m * images + i, 0:32, 0:D] for i in some]
+                grads = channel_backward(qs, ks, vs, kept, d_atts)
+            for i, parts in zip(some, grads):
+                for n in range(3):
+                    tmp[PATCHES * i : PATCHES * i + PAD, n * D : (n + 1) * D] = parts[n]
         tmp[real:rows, :] = jnp.zeros((rows - real, 3 * D), F32)
         again(m, keep_wide(m, 0, 3 * D))
         for n in range(3):
@@ -337,15 +380,13 @@
         x = x_in[m].astype(F32)
         norm_forward(m, x)
         again(m, keep_wide(m, FF, FF))
-        acc[0:rows, :] = x + bias_out
-        for c in range(0, FF, D):
-            hidden = dot(normed[...], w1[:, c : c + D], 1, 0) + bias[:, c : c + D]
+        for c in range(0, FF, CHUNK):
+            hidden = dot(normed[...], w1[:, c : c + CHUNK], 1, 0) + bias[:, c : c + CHUNK]
             value, diff = gelu_pair(hidden)
-            wide[:, c : c + D] = value.astype(BF)
-            big[m, 0:rows, c : c + D] = diff.astype(BF)
-            acc[0:rows, :] += dot(wide[:, c : c + D], w2[c : c + D, :], 1, 0)
+            wide[:, c : c + CHUNK] = value.astype(BF)
+            big[m, 0:rows, c : c + CHUNK] = diff.astype(BF)
         keep_wide(m, FF, FF).start()
-        v_out[m % 2] = acc[0:rows, :].astype(BF)
+        v_out[m % 2] = (x + bias_out + dot(wide[...], w2[...], 1, 0)).astype(BF)
 
     def feed_backward(m):
         keep_gout_left(m).start()
@@ -356,13 +397,8 @@
             d_hid = (d_act * big[m, 0:rows, c : c + D].astype(F32)).astype(BF)
             big[m, 0:rows, c : c + D] = d_hid
             small_ref[3 + n : 4 + n, :] += jnp.sum(d_hid.astype(F32), 0, keepdims=True)
-            back = dot(d_hid, w1[:, c : c + D], 1, 1)
-            if n == 0:
-                acc[0:rows, :] = back
-            else:
-                acc[0:rows, :] += back
         keep_hidden(m).start()
-        g_out[m % 2] = norm_back(acc[0:rows, :], m)
+        g_out[m % 2] = norm_back(dot(big[m, 0:rows], w1[...], 1, 1), m)
 
     def forward(m, run, first, last):
         if first:
@@ -548,9 +584,6 @@
         pltpu.VMEM((rows, FF), BF),
         pltpu.VMEM((tall, D), F32),
         pltpu.VMEM((tall, 3 * D), F32),
-        pltpu.VMEM((images, PAD, D), F32),
-        pltpu.VMEM((images, PAD, D), BF),
-        pltpu.VMEM((images, PAD, 3 * D), BF),
         dma((2,)), dma((2,)), dma((micros,)), dma((micros,)), dma((micros,)), dma((micros,)),
         dma((micros,)), dma((2, share)), dma((3,)), dma((micros,)), dma((micros,)),
     ]

time: 259 us -> 229 us (0.88)
  Pallas kernels: 246 us -> 216 us
    pallas_call x1, Pallas kernels: 146 us -> 117 us  [run_sections(): pl.pallas_call(functools.partial(sections_kernel, micros, rows, real), ou...]
where the time goes in v3:
time: 229 us
  Pallas kernels  216 us (94%)
  local copies, waits for them, and re-layouts  10.6 us (5%)
    pallas_call x1, Pallas kernels, run_sections(): pl.pallas_call(functools.partial(sections_kernel, micros, rows, real), ou...  117 us
    pallas_call x1, Pallas kernels, reduce_weights(): pl.pallas_call(functools.partial(weights_kernel, inner, real), out_shape=...  98.6 us
    unnamed x8, local copies, waits for them, and re-layouts  6.98 us

profile of v3, /device:TPU:1, one launch (start us, length us, event | category | flops | bytes accessed | tf_op | source)
XLA Modules:
  0.0 228.7 jit_solution(2257310777591980961)
XLA Ops:
  0.6 0.1 pad.5.clone
  0.7 1.5 maximum_maximum_fusion.par
  2.2 117.4 %sections.1 = (bf16[2,304,768]{2,1,0:T(8,128)(2,1)}, bf16[2,304,768]{2,1,0:T(8,128)(2,1)}, bf16[2,2432,768]{2,1,0:T(8,128)(2,1)}, bf16[2432,6144]{1,0:T(8,128)(2,1)}, f32[8,768]{1,0:T(8,128)}) custom-call(bf16[2352,768]{1,0:T(8,128)(2,1)} %tok_ref.1, bf16[2352,768]{1,0:T(8,128)(2,1)} %cot_ref.1, f32[8,3072]{1,0:T(8,128)} %maximum_maximum_fusion.par, ...), custom_call_target="tpu_custom_call" | custom-call | flops 91804925952 | bytes 60000000 | tf_op jit(solution)/shard_map/sections/pallas_call | solution.py:597
  119.6 98.6 %weights.1 = (f32[96,3072]{1,0:T(8,128)}, f32[3072,96]{1,0:T(8,128)}, f32[8,768]{1,0:T(8,128)}, bf16[588,768]{1,0:T(8,128)(2,1)}, bf16[588,768]{1,0:T(8,128)(2,1)}) custom-call(bf16[2,2432,768]{2,1,0:T(8,128)(2,1)} %get-tuple-element.18.left_ref, bf16[2432,6144]{1,0:T(8,128)(2,1)} %get-tuple-element.19.right_ref, f32[8,768]{1,0:T(8,128)} %get-tuple-element.20.small, ...), custom_call_target="tpu_custom_call" | custom-call | flops 22951231488 | bytes 40000000 | tf_op jit(solution)/shard_map/weights/pallas_call | solution.py:793
  218.2 0.0 copy-start.1
  218.2 0.0 copy-start
  218.2 0.9 fusion
  219.2 0.6 constant_dynamic-slice_fusion
  219.8 0.6 constant_dynamic-slice_fusion.2
  220.3 0.7 slice.14
  221.1 0.1 dynamic_slice.14
  221.2 0.6 broadcast_in_dim.21
  221.7 2.9 %copy.16 = f32[1,3072,96]{1,2,0:T(8,128)} copy(f32[1,3072,96]{2,1,0:T(8,128)} %bitcast.4) | data formatting | bytes 2359296
  224.6 2.2 copy.20
  226.8 0.0 copy-done.1
  226.8 0.9 copy.21
  227.7 0.0 copy-done
  227.7 1.0 copy.22
  (3 shorter events, 0.0 us)
Async XLA Ops:
  218.2 8.6 %copy-start.1 = (bf16[588,768]{1,0:T(8,128)(2,1)S(1)}, bf16[588,768]{1,0:T(8,128)(2,1)}, u32[]{:S(2)}) copy-start(bf16[588,768]{1,0:T(8,128)(2,1)} %get-tuple-element.50) | copy-start | bytes 2709508
  218.2 9.5 %copy-start = (f32[96,3072]{1,0:T(8,128)S(1)}, f32[96,3072]{1,0:T(8,128)}, u32[]{:S(2)}) copy-start(f32[96,3072]{1,0:T(8,128)} %get-tuple-element.26) | copy-start | bytes 3538948

commit v4 on v3

--- a/solution.py
+++ b/solution.py
@@ -18,7 +18,7 @@
 BLOCK = D // MEMBERS
 CHUNK = 512
 GROUPS = {True: 3, False: 6}
-WIDE = 384
+WIDE = 256
 MESH = pl.DeviceIdType.MESH
 BF = jnp.bfloat16
 F32 = jnp.float32
@@ -184,7 +184,7 @@
 
 def sections_kernel(
     micros, rows, real,
-    tok_ref, cot_ref, par, w1_ref, w2_ref,
+    tok_ref, cot_ref, gain_ref, shift_ref, bias_ref, bias_out_ref, w1_ref, w2_ref,
     lo_ref, ig_ref, left_ref, right_ref, small_ref,
     w1, w2, big, probs, x_in, g_in, v_out, g_out, raw, normed, att_low, wide, acc, tmp,
     w_sem, raw_sem, v_send, v_recv, g_send, g_recv, f_send, f_recv, k_sem, kg_sem, kh_sem,
@@ -204,10 +204,10 @@
     load_1.start()
 
     def owner(m):
-        return 3 - m // share
+        return m // share
 
     def first_row(m):
-        return owner(m) * (share * real) + (m % share) * real
+        return m * real
 
     def slab_start(m):
         return pl.multiple_of(jnp.minimum(first_row(m) // 16 * 16, total - slab), 16)
@@ -267,35 +267,38 @@
             device_id=(dp, (role + 3) % 4), device_id_type=MESH,
         )
 
-    def result_hop(n, src, ref, m):
+    def result_hop(m):
         return pltpu.make_async_remote_copy(
-            src_ref=src.at[m % 2], dst_ref=ref.at[m % share], send_sem=f_send.at[m],
-            recv_sem=f_recv.at[n, m % share], device_id=(dp, owner(m)), device_id_type=MESH,
-        )
-
-    def result_here(src, ref, m):
-        return pltpu.make_async_copy(src.at[m % 2], ref.at[m % share], f_send.at[m])
-
-    def result_start(n, src, ref, m):
+            src_ref=v_out.at[m % 2], dst_ref=lo_ref.at[m % share], send_sem=f_send.at[m],
+            recv_sem=f_recv.at[m % share], device_id=(dp, owner(m)), device_id_type=MESH,
+        )
+
+    def result_here(m):
+        return pltpu.make_async_copy(v_out.at[m % 2], lo_ref.at[m % share], f_send.at[m])
+
+    def result_start(m):
         @pl.when(owner(m) == role)
         def _():
-            result_here(src, ref, m).start()
+            result_here(m).start()
 
         @pl.when(owner(m) != role)
         def _():
-            result_hop(n, src, ref, m).start()
-
-    def result_wait(n, src, ref, m):
+            result_hop(m).start()
+
+    def result_wait(m):
         @pl.when(owner(m) == role)
         def _():
-            result_here(src, ref, m).wait()
+            result_here(m).wait()
 
         @pl.when(owner(m) != role)
         def _():
-            result_hop(n, src, ref, m).wait_send()
-
-    bias = par[0:1, :]
-    gain, shift_row, bias_out = par[1:2, :D], par[1:2, D : 2 * D], par[1:2, 2 * D : 3 * D]
+            result_hop(m).wait_send()
+
+    def grad_here(m):
+        return pltpu.make_async_copy(g_out.at[m % 2], ig_ref.at[m], g_send.at[m])
+
+    bias, bias_out = bias_ref[...], bias_out_ref[...]
+    gain, shift_row = gain_ref[...], shift_ref[...]
     image_row = lax.broadcasted_iota(jnp.int32, (PAD, 1), 0)
 
     def norm_forward(m, x):
@@ -412,14 +415,14 @@
 
         run(m)
         if last is True:
-            result_start(0, v_out, lo_ref, m)
+            result_start(m)
         elif last is False:
             next_hop(m).start()
         else:
 
             @pl.when(last)
             def _():
-                result_start(0, v_out, lo_ref, m)
+                result_start(m)
 
             @pl.when(jnp.logical_not(last))
             def _():
@@ -432,7 +435,7 @@
 
             @pl.when(last)
             def _():
-                result_wait(0, v_out, lo_ref, m)
+                result_wait(m)
 
             @pl.when(jnp.logical_not(last))
             def _():
@@ -457,13 +460,13 @@
 
         run(m)
         if first:
-            result_start(1, g_out, ig_ref, m)
+            grad_here(m).start()
         else:
             back_hop(m).start()
 
     def finish_backward(m, first):
         if first:
-            result_wait(1, g_out, ig_ref, m)
+            grad_here(m).wait()
         else:
             back_hop(m).wait_send()
 
@@ -547,21 +550,16 @@
 
     keep_left(0, micros - 1, normed).wait()
 
-    def arrived(n, carry):
-        @pl.when(role != 3)
-        def _():
-            result_hop(0, v_out, lo_ref, n).wait_recv()
-
-        @pl.when(role != 0)
-        def _():
-            result_hop(1, g_out, ig_ref, n).wait_recv()
-
-        return carry
-
-    lax.fori_loop(0, share, arrived, 0)
-
-
-def run_sections(tokens, cotangent, par, w1, w2, micros, rows, real):
+    @pl.when(role != 3)
+    def _():
+        def arrived(n, carry):
+            result_hop(n).wait_recv()
+            return carry
+
+        lax.fori_loop(0, share, arrived, 0)
+
+
+def run_sections(tokens, cotangent, gain, shift, bias, bias_out, w1, w2, micros, rows, real):
     images = real // PATCHES
     tall = max((PATCHES * (images - 1) + PAD + 7) // 8 * 8, rows)
     share = micros // 4
@@ -585,11 +583,11 @@
         pltpu.VMEM((tall, D), F32),
         pltpu.VMEM((tall, 3 * D), F32),
         dma((2,)), dma((2,)), dma((micros,)), dma((micros,)), dma((micros,)), dma((micros,)),
-        dma((micros,)), dma((2, share)), dma((3,)), dma((micros,)), dma((micros,)),
+        dma((micros,)), dma((share,)), dma((3,)), dma((micros,)), dma((micros,)),
     ]
     out_shape = (
         jax.ShapeDtypeStruct((share, rows, D), BF),
-        jax.ShapeDtypeStruct((share, rows, D), BF),
+        jax.ShapeDtypeStruct((micros, rows, D), BF),
         jax.ShapeDtypeStruct((2, micros * rows, D), BF),
         jax.ShapeDtypeStruct((micros * rows, 2 * FF), BF),
         jax.ShapeDtypeStruct((8, D), F32),
@@ -597,7 +595,7 @@
     return pl.pallas_call(
         functools.partial(sections_kernel, micros, rows, real),
         out_shape=out_shape,
-        in_specs=[hbm, hbm, vmem, hbm, hbm],
+        in_specs=[hbm, hbm, vmem, vmem, vmem, vmem, hbm, hbm],
         out_specs=(hbm, hbm, hbm, hbm, vmem),
         scratch_shapes=scratch,
         compiler_params=pltpu.CompilerParams(
@@ -607,19 +605,20 @@
             flops=2 * 4 * 2 * D * FF * micros * rows, bytes_accessed=60_000_000, transcendentals=0
         ),
         name="sections",
-    )(tokens, cotangent, par, w1, w2)
-
-
-LAG_X, LAG_Z, LAG_OUT = 0, 3, 6
+    )(tokens, cotangent, gain, shift, bias, bias_out, w1, w2)
+
+
+X_LAG = 5
+HOP = 3
 RING = 4
 
 
 def weights_kernel(
     inner, real,
     left_ref, right_ref, small, lo_ref, ig_ref,
-    first_ref, second_ref, vec_ref, lo_out, ig_out,
-    left, ring, part, from_x, from_z, vec_x, vec_z, halves, joined,
-    l_sem, r_sem, x_send, x_recv, z_send, z_recv, v_send, v_recv, h_sem,
+    first_out, second_out, vec_ref, lo_out, ig_out,
+    left, ring, part, from_x, from_z, vec_x, vec_z, lo_in, ig_in, joined, results, first_ref, second_ref,
+    l_sem, r_sem, x_send, x_recv, z_send, z_recv, v_send, v_recv, h_sem, g_send, g_recv, o_sem,
 ):
     dp, role = lax.axis_index("dp"), lax.axis_index("pipe")
     feed = role % 2
@@ -628,6 +627,8 @@
     lines = MEMBERS // 2
     per = FF // WIDE
     steps = per + per * feed
+    share = lo_in.shape[0]
+    all_steps = steps + (lines - 1) * HOP + X_LAG
 
     def at(zz, xx):
         return ((zz * 2 + xx) * inner + rest, role)
@@ -644,16 +645,34 @@
         cols = pl.ds(pl.multiple_of(k * WIDE, 128), WIDE)
         return pltpu.make_async_copy(right_ref.at[:, cols], ring.at[k % RING], r_sem.at[k % RING])
 
+    @pl.when(role != 0)
+    def _():
+        pl.semaphore_signal(barrier, inc=1, device_id=(dp, 0), device_id_type=MESH)
+
     load_left(0).start()
     load_right(0).start()
-    for k in range(1, RING - 1):
-        load_right(k).start()
-    load_left(1).start()
-    load_lo = pltpu.make_async_copy(lo_ref, halves.at[0], h_sem.at[0])
-    load_ig = pltpu.make_async_copy(ig_ref, halves.at[1], h_sem.at[1])
-    load_lo.start()
-    load_ig.start()
-    pl.semaphore_wait(barrier, lines)
+    load_lo = pltpu.make_async_copy(lo_ref, lo_in, h_sem.at[0])
+    load_ig = pltpu.make_async_copy(ig_ref.at[pl.ds(0, share)], ig_in, h_sem.at[1])
+
+    def grads_to(n):
+        return pltpu.make_async_remote_copy(
+            src_ref=ig_ref.at[pl.ds(n * share, share)], dst_ref=ig_in, send_sem=g_send.at[n - 1], recv_sem=g_recv,
+            device_id=(dp, n), device_id_type=MESH,
+        )
+
+    @pl.when(role == 0)
+    def _():
+        pl.semaphore_wait(barrier, lines + 3)
+        load_ig.start()
+        for n in range(1, 4):
+            grads_to(n).start()
+
+    @pl.when(role != 0)
+    def _():
+        pl.semaphore_wait(barrier, lines)
+
+    def z_first(k):
+        return jnp.where(feed == 1, k % 5 == 1, k == 0)
 
     def to_x(k):
         return pltpu.make_async_remote_copy(
@@ -661,17 +680,108 @@
             device_id=at(z, 1 - x), device_id_type=MESH,
         )
 
-    def to_z(k, zz):
+    def block_to_x(k):
         return pltpu.make_async_remote_copy(
-            src_ref=part.at[k, zz, x], dst_ref=from_z.at[k, z], send_sem=z_send.at[k, zz],
-            recv_sem=z_recv.at[k, z], device_id=at(zz, x), device_id_type=MESH,
-        )
-
-    def arrived_z(k, zz):
+            src_ref=part.at[k, z, 1 - x], dst_ref=from_x.at[k, 0], send_sem=x_send.at[k], recv_sem=x_recv.at[k],
+            device_id=at(z, 1 - x), device_id_type=MESH,
+        )
+
+    def hop(k, b, slot, target, whole):
+        src = part.at[k, b] if whole else part.at[k, b, x]
+        dst = from_z.at[k, slot] if whole else from_z.at[k, slot, 0]
         return pltpu.make_async_remote_copy(
-            src_ref=part.at[k, zz, x], dst_ref=from_z.at[k, zz], send_sem=z_send.at[k, zz],
-            recv_sem=z_recv.at[k, zz], device_id=at(zz, x), device_id_type=MESH,
-        )
+            src_ref=src, dst_ref=dst, send_sem=z_send.at[k, b], recv_sem=z_recv.at[k, slot],
+            device_id=at(target, x), device_id_type=MESH,
+        )
+
+    def up(k, b, whole):
+        return hop(k, b, b, jnp.minimum(z + 1, lines - 1), whole)
+
+    def down(k, b, whole):
+        return hop(k, b, jnp.where(b == z - 1, lines, b), jnp.maximum(z - 1, 0), whole)
+
+    def come(k, slot, whole):
+        hop(k, 0, slot, z, whole).wait_recv()
+
+    def add(k, b, slot, whole):
+        come(k, slot, whole)
+        if whole:
+            part[k, b] = (part[k, b].astype(F32) + from_z[k, slot].astype(F32)).astype(BF)
+        else:
+            part[k, b, x] = (part[k, b, x].astype(F32) + from_z[k, slot, 0].astype(F32)).astype(BF)
+
+    def in_range(k, whole):
+        kind = z_first(k) if whole else jnp.logical_not(z_first(k))
+        return (k >= 0) & (k < steps) & kind
+
+    def put_first(k):
+        place = pl.ds(pl.multiple_of((k % per) * WIDE, 128), WIDE)
+        return pltpu.make_async_copy(first_ref.at[:, place], first_out.at[:, place], o_sem.at[k])
+
+    def put_second(k):
+        place = pl.ds(pl.multiple_of((k % per) * WIDE, 128), WIDE)
+        return pltpu.make_async_copy(second_ref.at[:, place], second_out.at[:, place], o_sem.at[k])
+
+    put_zeros = pltpu.make_async_copy(second_ref, second_out, o_sem.at[per])
+
+    def write(k, total):
+        place = pl.ds(pl.multiple_of((k % per) * WIDE, 128), WIDE)
+
+        @pl.when(k < per)
+        def _():
+            first_ref[:, place] = total
+            put_first(k).start()
+
+        @pl.when(k >= per)
+        def _():
+            second_ref[:, place] = total
+            put_second(k).start()
+
+    def along_z(s, base, whole):
+        k_up = s - base - HOP * z
+
+        @pl.when(in_range(k_up, whole))
+        def _():
+            for b in range(1, lines):
+
+                @pl.when(b > z)
+                def _():
+                    @pl.when(z > 0)
+                    def _():
+                        add(k_up, b, b, whole)
+
+                    up(k_up, b, whole).start()
+
+        k_down = s - base - HOP * (lines - 1 - z)
+
+        @pl.when(in_range(k_down, whole))
+        def _():
+            for b in range(lines - 1):
+
+                @pl.when(b < z)
+                def _():
+                    @pl.when(z < lines - 1)
+                    def _():
+                        add(k_down, b, b, whole)
+
+                    down(k_down, b, whole).start()
+
+        k_end = s - base - HOP * (lines - 1)
+
+        @pl.when(in_range(k_end, whole))
+        def _():
+            @pl.when(z > 0)
+            def _():
+                add(k_end, z, z, whole)
+
+            @pl.when(z < lines - 1)
+            def _():
+                add(k_end, z, lines, whole)
+
+            if whole:
+                block_to_x(k_end).start()
+            else:
+                write(k_end, part[k_end, z, x].astype(F32))
 
     vec_to_x = pltpu.make_async_remote_copy(
         src_ref=small, dst_ref=vec_x.at[0], send_sem=v_send.at[0], recv_sem=v_recv.at[0],
@@ -691,7 +801,16 @@
         )
 
     load_left(0).wait()
+    for k in range(1, RING - 1):
+        load_right(k).start()
+    load_left(1).start()
+    load_lo.start()
     edge = jnp.where(feed == 1, per, 3 * D // WIDE)
+
+    def join(pieces, n):
+        for i in range(share):
+            joined[real * i : real * (i + 1), :] = pieces[i, :real].astype(F32)
+        results[n] = joined[: results.shape[1], :].astype(BF)
 
     def step(s, carry):
         @pl.when(s < steps)
@@ -708,35 +827,26 @@
 
             product = dot(left[s // edge], ring[s % RING], 0, 0)
             part[s] = product.astype(BF).reshape(lines, 2, BLOCK, WIDE)
-            to_x(s).start()
-
-        k2 = s - LAG_Z
-
-        @pl.when((k2 >= 0) & (k2 < steps))
-        def _():
-            to_x(k2).wait_recv()
-            part[k2, :, x] = (part[k2, :, x].astype(F32) + from_x[k2].astype(F32)).astype(BF)
-            for i in range(1, lines):
-                to_z(k2, (z + i) % lines).start()
-
-        k3 = s - LAG_OUT
-
-        @pl.when((k3 >= 0) & (k3 < steps))
-        def _():
-            total = part[k3, z, x].astype(F32)
-            for i in range(1, lines):
-                zz = (z + i) % lines
-                arrived_z(k3, zz).wait_recv()
-                total += from_z[k3, zz].astype(F32)
-            place = pl.multiple_of((k3 % per) * WIDE, 128)
-
-            @pl.when(k3 < per)
-            def _():
-                first_ref[:, pl.ds(place, WIDE)] = total
-
-            @pl.when(k3 >= per)
-            def _():
-                second_ref[pl.ds(place, WIDE), :] = total.T
+
+            @pl.when(jnp.logical_not(z_first(s)))
+            def _():
+                to_x(s).start()
+
+        k_x = s - X_LAG
+
+        @pl.when(in_range(k_x, False))
+        def _():
+            to_x(k_x).wait_recv()
+            part[k_x, :, x] = (part[k_x, :, x].astype(F32) + from_x[k_x].astype(F32)).astype(BF)
+
+        along_z(s, 0, True)
+        along_z(s, X_LAG, False)
+        k_out = s - (lines - 1) * HOP - X_LAG
+
+        @pl.when(in_range(k_out, True))
+        def _():
+            block_to_x(k_out).wait_recv()
+            write(k_out, part[k_out, z, x].astype(F32) + from_x[k_out, 0].astype(F32))
 
         @pl.when(s == 0)
         def _():
@@ -745,14 +855,26 @@
             @pl.when(feed == 0)
             def _():
                 second_ref[...] = jnp.zeros_like(second_ref)
+                put_zeros.start()
 
         @pl.when(s == 2)
         def _():
-            for n, load, dst in ((0, load_lo, lo_out), (1, load_ig, ig_out)):
-                load.wait()
-                for i in range(halves.shape[1]):
-                    joined[real * i : real * (i + 1), :] = halves[n, i, :real].astype(F32)
-                dst[...] = joined[: dst.shape[0], :].astype(BF)
+            load_lo.wait()
+            join(lo_in, 0)
+            pltpu.make_async_copy(results.at[0], lo_out, h_sem.at[0]).start()
+
+        @pl.when(s == all_steps - 2)
+        def _():
+            @pl.when(role == 0)
+            def _():
+                load_ig.wait()
+
+            @pl.when(role != 0)
+            def _():
+                grads_to(1).wait_recv()
+
+            join(ig_in, 1)
+            pltpu.make_async_copy(results.at[1], ig_out, h_sem.at[1]).start()
 
         @pl.when(s == 4)
         def _():
@@ -763,7 +885,7 @@
 
         return carry
 
-    lax.fori_loop(0, steps + LAG_OUT, step, 0)
+    lax.fori_loop(0, all_steps, step, 0)
     total = vec_x[1]
     for i in range(1, lines):
         zz = (z + i) % lines
@@ -774,12 +896,40 @@
     vec_to_x.wait_send()
 
     def drain(k, carry):
-        to_x(k).wait_send()
-        for i in range(1, lines):
-            to_z(k, (z + i) % lines).wait_send()
+        for whole in (False, True):
+
+            @pl.when(in_range(k, whole))
+            def _():
+                (block_to_x(k) if whole else to_x(k)).wait_send()
+                for b in range(lines):
+
+                    @pl.when(b != z)
+                    def _():
+                        up(k, b, whole).wait_send()
+
+        @pl.when(k < per)
+        def _():
+            put_first(k).wait()
+
+        @pl.when(k >= per)
+        def _():
+            put_second(k).wait()
+
         return carry
 
     lax.fori_loop(0, steps, drain, 0)
+
+    @pl.when(feed == 0)
+    def _():
+        put_zeros.wait()
+
+    @pl.when(role == 0)
+    def _():
+        for n in range(1, 4):
+            grads_to(n).wait_send()
+
+    pltpu.make_async_copy(results.at[0], lo_out, h_sem.at[0]).wait()
+    pltpu.make_async_copy(results.at[1], ig_out, h_sem.at[1]).wait()
 
 
 def reduce_weights(left, right, small, lo, ig, inner, real):
@@ -794,25 +944,30 @@
         functools.partial(weights_kernel, inner, real),
         out_shape=(
             jax.ShapeDtypeStruct((BLOCK, FF), F32),
-            jax.ShapeDtypeStruct((FF, BLOCK), F32),
+            jax.ShapeDtypeStruct((BLOCK, FF), F32),
             jax.ShapeDtypeStruct((8, D), F32),
             jax.ShapeDtypeStruct((share * real, D), BF),
             jax.ShapeDtypeStruct((share * real, D), BF),
         ),
         in_specs=[hbm, hbm, vmem, hbm, hbm],
-        out_specs=(vmem, vmem, vmem, vmem, vmem),
+        out_specs=(hbm, hbm, vmem, hbm, hbm),
         scratch_shapes=[
             pltpu.VMEM((2, count, D), BF),
             pltpu.VMEM((RING, count, WIDE), BF),
             pltpu.VMEM((2 * per, lines, 2, BLOCK, WIDE), BF),
             pltpu.VMEM((2 * per, lines, BLOCK, WIDE), BF),
-            pltpu.VMEM((2 * per, lines, BLOCK, WIDE), BF),
+            pltpu.VMEM((2 * per, lines + 1, 2, BLOCK, WIDE), BF),
             pltpu.VMEM((2, 8, D), F32),
             pltpu.VMEM((lines, 8, D), F32),
-            pltpu.VMEM((2,) + lo.shape, BF),
+            pltpu.VMEM(lo.shape, BF),
+            pltpu.VMEM(lo.shape, BF),
             pltpu.VMEM(((share * real + 7) // 8 * 8, D), F32),
+            pltpu.VMEM((2, share * real, D), BF),
+            pltpu.VMEM((BLOCK, FF), F32),
+            pltpu.VMEM((BLOCK, FF), F32),
             dma((2,)), dma((RING,)), dma((2 * per,)), dma((2 * per,)),
-            dma((2 * per, lines)), dma((2 * per, lines)), dma((1 + lines,)), dma((1 + lines,)), dma((2,)),
+            dma((2 * per, lines)), dma((2 * per, lines + 1)), dma((1 + lines,)), dma((1 + lines,)), dma((2,)),
+            dma((3,)), dma(()), dma((2 * per,)),
         ],
         compiler_params=pltpu.CompilerParams(
             collective_id=1, has_side_effects=True, vmem_limit_bytes=63 * 2**20
@@ -824,17 +979,68 @@
     )(left, right, small, lo, ig)
 
 
+def finish_kernel(
+    groups, first, second, vec, lo, ig,
+    first_out, second_out, lo_out, ig_out, gain_out, shift_out, bias_out, last_out,
+    first_mid, second_mid, lo_mid, ig_mid, in_sem, out_sem,
+):
+    arrays = (
+        (first, first_mid, first_out), (second, second_mid, second_out), (lo, lo_mid, lo_out), (ig, ig_mid, ig_out)
+    )
+    come = [pltpu.make_async_copy(src, mid, in_sem.at[n]) for n, (src, mid, _) in enumerate(arrays)]
+    go = [pltpu.make_async_copy(mid, dst, out_sem.at[n]) for n, (_, mid, dst) in enumerate(arrays)]
+    for copy in come:
+        copy.start()
+    dp = lax.axis_index("dp")
+    size = D // groups
+    turned = pltpu.roll(vec[...], lax.rem(D - dp * size, D), 1)
+    gain_out[...] = turned[0:1, :size]
+    shift_out[...] = turned[1:2, :size]
+    last_out[...] = turned[2:3, :size]
+    for n in range(4):
+        @pl.when(dp // (groups // 4) == n)
+        def _():
+            shift = (dp % (groups // 4)) * (4 * size)
+            bias_out[...] = pltpu.roll(vec[3 + n : 4 + n, :], lax.rem(D - shift, D), 1)[:, : 4 * size]
+
+    for first_half, second_half in zip(come, go):
+        first_half.wait()
+        second_half.start()
+    for copy in go:
+        copy.wait()
+
+
+def finish(first, second, vec, lo, ig, groups):
+    hbm = pl.BlockSpec(memory_space=pl.ANY)
+    vmem = pl.BlockSpec(memory_space=pltpu.VMEM)
+    size = D // groups
+    row = jax.ShapeDtypeStruct((1, size), F32)
+    return pl.pallas_call(
+        functools.partial(finish_kernel, groups),
+        out_shape=(
+            jax.ShapeDtypeStruct(first.shape, F32), jax.ShapeDtypeStruct(second.shape, F32),
+            jax.ShapeDtypeStruct(lo.shape, BF), jax.ShapeDtypeStruct(ig.shape, BF),
+            row, row, jax.ShapeDtypeStruct((1, 4 * size), F32), row,
+        ),
+        in_specs=[hbm, hbm, vmem, hbm, hbm],
+        out_specs=(hbm, hbm, hbm, hbm, vmem, vmem, vmem, vmem),
+        scratch_shapes=[
+            pltpu.VMEM(first.shape, F32), pltpu.VMEM(second.shape, F32),
+            pltpu.VMEM(lo.shape, BF), pltpu.VMEM(ig.shape, BF),
+            pltpu.SemaphoreType.DMA((4,)), pltpu.SemaphoreType.DMA((4,)),
+        ],
+        name="finish",
+    )(first, second, vec, lo, ig)
+
+
 def on_device(tokens, cotangent, norm_gain, norm_shift, w_first, b_first, w_second, b_second):
-    dp = lax.axis_index("dp")
     groups = lax.axis_size("dp")
     inner = groups // MEMBERS
     micros = MICROS
     real = tokens.shape[0] // micros
     rows = (real + 15) // 16 * 16
-    line = jnp.concatenate([norm_gain, norm_shift, b_second, jnp.zeros((1, FF - 3 * D), F32)], 1)
-    par = jnp.concatenate([b_first, line, jnp.zeros((6, FF), F32)], 0)
     lo, ig, left, right, small = run_sections(
-        tokens, cotangent, par, w_first[0], w_second[0], micros, rows, real
+        tokens, cotangent, norm_gain, norm_shift, b_first, b_second, w_first[0], w_second[0], micros, rows, real
     )
     g_first, g_second, vec, layer_out, input_grad = reduce_weights(left, right, small, lo, ig, inner, real)
 
@@ -847,23 +1053,13 @@
             )
 
         g_first = over_members(g_first, 0)
-        g_second = over_members(g_second, 1)
+        g_second = over_members(g_second, 0)
         vec = lax.psum(vec, "dp", axis_index_groups=members)
 
-    def piece(vec):
-        size = vec.shape[0] // groups
-        return lax.dynamic_slice_in_dim(vec, dp * size, size, 0)[None]
-
-    return (
-        layer_out,
-        input_grad,
-        piece(vec[0]),
-        piece(vec[1]),
-        g_first[None],
-        piece(vec[3:7].reshape(FF)),
-        g_second[None],
-        piece(vec[2]),
+    g_first, g_second, layer_out, input_grad, g_gain, g_shift, g_bias, g_last = finish(
+        g_first, g_second, vec, layer_out, input_grad, groups
     )
+    return (layer_out, input_grad, g_gain, g_shift, g_first[None], g_bias, g_second.T[None], g_last)
 
 
 def solution(mesh):

time: 229 us -> 208 us (0.908)
  local copies, waits for them, and re-layouts: 10.6 us -> 0 us
  Pallas kernels: 216 us -> 207 us
    pallas_call x1, Pallas kernels: 98.6 us -> 88 us  [reduce_weights(): pl.pallas_call(functools.partial(weights_kernel, inner, real), out_shape=...]
    unnamed x8 -> x0, local copies, waits for them, and re-layouts: 6.98 us -> none
    pallas_call x0 -> x1, Pallas kernels: none -> 4.65 us  [finish(): pl.pallas_call(functools.partial(finish_kernel, groups), out_shape=(jax.S...]
    pallas_call x1, Pallas kernels: 117 us -> 114 us  [run_sections(): pl.pallas_call(functools.partial(sections_kernel, micros, rows, real), ou...]
where the time goes in v4:
time: 208 us
  Pallas kernels  207 us (100%)
    pallas_call x1, Pallas kernels, run_sections(): pl.pallas_call(functools.partial(sections_kernel, micros, rows, real), ou...  114 us
    pallas_call x1, Pallas kernels, reduce_weights(): pl.pallas_call(functools.partial(weights_kernel, inner, real), out_shape=...  88 us
    pallas_call x1, Pallas kernels, finish(): pl.pallas_call(functools.partial(finish_kernel, groups), out_shape=(jax.S...  4.65 us

profile of v4, /device:TPU:1, one launch (start us, length us, event | category | flops | bytes accessed | tf_op | source)
XLA Modules:
  0.0 207.9 jit_solution(2154398352064205026)
XLA Ops:
  0.6 114.4 %sections.1 = (bf16[2,304,768]{2,1,0:T(8,128)(2,1)}, bf16[8,304,768]{2,1,0:T(8,128)(2,1)}, bf16[2,2432,768]{2,1,0:T(8,128)(2,1)}, bf16[2432,6144]{1,0:T(8,128)(2,1)}, f32[8,768]{1,0:T(8,128)}) custom-call(bf16[2352,768]{1,0:T(8,128)(2,1)} %tok_ref.1, bf16[2352,768]{1,0:T(8,128)(2,1)} %cot_ref.1, f32[1,768]{1,0:T(1,128)} %gain_ref.1, f32[1,768]{1,0:T(1,128)} %shift_ref.1, ...), custom_call_target="tpu_custom_call" | custom-call | flops 91804925952 | bytes 60000000 | tf_op jit(solution)/shard_map/sections/pallas_call | solution.py:595
  115.1 88.0 %weights.1 = (f32[96,3072]{1,0:T(8,128)}, f32[96,3072]{1,0:T(8,128)}, f32[8,768]{1,0:T(8,128)}, bf16[588,768]{1,0:T(8,128)(2,1)}, bf16[588,768]{1,0:T(8,128)(2,1)}) custom-call(bf16[2,2432,768]{2,1,0:T(8,128)(2,1)} %get-tuple-element.26.left_ref, bf16[2432,6144]{1,0:T(8,128)(2,1)} %get-tuple-element.27.right_ref, f32[8,768]{1,0:T(8,128)} %get-tuple-element.28.small, ...), custom_call_target="tpu_custom_call" | custom-call | flops 22951231488 | bytes 40000000 | tf_op jit(solution)/shard_map/weights/pallas_call | solution.py:943
  203.1 4.6 %finish.1 = (f32[96,3072]{1,0:T(8,128)}, f32[96,3072]{1,0:T(8,128)}, bf16[588,768]{1,0:T(8,128)(2,1)}, bf16[588,768]{1,0:T(8,128)(2,1)}, f32[1,96]{1,0:T(1,128)}...) custom-call(f32[96,3072]{1,0:T(8,128)} %get-tuple-element.31.first, f32[96,3072]{1,0:T(8,128)} %get-tuple-element.32.second, ...), custom_call_target="tpu_custom_call" | custom-call | tf_op jit(solution)/shard_map/finish/pallas_call | solution.py:1018

commit v5 on v4

v5 whole, which is shorter than its diff:
```python
import functools

import jax
import jax.experimental.pallas as pl
import jax.experimental.pallas.tpu as pltpu
import jax.numpy as jnp
from jax import lax
from jax.sharding import PartitionSpec as P

D = 768
FF = 3072
PATCHES = 49
PAD = 64
EPS = 1e-05
SCALE = 32 ** (-0.5)
MICROS = 8
MEMBERS = 8
BLOCK = D // MEMBERS
CHUNK = 512
GROUPS = {True: 3, False: 6}
WIDE = 256
X_LAG = 5
HOP = 3
RING = 3
LINES = MEMBERS // 2
SLOTS = LINES + 1
PER = FF // WIDE
Z_FIRST = 5
MESH = pl.DeviceIdType.MESH
BF = jnp.bfloat16
F32 = jnp.float32


def dot(a, b, ca, cb):
    return lax.dot_general(a, b, (((ca,), (cb,)), ((), ())), preferred_element_type=F32)


def gelu_pair(h):
    cdf = 0.5 + 0.5 * lax.erf(h * 0.7071067811865476)
    bell = jnp.exp(-0.5 * h * h)
    return h * cdf, cdf + h * (0.3989422804014327 * bell)


def norm_parts(x):
    center = x - jnp.mean(x, -1, keepdims=True)
    inverse = lax.rsqrt(jnp.mean(center * center, -1, keepdims=True) + EPS)
    return center * inverse, inverse


def head_masks(width):
    lane = lax.broadcasted_iota(jnp.int32, (1, width), 1) // 32
    return [lane == h for h in range(width // 32)]


def spread(block, masks):
    return jnp.concatenate([jnp.where(m, block, jnp.zeros_like(block)) for m in masks], 0)


def gather_heads(stacked, masks):
    total = None
    for h, m in enumerate(masks):
        part = jnp.where(m, stacked[PAD * h : PAD * (h + 1)], 0.0)
        total = part if total is None else total + part
    return total


def spread_turned(block):
    turned = block.T
    twice = jnp.concatenate([turned, turned], 1)
    lane = lax.broadcasted_iota(jnp.int32, (1, 2 * PAD), 1) // PAD
    none = jnp.zeros((32, 2 * PAD), block.dtype)
    rows = []
    for h in range(8):
        part = jnp.where(lane == h % 2, twice[32 * h : 32 * (h + 1)], none)
        rows.append(jnp.concatenate([part if c == h // 2 else none for c in range(4)], 1))
    return jnp.concatenate(rows, 0)


WIDE_STARTS = range(0, D, 256)
STARTS = range(0, D, 128)


def heads_apart(stacked, values):
    four = head_masks(128)
    parts = []
    for n, s in enumerate(STARTS):
        cols = slice(256 * (n % 2), 256 * (n % 2) + 256)
        parts.append(gather_heads(dot(stacked[n // 2][:, cols], values[:, s : s + 128], 0, 0), four))
    return parts


def window_forward(qs, ks, vs):
    every = range(len(qs))
    row = lax.broadcasted_iota(jnp.int32, (PAD, 1), 0)
    scores = [
        [dot(ks[i][:, s : s + 256], spread_turned(qs[i][:, s : s + 256]), 1, 0) for s in WIDE_STARTS]
        for i in every
    ]
    probs = []
    for i in every:
        blocks = []
        for block in scores[i]:
            block = jnp.where(row < PATCHES, block, -1e30)
            e = jnp.exp((block - jnp.max(block, 0, keepdims=True)) * SCALE)
            blocks.append((e * (1.0 / jnp.sum(e, 0, keepdims=True))).astype(BF))
        probs.append(blocks)
    parts = [jnp.concatenate(heads_apart(probs[i], vs[i]), 1) for i in every]
    return probs, parts


def window_backward(qs, ks, vs, probs, d_atts):
    eight = head_masks(256)
    every = range(len(qs))
    d_probs = [
        [dot(vs[i][:, s : s + 256], spread_turned(d_atts[i][:, s : s + 256]), 1, 0) for s in WIDE_STARTS]
        for i in every
    ]
    d_v = [
        [dot(probs[i][n], spread(d_atts[i][:, s : s + 256], eight), 1, 0) for n, s in enumerate(WIDE_STARTS)]
        for i in every
    ]
    d_scores = []
    for i in every:
        blocks = []
        for n in range(len(WIDE_STARTS)):
            p = probs[i][n].astype(F32)
            product = p * d_probs[i][n]
            blocks.append((product - p * jnp.sum(product, 0, keepdims=True)).astype(BF))
        d_scores.append(blocks)
    d_k = [
        [dot(d_scores[i][n], spread(qs[i][:, s : s + 256], eight), 1, 0) * SCALE for n, s in enumerate(WIDE_STARTS)]
        for i in every
    ]
    d_q = [[part * SCALE for part in heads_apart(d_scores[i], ks[i])] for i in every]
    return [[jnp.concatenate(parts[i], 1) for parts in (d_q, d_k, d_v)] for i in every]


def compress(block, masks):
    total = None
    for h, m in enumerate(masks):
        part = jnp.where(m, block[32 * h : 32 * h + 32], 0.0)
        total = part if total is None else total + part
    return total


def diagonal_turned(block):
    turned = jnp.concatenate([block.T] * 4, 1)
    r = lax.broadcasted_iota(jnp.int32, (128, 128), 0) // 32
    c = lax.broadcasted_iota(jnp.int32, (128, 128), 1) // 32
    return jnp.where(r == c, turned, jnp.zeros_like(turned))


def channel_forward(qs, ks, vs):
    four = head_masks(128)
    every = range(len(qs))
    scores = [[dot(ks[i][:, s : s + 128], qs[i][:, s : s + 128], 0, 0) for s in STARTS] for i in every]
    scores = [jnp.concatenate([compress(block, four) for block in scores[i]], 1) for i in every]
    es = [jnp.exp((block - jnp.max(block, 0, keepdims=True)) * SCALE) for block in scores]
    probs = [(e * (1.0 / jnp.sum(e, 0, keepdims=True))).astype(BF) for e in es]
    parts = [
        jnp.concatenate([dot(vs[i][:, s : s + 128], spread(probs[i][:, s : s + 128], four), 1, 0) for s in STARTS], 1)
        for i in every
    ]
    return probs, parts


def channel_backward(qs, ks, vs, probs, d_atts):
    four = head_masks(128)
    every = range(len(qs))
    d_probs = [[dot(vs[i][:, s : s + 128], d_atts[i][:, s : s + 128], 0, 0) for s in STARTS] for i in every]
    d_v = [
        [dot(d_atts[i][:, s : s + 128], diagonal_turned(probs[i][:, s : s + 128]), 1, 0) for s in STARTS]
        for i in every
    ]
    d_scores = []
    for i in every:
        block = jnp.concatenate([compress(block, four) for block in d_probs[i]], 1)
        p = probs[i].astype(F32)
        product = p * block
        d_scores.append((product - p * jnp.sum(product, 0, keepdims=True)).astype(BF))
    d_q = [
        [dot(ks[i][:, s : s + 128], spread(d_scores[i][:, s : s + 128], four), 1, 0) * SCALE for s in STARTS]
        for i in every
    ]
    d_k = [
        [dot(qs[i][:, s : s + 128], diagonal_turned(d_scores[i][:, s : s + 128]), 1, 0) * SCALE for s in STARTS]
        for i in every
    ]
    return [[jnp.concatenate(parts[i], 1) for parts in (d_q, d_k, d_v)] for i in every]


def layer_kernel(
    micros, rows, real, inner,
    tok_ref, cot_ref, gain_ref, shift_ref, bias_ref, bias_out_ref, w1_ref, w2_ref,
    lo_ref, ig_ref, active_ref, first_out, second_out, vec_ref,
    w1, w2, big, flat, x_in, g_in, normed, v_out, g_out, raw, wide, acc, tmp, from_z, small_ref, vec_x, vec_z,
    w_sem, raw_sem, v_send, v_recv, g_send, g_recv, f_send, f_recv, i_recv, k_sem,
    r_sem, x_send, x_recv, z_send, z_recv, vec_send, vec_recv, o_sem, ready,
):
    dp, role = lax.axis_index("dp"), lax.axis_index("pipe")
    feed = role % 2
    outer, rest = dp // inner, dp % inner
    z, x = outer // 2, outer % 2
    count = micros * rows

    def at(zz, xx):
        return ((zz * 2 + xx) * inner + rest, role)

    images = real // PATCHES
    share = micros // 4
    slab = raw.shape[1]
    total = tok_ref.shape[0]

    barrier = pltpu.get_barrier_semaphore()
    for n in range(1, 4):
        pl.semaphore_signal(barrier, inc=1, device_id=(dp, (role + n) % 4), device_id_type=MESH)
    pl.semaphore_signal(barrier, inc=1, device_id=at(z, 1 - x), device_id_type=MESH)
    for n in range(1, LINES):
        pl.semaphore_signal(barrier, inc=1, device_id=at((z + n) % LINES, x), device_id_type=MESH)

    load_1 = pltpu.make_async_copy(w1_ref, w1, w_sem.at[0])
    load_2 = pltpu.make_async_copy(w2_ref, w2, w_sem.at[1])
    load_1.start()

    def owner(m):
        return m // share

    def first_row(m):
        return m * real

    def slab_start(m):
        return pl.multiple_of(jnp.minimum(first_row(m) // 16 * 16, total - slab), 16)

    def load_slab(ref, m):
        return pltpu.make_async_copy(ref.at[pl.ds(slab_start(m), slab)], raw.at[m % 2], raw_sem.at[m % 2])

    def take_slab(ref, m, dst):
        load_slab(ref, m).wait()
        shift = first_row(m) - slab_start(m)
        moved = pltpu.roll(raw[m % 2].astype(F32), slab - shift, 0)[:rows]
        row = lax.broadcasted_iota(jnp.int32, (rows, 1), 0)
        dst[m] = jnp.where(row < real, moved, 0.0).astype(BF)

        @pl.when(m + 2 < micros)
        def _():
            load_slab(ref, m + 2).start()

    small_ref[...] = jnp.zeros_like(small_ref)

    def keep_active(m):
        return pltpu.make_async_copy(wide, active_ref.at[m], k_sem)

    def again(m, copy):
        @pl.when(m > 0)
        def _():
            copy.wait()

    def next_hop(m):
        return pltpu.make_async_remote_copy(
            src_ref=v_out.at[m % 2], dst_ref=x_in.at[m], send_sem=v_send.at[m], recv_sem=v_recv.at[m],
            device_id=(dp, (role + 1) % 4), device_id_type=MESH,
        )

    def back_hop(m):
        return pltpu.make_async_remote_copy(
            src_ref=g_out.at[m % 2], dst_ref=g_in.at[m], send_sem=g_send.at[m], recv_sem=g_recv.at[m],
            device_id=(dp, (role + 3) % 4), device_id_type=MESH,
        )

    def result_hop(m, back):
        src, ref, recv = (g_out, ig_ref, i_recv) if back else (v_out, lo_ref, f_recv)
        return pltpu.make_async_remote_copy(
            src_ref=src.at[m % 2], dst_ref=ref.at[m % share], send_sem=f_send.at[m],
            recv_sem=recv.at[m % share], device_id=(dp, owner(m)), device_id_type=MESH,
        )

    def result_here(m, back):
        src, ref = (g_out, ig_ref) if back else (v_out, lo_ref)
        return pltpu.make_async_copy(src.at[m % 2], ref.at[m % share], f_send.at[m])

    def result_start(m, back):
        @pl.when(owner(m) == role)
        def _():
            result_here(m, back).start()

        @pl.when(owner(m) != role)
        def _():
            result_hop(m, back).start()

    def result_wait(m, back):
        @pl.when(owner(m) == role)
        def _():
            result_here(m, back).wait()

        @pl.when(owner(m) != role)
        def _():
            result_hop(m, back).wait_send()

    bias, bias_out = bias_ref[...], bias_out_ref[...]
    gain, shift_row = gain_ref[...], shift_ref[...]
    image_row = lax.broadcasted_iota(jnp.int32, (PAD, 1), 0)

    def norm_forward(m, x):
        scaled, _ = norm_parts(x)
        normed[m] = (scaled * gain + shift_row).astype(BF)

    def norm_back(d_normed, m):
        scaled, inverse = norm_parts(x_in[m].astype(F32))
        small_ref[0:1, :] += jnp.sum(d_normed * scaled, 0, keepdims=True)
        small_ref[1:2, :] += jnp.sum(d_normed, 0, keepdims=True)
        d_scaled = d_normed * gain
        mean = jnp.mean(d_scaled, -1, keepdims=True)
        cross = jnp.mean(d_scaled * scaled, -1, keepdims=True)
        return (g_in[m].astype(F32) + inverse * (d_scaled - mean - scaled * cross)).astype(BF)

    def cut(src, n, c):
        part = src[PATCHES * n : PATCHES * n + PAD, c : c + D]
        return jnp.where(image_row < PATCHES, part, 0.0).astype(BF)

    def place(i, n):
        return (3 * i + n) // 4 * PAD, (3 * i + n) % 4 * D

    def projected(m, some, n):
        parts = []
        for i in some:
            r, c = place(i, n)
            parts.append(big[m, r : r + PAD, c : c + D])
        return parts

    def probs_at(m, i, j, size):
        return pl.ds(pl.multiple_of(((m * images + i) * 6 + j) * PAD, PAD), size)

    def out_rows(m):
        return pl.ds(pl.multiple_of(m * rows, 16), rows)

    def attention_forward(m, spatial):
        x = x_in[m].astype(F32)
        norm_forward(m, x)
        for c in range(0, 3 * D, D):
            tmp[0:rows, c : c + D] = dot(normed[m], w1[:, c : c + D], 1, 0) + bias[:, c : c + D]
        for i in range(images):
            for n in range(3):
                r, c = place(i, n)
                big[m, r : r + PAD, c : c + D] = cut(tmp, i, n * D)

        for start in range(0, images, GROUPS[spatial]):
            some = range(start, min(start + GROUPS[spatial], images))
            qs, ks, vs = (projected(m, some, n) for n in range(3))
            if spatial:
                kept, parts = window_forward(qs, ks, vs)
                for i, blocks in zip(some, kept):
                    for j in range(6):
                        flat[probs_at(m, i, j, PAD), :] = blocks[j // 2][:, 256 * (j % 2) : 256 * (j % 2) + 256]
            else:
                kept, parts = channel_forward(qs, ks, vs)
                for i, block in zip(some, kept):
                    for j in range(3):
                        flat[probs_at(m, i, j, 32), :] = block[:, 256 * j : 256 * (j + 1)]
            for i, part in zip(some, parts):
                acc[PATCHES * i : PATCHES * i + PAD, :] = part
        acc[real:rows, :] = jnp.zeros((rows - real, D), F32)
        att_low = acc[0:rows, :].astype(BF)
        w2[out_rows(m), :] = att_low
        branch = dot(att_low, w1[:, 3 * D :], 1, 0) + bias[:, 3 * D :]
        v_out[m % 2] = (x + branch).astype(BF)

    def attention_backward(m, spatial):
        g = g_in[m]
        small_ref[6:7, :] += jnp.sum(g.astype(F32), 0, keepdims=True)
        acc[0:rows, :] = dot(g, w1[:, 3 * D :], 1, 1)
        for start in range(0, images, GROUPS[spatial]):
            some = range(start, min(start + GROUPS[spatial], images))
            qs, ks, vs = (projected(m, some, n) for n in range(3))
            d_atts = [cut(acc, i, 0) for i in some]
            if spatial:
                kept = [
                    [
                        jnp.concatenate([flat[probs_at(m, i, 2 * n + a, PAD), :] for a in range(2)], 1)
                        for n in range(3)
                    ]
                    for i in some
                ]
                grads = window_backward(qs, ks, vs, kept, d_atts)
            else:
                kept = [
                    jnp.concatenate([flat[probs_at(m, i, j, 32), :] for j in range(3)], 1) for i in some
                ]
                grads = channel_backward(qs, ks, vs, kept, d_atts)
            for i, parts in zip(some, grads):
                for n in range(3):
                    tmp[PATCHES * i : PATCHES * i + PAD, n * D : (n + 1) * D] = parts[n]
        tmp[real:rows, :] = jnp.zeros((rows - real, 3 * D), F32)
        for n in range(3):
            part = tmp[0:rows, n * D : (n + 1) * D]
            big[m, 0:rows, n * D : (n + 1) * D] = part.astype(BF)
            small_ref[3 + n : 4 + n, :] += jnp.sum(part, 0, keepdims=True)
        g_out[m % 2] = norm_back(dot(big[m, 0:rows, : 3 * D], w1[:, : 3 * D], 1, 1), m)

    def feed_forward(m):
        x = x_in[m].astype(F32)
        norm_forward(m, x)
        again(m, keep_active(m))
        for c in range(0, FF, CHUNK):
            hidden = dot(normed[m], w1[:, c : c + CHUNK], 1, 0) + bias[:, c : c + CHUNK]
            value, diff = gelu_pair(hidden)
            wide[:, c : c + CHUNK] = value.astype(BF)
            big[m, 0:rows, c : c + CHUNK] = diff.astype(BF)
        keep_active(m).start()
        v_out[m % 2] = (x + bias_out + dot(wide[...], w2[...], 1, 0)).astype(BF)

    def feed_backward(m):
        small_ref[2:3, :] += jnp.sum(g_in[m].astype(F32), 0, keepdims=True)
        for n in range(FF // D):
            c = n * D
            d_act = dot(g_in[m], w2[c : c + D, :], 1, 1)
            d_hid = (d_act * big[m, 0:rows, c : c + D].astype(F32)).astype(BF)
            big[m, 0:rows, c : c + D] = d_hid
            small_ref[3 + n : 4 + n, :] += jnp.sum(d_hid.astype(F32), 0, keepdims=True)
        g_out[m % 2] = norm_back(dot(big[m, 0:rows], w1[...], 1, 1), m)

    def forward(m, run, first, last):
        if first:
            take_slab(tok_ref, m, x_in)
        else:
            next_hop(m).wait_recv()

        @pl.when(m >= 2)
        def _():
            finish_forward(m - 2, last)

        run(m)
        if last is True:
            result_start(m, False)
        elif last is False:
            next_hop(m).start()
        else:

            @pl.when(last)
            def _():
                result_start(m, False)

            @pl.when(jnp.logical_not(last))
            def _():
                next_hop(m).start()

    def finish_forward(m, last):
        if last is False:
            next_hop(m).wait_send()
        else:

            @pl.when(last)
            def _():
                result_wait(m, False)

            @pl.when(jnp.logical_not(last))
            def _():
                next_hop(m).wait_send()

    def backward(m, run, first, last):
        if last is False:
            back_hop(m).wait_recv()
        else:

            @pl.when(last)
            def _():
                take_slab(cot_ref, m, g_in)

            @pl.when(jnp.logical_not(last))
            def _():
                back_hop(m).wait_recv()

        @pl.when(m >= 2)
        def _():
            finish_backward(m - 2, first)

        run(m)
        if first:
            result_start(m, True)
        else:
            back_hop(m).start()

    def finish_backward(m, first):
        if first:
            result_wait(m, True)
        else:
            back_hop(m).wait_send()

    def pipeline(run_forward, run_backward, lag, first, last):
        def step(s, carry):
            @pl.when(s < micros)
            def _():
                forward(s, run_forward, first, last)

            @pl.when(s >= lag)
            def _():
                backward(s - lag, run_backward, first, last)

            return carry

        lax.fori_loop(0, micros + lag, step, 0)

    @pl.when(role == 0)
    def _():
        load_slab(tok_ref, 0).start()
        load_slab(tok_ref, 1).start()

    @pl.when(role == 3)
    def _():
        load_slab(cot_ref, 0).start()
        load_slab(cot_ref, 1).start()

    @pl.when(role % 2 == 1)
    def _():
        load_2.start()

    load_1.wait()
    pl.semaphore_wait(barrier, 3 + LINES)

    @pl.when(role == 0)
    def _():
        tmp[rows:, :] = jnp.zeros((tmp.shape[0] - rows, 3 * D), F32)
        acc[rows:, :] = jnp.zeros((acc.shape[0] - rows, D), F32)
        pipeline(
            functools.partial(attention_forward, spatial=True),
            functools.partial(attention_backward, spatial=True),
            micros, True, False,
        )

    @pl.when(role == 2)
    def _():
        tmp[rows:, :] = jnp.zeros((tmp.shape[0] - rows, 3 * D), F32)
        acc[rows:, :] = jnp.zeros((acc.shape[0] - rows, D), F32)
        pipeline(
            functools.partial(attention_forward, spatial=False),
            functools.partial(attention_backward, spatial=False),
            2, False, False,
        )

    @pl.when(feed == 1)
    def _():
        load_2.wait()
        pipeline(feed_forward, feed_backward, jnp.where(role == 3, 0, micros), False, role == 3)
        keep_active(micros - 1).wait()

    steps = PER + PER * feed
    all_steps = steps + (LINES - 1) * HOP + X_LAG
    pl.semaphore_signal(ready, inc=1, device_id=at(z, 1 - x), device_id_type=MESH)

    def columns(k):
        return pl.ds(pl.multiple_of(k * WIDE, WIDE), WIDE)

    def load_active(k):
        j = k - PER
        return pltpu.make_async_copy(
            active_ref.at[:, :, columns(j)], x_in.at[:, :, columns(j % RING)], r_sem.at[j % RING]
        )

    @pl.when(feed == 1)
    def _():
        for j in range(RING):
            load_active(PER + j).start()

    def chunk_rows(k, xx, zz, size):
        return pl.ds(pl.multiple_of(((k * 2 + xx) * LINES + zz) * BLOCK, 32), size * BLOCK)

    def multiply(k):
        def put(left, right):
            product = dot(left.reshape(count, D), right.reshape(count, WIDE), 0, 0).astype(BF)
            product = product.reshape(LINES, 2, BLOCK, WIDE)
            for xx in range(2):
                flat[chunk_rows(k, xx, 0, LINES), :] = product[:, xx].reshape(LINES * BLOCK, WIDE)

        @pl.when((feed == 1) & (k < PER) | (feed == 0) & (k < 3 * D // WIDE))
        def _():
            put(normed[...], big[:, 0:rows, columns(k)])

        @pl.when((feed == 1) & (k >= PER))
        def _():
            load_active(k).wait()
            put(g_in[...], x_in[:, :, columns((k - PER) % RING)])

            @pl.when(k + RING < steps)
            def _():
                load_active(k + RING).start()

        @pl.when((feed == 0) & (k >= 3 * D // WIDE))
        def _():
            put(w2[0:count, :], g_in[:, :, columns(k - 3 * D // WIDE)])

    def z_first(k):
        return jnp.where(feed == 1, k % Z_FIRST == 1, k == 0)

    def extra(k):
        return 2 * PER + k // Z_FIRST

    def x_place(k, size):
        return w1.at[pl.ds(pl.multiple_of(k % 2 * (LINES * BLOCK), 32), size * BLOCK), columns(k // 2)]

    def along_x(k, src, size):
        return pltpu.make_async_remote_copy(
            src_ref=flat.at[src], dst_ref=x_place(k, size), send_sem=x_send.at[k], recv_sem=x_recv.at[k],
            device_id=at(z, 1 - x), device_id_type=MESH,
        )

    def to_x(k):
        return along_x(k, chunk_rows(k, 1 - x, 0, LINES), LINES)

    def block_to_x(k):
        return along_x(k, chunk_rows(k, 1 - x, z, 1), 1)

    def hop(k, b, slot, target, other):
        xx, row = (1 - x, extra(k)) if other else (x, k)
        return pltpu.make_async_remote_copy(
            src_ref=flat.at[chunk_rows(k, xx, b, 1)], dst_ref=from_z.at[row * SLOTS + slot],
            send_sem=z_send.at[row, b], recv_sem=z_recv.at[row, slot],
            device_id=at(target, x), device_id_type=MESH,
        )

    def up(k, b, other):
        return hop(k, b, b, jnp.minimum(z + 1, LINES - 1), other)

    def down(k, b, other):
        return hop(k, b, jnp.where(b == z - 1, LINES, b), jnp.maximum(z - 1, 0), other)

    def add(k, b, slot, whole):
        for other in (False, True)[: 1 + whole]:
            hop(k, 0, slot, z, other).wait_recv()
            xx, row = (1 - x, extra(k)) if other else (x, k)
            here = chunk_rows(k, xx, b, 1)
            flat[here, :] = (flat[here, :].astype(F32) + from_z[row * SLOTS + slot].astype(F32)).astype(BF)

    def in_range(k, whole):
        kind = z_first(k) if whole else jnp.logical_not(z_first(k))
        return (k >= 0) & (k < steps) & kind

    def result_place(k):
        return tmp.at[pl.ds(pl.multiple_of(k % 3 * BLOCK, 8), BLOCK), columns(k // 3)]

    def put_first(k):
        return pltpu.make_async_copy(result_place(k), first_out.at[:, columns(k)], o_sem.at[k])

    def put_second(k):
        return pltpu.make_async_copy(result_place(k), second_out.at[:, columns(k - PER)], o_sem.at[k])

    def write(k, total):
        result_place(k)[...] = total

        @pl.when(k < PER)
        def _():
            put_first(k).start()

        @pl.when(k >= PER)
        def _():
            put_second(k).start()

    def along_z(s, base, whole):
        halves = (False, True)[: 1 + whole]
        k_up = s - base - HOP * z

        @pl.when(in_range(k_up, whole))
        def _():
            for b in range(1, LINES):

                @pl.when(b > z)
                def _():
                    @pl.when(z > 0)
                    def _():
                        add(k_up, b, b, whole)

                    for other in halves:
                        up(k_up, b, other).start()

        k_down = s - base - HOP * (LINES - 1 - z)

        @pl.when(in_range(k_down, whole))
        def _():
            for b in range(LINES - 1):

                @pl.when(b < z)
                def _():
                    @pl.when(z < LINES - 1)
                    def _():
                        add(k_down, b, b, whole)

                    for other in halves:
                        down(k_down, b, other).start()

        k_end = s - base - HOP * (LINES - 1)

        @pl.when(in_range(k_end, whole))
        def _():
            @pl.when(z > 0)
            def _():
                add(k_end, z, z, whole)

            @pl.when(z < LINES - 1)
            def _():
                add(k_end, z, LINES, whole)

            if whole:
                block_to_x(k_end).start()
            else:
                write(k_end, flat[chunk_rows(k_end, x, z, 1), :].astype(F32))

    vec_to_x = pltpu.make_async_remote_copy(
        src_ref=small_ref, dst_ref=vec_x.at[0], send_sem=vec_send.at[0], recv_sem=vec_recv.at[0],
        device_id=at(z, 1 - x), device_id_type=MESH,
    )

    def vec_to_z(zz, slot):
        return pltpu.make_async_remote_copy(
            src_ref=vec_x.at[1], dst_ref=vec_z.at[slot], send_sem=vec_send.at[1 + zz],
            recv_sem=vec_recv.at[1 + slot], device_id=at(zz, x), device_id_type=MESH,
        )

    multiply(0)
    pl.semaphore_wait(ready, 1)

    def sums(s, carry):
        @pl.when(in_range(s, False))
        def _():
            to_x(s).start()

        @pl.when(s + 1 < steps)
        def _():
            multiply(s + 1)

        k_x = s - X_LAG

        @pl.when(in_range(k_x, False))
        def _():
            to_x(k_x).wait_recv()
            here = chunk_rows(k_x, x, 0, LINES)
            flat[here, :] = (flat[here, :].astype(F32) + x_place(k_x, LINES)[...].astype(F32)).astype(BF)

        along_z(s, 0, True)
        along_z(s, X_LAG, False)
        k_out = s - (LINES - 1) * HOP - X_LAG

        @pl.when(in_range(k_out, True))
        def _():
            block_to_x(k_out).wait_recv()
            write(k_out, flat[chunk_rows(k_out, x, z, 1), :].astype(F32) + x_place(k_out, 1)[...].astype(F32))

        @pl.when(s == 0)
        def _():
            vec_to_x.start()

        @pl.when(s == 4)
        def _():
            vec_to_x.wait_recv()
            vec_x[1] = small_ref[...] + vec_x[0]
            for i in range(1, LINES):
                vec_to_z((z + i) % LINES, z).start()

        return carry

    lax.fori_loop(0, all_steps, sums, 0)
    total = vec_x[1]
    for i in range(1, LINES):
        zz = (z + i) % LINES
        vec_to_z(zz, zz).wait_recv()
        total += vec_z[zz]
        vec_to_z(zz, z).wait_send()
    vec_ref[...] = total
    vec_to_x.wait_send()

    def drain(k, carry):
        for whole in (False, True):

            @pl.when(in_range(k, whole))
            def _():
                (block_to_x(k) if whole else to_x(k)).wait_send()
                for b in range(LINES):

                    @pl.when(b != z)
                    def _():
                        for other in (False, True)[: 1 + whole]:
                            up(k, b, other).wait_send()

        @pl.when(k < PER)
        def _():
            put_first(k).wait()

        @pl.when(k >= PER)
        def _():
            put_second(k).wait()

        return carry

    lax.fori_loop(0, steps, drain, 0)

    for m in (micros - 2, micros - 1):

        @pl.when(role == 3)
        def _():
            result_wait(m, False)

        @pl.when(role != 3)
        def _():
            next_hop(m).wait_send()

        @pl.when(role == 0)
        def _():
            result_wait(m, True)

        @pl.when(role != 0)
        def _():
            back_hop(m).wait_send()

    for n in range(share):

        @pl.when(role != 3)
        def _():
            result_hop(n, False).wait_recv()

        @pl.when(role != 0)
        def _():
            result_hop(n, True).wait_recv()


def run_layer(tokens, cotangent, gain, shift, bias, bias_out, w1, w2, micros, rows, real, inner):
    images = real // PATCHES
    tall = max((PATCHES * (images - 1) + PAD + 7) // 8 * 8, rows)
    share = micros // 4
    slab = min(rows + 16, tokens.shape[0])
    deep = max((3 * images + 3) // 4 * PAD, rows)
    hbm = pl.BlockSpec(memory_space=pl.ANY)
    vmem = pl.BlockSpec(memory_space=pltpu.VMEM)
    dma = pltpu.SemaphoreType.DMA
    chunks = 2 * PER
    extras = (chunks + Z_FIRST - 1) // Z_FIRST
    scratch = [
        pltpu.VMEM((D, FF), BF),
        pltpu.VMEM((FF, D), BF),
        pltpu.VMEM((micros, deep, FF), BF),
        pltpu.VMEM((max(micros * images * 6 * PAD, chunks * MEMBERS * BLOCK), WIDE), BF),
        pltpu.VMEM((micros, rows, D), BF),
        pltpu.VMEM((micros, rows, D), BF),
        pltpu.VMEM((micros, rows, D), BF),
        pltpu.VMEM((2, rows, D), BF),
        pltpu.VMEM((2, rows, D), BF),
        pltpu.VMEM((2, slab, D), BF),
        pltpu.VMEM((rows, FF), BF),
        pltpu.VMEM((tall, D), F32),
        pltpu.VMEM((tall, 3 * D), F32),
        pltpu.VMEM(((chunks + extras) * SLOTS, BLOCK, WIDE), BF),
        pltpu.VMEM((8, D), F32),
        pltpu.VMEM((2, 8, D), F32),
        pltpu.VMEM((LINES, 8, D), F32),
        dma((2,)), dma((2,)), dma((micros,)), dma((micros,)), dma((micros,)), dma((micros,)),
        dma((micros,)), dma((share,)), dma((share,)), dma(()),
        dma((RING,)), dma((chunks,)), dma((chunks,)), dma((chunks + extras, LINES)), dma((chunks + extras, SLOTS)),
        dma((1 + LINES,)), dma((1 + LINES,)), dma((chunks,)), pltpu.SemaphoreType.REGULAR,
    ]
    out_shape = (
        jax.ShapeDtypeStruct((share, rows, D), BF),
        jax.ShapeDtypeStruct((share, rows, D), BF),
        jax.ShapeDtypeStruct((micros, rows, FF), BF),
        jax.ShapeDtypeStruct((BLOCK, FF), F32),
        jax.ShapeDtypeStruct((BLOCK, FF), F32),
        jax.ShapeDtypeStruct((8, D), F32),
    )
    return pl.pallas_call(
        functools.partial(layer_kernel, micros, rows, real, inner),
        out_shape=out_shape,
        in_specs=[hbm, hbm, vmem, vmem, vmem, vmem, hbm, hbm],
        out_specs=(hbm, hbm, hbm, hbm, hbm, vmem),
        scratch_shapes=scratch,
        compiler_params=pltpu.CompilerParams(
            collective_id=0, has_side_effects=True, vmem_limit_bytes=64 * 2**20 - 2**17
        ),
        cost_estimate=pl.CostEstimate(
            flops=2 * 6 * 2 * D * FF * micros * rows, bytes_accessed=60_000_000, transcendentals=0
        ),
        name="layer",
    )(tokens, cotangent, gain, shift, bias, bias_out, w1, w2)


def finish_kernel(
    groups, real, first, second, vec, lo, ig,
    first_out, second_out, lo_out, ig_out, gain_out, shift_out, bias_out, last_out,
    first_mid, second_mid, pieces, whole, joined, in_sem, out_sem,
):
    dp, role = lax.axis_index("dp"), lax.axis_index("pipe")
    feed = role % 2
    come = [
        pltpu.make_async_copy(src, dst, in_sem.at[n])
        for n, (src, dst) in enumerate(
            ((lo, pieces.at[0]), (ig, pieces.at[1]), (first, first_mid), (second, second_mid))
        )
    ]
    go = [
        pltpu.make_async_copy(src, dst, out_sem.at[n])
        for n, (src, dst) in enumerate(
            ((whole.at[0], lo_out), (whole.at[1], ig_out), (first_mid, first_out), (second_mid, second_out))
        )
    ]
    for n in range(3):
        come[n].start()

    @pl.when(feed == 1)
    def _():
        come[3].start()

    @pl.when(feed == 0)
    def _():
        second_mid[...] = jnp.zeros_like(second_mid)
        go[3].start()

    size = D // groups
    turned = pltpu.roll(vec[...], lax.rem(D - dp * size, D), 1)
    gain_out[...] = turned[0:1, :size]
    shift_out[...] = turned[1:2, :size]
    last_out[...] = turned[2:3, :size]
    for n in range(4):
        @pl.when(dp // (groups // 4) == n)
        def _():
            shift = (dp % (groups // 4)) * (4 * size)
            bias_out[...] = pltpu.roll(vec[3 + n : 4 + n, :], lax.rem(D - shift, D), 1)[:, : 4 * size]

    for n in range(2):
        come[n].wait()
        for i in range(pieces.shape[1]):
            joined[real * i : real * (i + 1), :] = pieces[n, i, :real].astype(F32)
        whole[n] = joined[: whole.shape[1], :].astype(BF)
        go[n].start()
    come[2].wait()
    go[2].start()

    @pl.when(feed == 1)
    def _():
        come[3].wait()
        go[3].start()

    for copy in go:
        copy.wait()


def finish(first, second, vec, lo, ig, groups, real):
    hbm = pl.BlockSpec(memory_space=pl.ANY)
    vmem = pl.BlockSpec(memory_space=pltpu.VMEM)
    size = D // groups
    share = lo.shape[0]
    row = jax.ShapeDtypeStruct((1, size), F32)
    flat = jax.ShapeDtypeStruct((share * real, D), BF)
    return pl.pallas_call(
        functools.partial(finish_kernel, groups, real),
        out_shape=(
            jax.ShapeDtypeStruct(first.shape, F32), jax.ShapeDtypeStruct(second.shape, F32), flat, flat,
            row, row, jax.ShapeDtypeStruct((1, 4 * size), F32), row,
        ),
        in_specs=[hbm, hbm, vmem, hbm, hbm],
        out_specs=(hbm, hbm, hbm, hbm, vmem, vmem, vmem, vmem),
        scratch_shapes=[
            pltpu.VMEM(first.shape, F32), pltpu.VMEM(second.shape, F32),
            pltpu.VMEM((2,) + lo.shape, BF), pltpu.VMEM((2, share * real, D), BF),
            pltpu.VMEM(((share * real + 7) // 8 * 8, D), F32),
            pltpu.SemaphoreType.DMA((4,)), pltpu.SemaphoreType.DMA((4,)),
        ],
        compiler_params=pltpu.CompilerParams(vmem_limit_bytes=60 * 2**20),
        name="finish",
    )(first, second, vec, lo, ig)


def on_device(tokens, cotangent, norm_gain, norm_shift, w_first, b_first, w_second, b_second):
    groups = lax.axis_size("dp")
    inner = groups // MEMBERS
    micros = MICROS
    real = tokens.shape[0] // micros
    rows = (real + 15) // 16 * 16
    lo, ig, _, g_first, g_second, vec = run_layer(
        tokens, cotangent, norm_gain, norm_shift, b_first, b_second, w_first[0], w_second[0],
        micros, rows, real, inner,
    )

    if inner > 1:
        members = [[o * inner + i for i in range(inner)] for o in range(MEMBERS)]

        def over_members(part, dim):
            return lax.psum_scatter(
                part, "dp", scatter_dimension=dim, axis_index_groups=members, tiled=True
            )

        g_first = over_members(g_first, 0)
        g_second = over_members(g_second, 0)
        vec = lax.psum(vec, "dp", axis_index_groups=members)

    g_first, g_second, layer_out, input_grad, g_gain, g_shift, g_bias, g_last = finish(
        g_first, g_second, vec, lo, ig, groups, real
    )
    return (layer_out, input_grad, g_gain, g_shift, g_first[None], g_bias, g_second.T[None], g_last)


def solution(mesh):
    in_specs = (
        P("dp", None), P("dp", None), P("pipe", None), P("pipe", None),
        P("pipe", None, None), P("pipe", None), P("pipe", None, None), P("pipe", None),
    )
    out_specs = (
        P(("dp", "pipe"), None), P(("dp", "pipe"), None), P("pipe", "dp"), P("pipe", "dp"),
        P("pipe", "dp", None), P("pipe", "dp"), P("pipe", None, "dp"), P("pipe", "dp"),
    )
    return jax.shard_map(
        on_device, mesh=mesh, in_specs=in_specs, out_specs=out_specs, check_vma=False
    )
```

time: 208 us -> 204 us (0.981)
  Pallas kernels: 207 us -> 203 us
    pallas_call x3 -> x2, Pallas kernels: 207 us -> 203 us  [the longest x1 199 us: run_layer(): pl.pallas_call(functools.partial(layer_kernel, micros, rows, real, inner)...]
where the time goes in v5:
time: 204 us
  Pallas kernels  203 us (100%)
    pallas_call x1, Pallas kernels, run_layer(): pl.pallas_call(functools.partial(layer_kernel, micros, rows, real, inner)...  199 us
    pallas_call x1, Pallas kernels, finish(): pl.pallas_call(functools.partial(finish_kernel, groups, real), out_shape=...  4.81 us

profile of v5, /device:TPU:1, one launch (start us, length us, event | category | flops | bytes accessed | tf_op | source)
XLA Modules:
  0.0 204.2 jit_solution(13030788394766650965)
XLA Ops:
  0.6 198.5 %layer.1 = (bf16[2,304,768]{2,1,0:T(8,128)(2,1)}, bf16[2,304,768]{2,1,0:T(8,128)(2,1)}, bf16[8,304,3072]{2,1,0:T(8,128)(2,1)}, f32[96,3072]{1,0:T(8,128)}, f32[96,3072]{1,0:T(8,128)}, /*index=5*/f32[8,768]{1,0:T(8,128)}) custom-call(bf16[2352,768]{1,0:T(8,128)(2,1)} %tok_ref.1, bf16[2352,768]{1,0:T(8,128)(2,1)} %cot_ref.1, f32[1,768]{1,0:T(1,128)} %gain_ref.1, ...), custom_call_target="tpu_custom_call" | custom-call | flops 137707388928 | bytes 60000000 | tf_op jit(solution)/shard_map/layer/pallas_call | solution.py:864
  199.2 4.8 %finish.1 = (f32[96,3072]{1,0:T(8,128)}, f32[96,3072]{1,0:T(8,128)}, bf16[588,768]{1,0:T(8,128)(2,1)}, bf16[588,768]{1,0:T(8,128)(2,1)}, f32[1,96]{1,0:T(1,128)}...) custom-call(f32[96,3072]{1,0:T(8,128)} %get-tuple-element.21.first, f32[96,3072]{1,0:T(8,128)} %get-tuple-element.22.second, ...), custom_call_target="tpu_custom_call" | custom-call | tf_op jit(solution)/shard_map/finish/pallas_call | solution.py:947

commit v6 on v5

--- a/solution.py
+++ b/solution.py
@@ -25,7 +25,7 @@
 LINES = MEMBERS // 2
 SLOTS = LINES + 1
 PER = FF // WIDE
-Z_FIRST = 5
+Z_FIRST = 6
 MESH = pl.DeviceIdType.MESH
 BF = jnp.bfloat16
 F32 = jnp.float32
@@ -208,7 +208,7 @@
 
     images = real // PATCHES
     share = micros // 4
-    slab = raw.shape[1]
+    slab = raw.shape[0]
     total = tok_ref.shape[0]
 
     barrier = pltpu.get_barrier_semaphore()
@@ -232,18 +232,18 @@
         return pl.multiple_of(jnp.minimum(first_row(m) // 16 * 16, total - slab), 16)
 
     def load_slab(ref, m):
-        return pltpu.make_async_copy(ref.at[pl.ds(slab_start(m), slab)], raw.at[m % 2], raw_sem.at[m % 2])
+        return pltpu.make_async_copy(ref.at[pl.ds(slab_start(m), slab)], raw, raw_sem)
 
     def take_slab(ref, m, dst):
         load_slab(ref, m).wait()
         shift = first_row(m) - slab_start(m)
-        moved = pltpu.roll(raw[m % 2].astype(F32), slab - shift, 0)[:rows]
+        moved = pltpu.roll(raw[...].astype(F32), slab - shift, 0)[:rows]
         row = lax.broadcasted_iota(jnp.int32, (rows, 1), 0)
         dst[m] = jnp.where(row < real, moved, 0.0).astype(BF)
 
-        @pl.when(m + 2 < micros)
-        def _():
-            load_slab(ref, m + 2).start()
+        @pl.when(m + 1 < micros)
+        def _():
+            load_slab(ref, m + 1).start()
 
     small_ref[...] = jnp.zeros_like(small_ref)
 
@@ -400,13 +400,22 @@
         x = x_in[m].astype(F32)
         norm_forward(m, x)
         again(m, keep_active(m))
+        def hidden_at(c):
+            return dot(normed[m], w1[:, c : c + CHUNK], 1, 0) + bias[:, c : c + CHUNK]
+
+        coming = hidden_at(0)
+        total = x + bias_out
         for c in range(0, FF, CHUNK):
-            hidden = dot(normed[m], w1[:, c : c + CHUNK], 1, 0) + bias[:, c : c + CHUNK]
+            hidden = coming
+            if c + CHUNK < FF:
+                coming = hidden_at(c + CHUNK)
             value, diff = gelu_pair(hidden)
-            wide[:, c : c + CHUNK] = value.astype(BF)
+            value = value.astype(BF)
+            wide[:, c : c + CHUNK] = value
             big[m, 0:rows, c : c + CHUNK] = diff.astype(BF)
+            total += dot(value, w2[c : c + CHUNK, :], 1, 0)
         keep_active(m).start()
-        v_out[m % 2] = (x + bias_out + dot(wide[...], w2[...], 1, 0)).astype(BF)
+        v_out[m % 2] = total.astype(BF)
 
     def feed_backward(m):
         small_ref[2:3, :] += jnp.sum(g_in[m].astype(F32), 0, keepdims=True)
@@ -502,12 +511,10 @@
     @pl.when(role == 0)
     def _():
         load_slab(tok_ref, 0).start()
-        load_slab(tok_ref, 1).start()
 
     @pl.when(role == 3)
     def _():
         load_slab(cot_ref, 0).start()
-        load_slab(cot_ref, 1).start()
 
     @pl.when(role % 2 == 1)
     def _():
@@ -840,7 +847,7 @@
         pltpu.VMEM((micros, rows, D), BF),
         pltpu.VMEM((2, rows, D), BF),
         pltpu.VMEM((2, rows, D), BF),
-        pltpu.VMEM((2, slab, D), BF),
+        pltpu.VMEM((slab, D), BF),
         pltpu.VMEM((rows, FF), BF),
         pltpu.VMEM((tall, D), F32),
         pltpu.VMEM((tall, 3 * D), F32),
@@ -848,7 +855,7 @@
         pltpu.VMEM((8, D), F32),
         pltpu.VMEM((2, 8, D), F32),
         pltpu.VMEM((LINES, 8, D), F32),
-        dma((2,)), dma((2,)), dma((micros,)), dma((micros,)), dma((micros,)), dma((micros,)),
+        dma((2,)), dma(()), dma((micros,)), dma((micros,)), dma((micros,)), dma((micros,)),
         dma((micros,)), dma((share,)), dma((share,)), dma(()),
         dma((RING,)), dma((chunks,)), dma((chunks,)), dma((chunks + extras, LINES)), dma((chunks + extras, SLOTS)),
         dma((1 + LINES,)), dma((1 + LINES,)), dma((chunks,)), pltpu.SemaphoreType.REGULAR,
@@ -887,26 +894,28 @@
     come = [
         pltpu.make_async_copy(src, dst, in_sem.at[n])
         for n, (src, dst) in enumerate(
-            ((lo, pieces.at[0]), (ig, pieces.at[1]), (first, first_mid), (second, second_mid))
+            ((first, first_mid), (second, second_mid), (lo, pieces.at[0]), (ig, pieces.at[1]))
         )
     ]
     go = [
         pltpu.make_async_copy(src, dst, out_sem.at[n])
         for n, (src, dst) in enumerate(
-            ((whole.at[0], lo_out), (whole.at[1], ig_out), (first_mid, first_out), (second_mid, second_out))
+            ((first_mid, first_out), (second_mid, second_out), (whole.at[0], lo_out), (whole.at[1], ig_out))
         )
     ]
-    for n in range(3):
-        come[n].start()
+    come[0].start()
 
     @pl.when(feed == 1)
     def _():
-        come[3].start()
+        come[1].start()
+
+    come[2].start()
+    come[3].start()
 
     @pl.when(feed == 0)
     def _():
         second_mid[...] = jnp.zeros_like(second_mid)
-        go[3].start()
+        go[1].start()
 
     size = D // groups
     turned = pltpu.roll(vec[...], lax.rem(D - dp * size, D), 1)
@@ -919,20 +928,20 @@
             shift = (dp % (groups // 4)) * (4 * size)
             bias_out[...] = pltpu.roll(vec[3 + n : 4 + n, :], lax.rem(D - shift, D), 1)[:, : 4 * size]
 
+    come[0].wait()
+    go[0].start()
+
+    @pl.when(feed == 1)
+    def _():
+        come[1].wait()
+        go[1].start()
+
     for n in range(2):
-        come[n].wait()
+        come[2 + n].wait()
         for i in range(pieces.shape[1]):
             joined[real * i : real * (i + 1), :] = pieces[n, i, :real].astype(F32)
         whole[n] = joined[: whole.shape[1], :].astype(BF)
-        go[n].start()
-    come[2].wait()
-    go[2].start()
-
-    @pl.when(feed == 1)
-    def _():
-        come[3].wait()
-        go[3].start()
-
+        go[2 + n].start()
     for copy in go:
         copy.wait()
 

time: 204 us -> 202 us (level)
  Pallas kernels: 203 us -> 200 us
    pallas_call x1, Pallas kernels: 199 us -> 196 us  [run_layer(): pl.pallas_call(functools.partial(layer_kernel, micros, rows, real, inner)...]
where the time goes in v6:
time: 202 us; the launch traced here: 201 us
  Pallas kernels  200 us (99%)
    pallas_call x1, Pallas kernels, run_layer(): pl.pallas_call(functools.partial(layer_kernel, micros, rows, real, inner)...  196 us
    pallas_call x1, Pallas kernels, finish(): pl.pallas_call(functools.partial(finish_kernel, groups, real), out_shape=...  4.74 us

profile of v6, /device:TPU:1, one launch (start us, length us, event | category | flops | bytes accessed | tf_op | source)
XLA Modules:
  0.0 201.3 jit_solution(14890166108241257966)
XLA Ops:
  0.6 195.7 %layer.1 = (bf16[2,304,768]{2,1,0:T(8,128)(2,1)}, bf16[2,304,768]{2,1,0:T(8,128)(2,1)}, bf16[8,304,3072]{2,1,0:T(8,128)(2,1)}, f32[96,3072]{1,0:T(8,128)}, f32[96,3072]{1,0:T(8,128)}, /*index=5*/f32[8,768]{1,0:T(8,128)}) custom-call(bf16[2352,768]{1,0:T(8,128)(2,1)} %tok_ref.1, bf16[2352,768]{1,0:T(8,128)(2,1)} %cot_ref.1, f32[1,768]{1,0:T(1,128)} %gain_ref.1, ...), custom_call_target="tpu_custom_call" | custom-call | flops 137707388928 | bytes 60000000 | tf_op jit(solution)/shard_map/layer/pallas_call | solution.py:871
  196.4 4.7 %finish.1 = (f32[96,3072]{1,0:T(8,128)}, f32[96,3072]{1,0:T(8,128)}, bf16[588,768]{1,0:T(8,128)(2,1)}, bf16[588,768]{1,0:T(8,128)(2,1)}, f32[1,96]{1,0:T(1,128)}...) custom-call(f32[96,3072]{1,0:T(8,128)} %get-tuple-element.21.first, f32[96,3072]{1,0:T(8,128)} %get-tuple-element.22.second, ...), custom_call_target="tpu_custom_call" | custom-call | tf_op jit(solution)/shard_map/finish/pallas_call | solution.py:956
